TPU v7x, 32 devices: a whole 2x2x4 slice. The times are simulated.
32 devices in a mesh: dp: 16 (over z, y, x), fsdp: 2 (over core).
Axes of the slice: x: 2, y: 2, z: 4, core: 2. Of those that a mesh axis runs over, the one named last changes fastest.
Arguments:
- table: bfloat16 [32128, 768], P('dp'), may hold values from -6 to 6
- row_in_owner: int32 [16384], P(('dp', 'fsdp')), may hold values from 0 to 2007
- send_counts: int32 [32, 16], P(('dp', 'fsdp')), may hold values from 0 to 64, as said below
- row_order: int32 [32, 512], P(('dp', 'fsdp')), may hold values from 0 to 511, each once within a row
- bucket: int32 [32], P(('dp', 'fsdp')), may hold values from 0 to 3, as said below
- lengths: int32 [256], P(('dp', 'fsdp')), may hold values from 16 to 512, as said below
- norm1_gain: bfloat16 [768], P(('dp', 'fsdp')), may hold values from 0.5 to 1.5
- w_query: bfloat16 [768, 768], P(('dp', 'fsdp')), may hold values from -0.21875 to 0.21875
- w_key: bfloat16 [768, 768], P(('dp', 'fsdp')), may hold values from -0.0546875 to 0.0546875
- w_value: bfloat16 [768, 768], P(('dp', 'fsdp')), may hold values from -0.21875 to 0.21875
- w_output: bfloat16 [768, 768], P(('dp', 'fsdp')), may hold values from -1.75 to 1.75
- position_bias: bfloat16 [384], P(('dp', 'fsdp')), may hold values from -4 to 4
- norm2_gain: bfloat16 [768], P(('dp', 'fsdp')), may hold values from 0.5 to 1.5
- w_inner: bfloat16 [768, 3072], P(('dp', 'fsdp')), may hold values from -0.21875 to 0.21875
- w_outer: bfloat16 [3072, 768], P(('dp', 'fsdp')), may hold values from -0.109375 to 0.109375
- cotangent: bfloat16 [16384, 768], P(('dp', 'fsdp')), may hold values from -6 to 6
Outputs:
- block_out: bfloat16 [16384, 768], P(('dp', 'fsdp'))
- input_grad: float32 [16384, 768], P(('dp', 'fsdp'))
- table_grad: float32 [32128, 768], P('dp')
- norm1_gain_grad: float32 [768], P(('dp', 'fsdp'))
- w_query_grad: float32 [768, 768], P(('dp', 'fsdp'))
- w_key_grad: float32 [768, 768], P(('dp', 'fsdp'))
- w_value_grad: float32 [768, 768], P(('dp', 'fsdp'))
- w_output_grad: float32 [768, 768], P(('dp', 'fsdp'))
- position_bias_grad: float32 [384], P(('dp', 'fsdp'))
- norm2_gain_grad: float32 [768], P(('dp', 'fsdp'))
- w_inner_grad: float32 [768, 3072], P(('dp', 'fsdp'))
- w_outer_grad: float32 [3072, 768], P(('dp', 'fsdp'))
Inputs may be any that keep to these rules, and one draw needn't show every extreme that they name: `send_counts`: each row sums to 512; every entry is at most 64, and in every draw one dp index receives exactly 64 tokens from every block. Block e's documents are all padded to 64 * 2**bucket[e]; some block has the longest bucket. `lengths`: entry k of block e is the length of document k for k below 512 // (64 * 2**bucket[e]), between a quarter of the padded length and the padded length; document 0 of every block is full; other entries are unused.
All inputs are finite; a program needn't handle non-finite values.
Results may differ from a plain program's by a relative error of at most 0.015.
Values may be sent and summed in bfloat16 or wider, within the bound.
A program may use at most 320 MiB of HBM per device.

v0:
```python
from functools import partial

import jax
import jax.numpy as jnp
from jax import lax
from jax.sharding import PartitionSpec as P

D = 768
HEADS = 12
HEAD_DIM = 64
NB = 32
SHORT = 64
TOK_DEV = 512


EPSILON = 1e-06
THRESHOLDS = (12, 16, 23, 32, 46, 64, 91)


def relative_bucket(offset):
    distance = jnp.abs(offset)
    far_bucket = 8 + sum(((distance >= threshold).astype(jnp.int32) for threshold in THRESHOLDS))
    near_far = jnp.where(distance < 8, distance, jnp.minimum(far_bucket, 15))
    return near_far + 16 * (offset > 0).astype(jnp.int32)


def normalize(activations, gains):
    return (
        activations
        * lax.rsqrt(jnp.mean(activations * activations, axis=-1, keepdims=True) + EPSILON)
        * gains
    )


def lowered(array_in):
    return array_in.astype(jnp.bfloat16)


def plain_product(left_side, right_side):
    return jnp.dot(left_side, right_side, preferred_element_type=jnp.float32)


def gram_product(left_side, right_side):
    return lax.dot_general(
        left_side, right_side, (((0,), (0,)), ((), ())), preferred_element_type=jnp.float32
    )


def back_product(left_side, right_side):
    return lax.dot_general(
        left_side, right_side, (((1,), (1,)), ((), ())), preferred_element_type=jnp.float32
    )


def span_buckets(doc_span):
    places = jnp.arange(doc_span, dtype=jnp.int32)
    return relative_bucket(places[None, :] - places[:, None])


def attention_scores(doc_span, queries, key_rows, bias_table, doc_lengths):
    doc_count = TOK_DEV // doc_span
    query_heads = queries.reshape(doc_count, doc_span, HEADS, HEAD_DIM)
    key_heads = key_rows.reshape(doc_count, doc_span, HEADS, HEAD_DIM)
    scores = jnp.einsum(
        "nqhe,nkhe->nhqk", query_heads, key_heads, preferred_element_type=jnp.float32
    )
    position_term = jnp.transpose(bias_table[span_buckets(doc_span)], (2, 0, 1))
    scores = scores + position_term[None]
    places = jnp.arange(doc_span, dtype=jnp.int32)
    allowed = places[None, :] < doc_lengths[:doc_count, None]
    scores = jnp.where(allowed[:, None, None, :], scores, -1000000000.0)
    return (scores, query_heads, key_heads)


def attend_forward(doc_span, queries, key_rows, value_rows, bias_table, doc_lengths):
    doc_count = TOK_DEV // doc_span
    scores = attention_scores(doc_span, queries, key_rows, bias_table, doc_lengths)[0]
    value_heads = value_rows.reshape(doc_count, doc_span, HEADS, HEAD_DIM)
    row_peak = jnp.max(scores, axis=-1, keepdims=True)
    exp_scores = jnp.exp(scores - row_peak)
    denominator = jnp.sum(exp_scores, axis=-1, keepdims=True)
    probability = exp_scores / denominator
    attended = jnp.einsum(
        "nhqk,nkhe->nqhe", lowered(probability), value_heads, preferred_element_type=jnp.float32
    )
    log_total = (row_peak + jnp.log(denominator))[..., 0]
    log_total = jnp.transpose(log_total, (1, 0, 2)).reshape(HEADS, TOK_DEV)
    return (lowered(attended.reshape(TOK_DEV, D)), log_total)


def attend_backward(
    doc_span, queries, key_rows, value_rows, bias_table, doc_lengths, log_total, grad_attended
):
    doc_count = TOK_DEV // doc_span
    scores, query_heads, key_heads = attention_scores(
        doc_span, queries, key_rows, bias_table, doc_lengths
    )
    value_heads = value_rows.reshape(doc_count, doc_span, HEADS, HEAD_DIM)
    kept_total = jnp.transpose(log_total.reshape(HEADS, doc_count, doc_span), (1, 0, 2))[..., None]
    probability = jnp.exp(scores - kept_total)
    grad_heads = grad_attended.reshape(doc_count, doc_span, HEADS, HEAD_DIM)
    grad_prob = jnp.einsum(
        "nqhe,nkhe->nhqk", grad_heads, value_heads, preferred_element_type=jnp.float32
    )
    grad_values = jnp.einsum(
        "nhqk,nqhe->nkhe", lowered(probability), grad_heads, preferred_element_type=jnp.float32
    )
    row_inner = jnp.sum(probability * grad_prob, axis=-1, keepdims=True)
    grad_scores = lowered(probability * (grad_prob - row_inner))
    grad_queries = jnp.einsum(
        "nhqk,nkhe->nqhe", grad_scores, key_heads, preferred_element_type=jnp.float32
    )
    grad_keys = jnp.einsum(
        "nhqk,nqhe->nkhe", grad_scores, query_heads, preferred_element_type=jnp.float32
    )
    table_onehot = (
        span_buckets(doc_span).reshape(-1)[:, None] == jnp.arange(NB, dtype=jnp.int32)[None, :]
    ).astype(jnp.bfloat16)
    flat_scores = grad_scores.reshape(doc_count * HEADS, doc_span * doc_span)
    grad_bias = jnp.sum(
        plain_product(flat_scores, table_onehot).reshape(doc_count, HEADS, NB), axis=0
    ).T
    return (
        lowered(grad_queries.reshape(TOK_DEV, D)),
        lowered(grad_keys.reshape(TOK_DEV, D)),
        lowered(grad_values.reshape(TOK_DEV, D)),
        grad_bias,
    )


def block_parts(embedded, weights_all, level_index, doc_lengths):
    gain_one, w_query, w_key, w_value, w_output, position_bias, gain_two, w_inner, w_outer = (
        weights_all
    )
    normed = lowered(normalize(embedded, gain_one.astype(jnp.float32)))
    queries = lowered(plain_product(normed, w_query))
    key_rows = lowered(plain_product(normed, w_key))
    value_rows = lowered(plain_product(normed, w_value))
    bias_table = position_bias.astype(jnp.float32).reshape(NB, HEADS)
    branches = [partial(attend_forward, SHORT * 2**level_num) for level_num in range(4)]
    attended, log_total = lax.switch(
        level_index, branches, queries, key_rows, value_rows, bias_table, doc_lengths
    )
    residual = embedded + plain_product(attended, w_output)
    normed_two = lowered(normalize(residual, gain_two.astype(jnp.float32)))
    inner_act = plain_product(normed_two, w_inner)
    hidden = lowered(jax.nn.gelu(inner_act, approximate=True))
    layer_out = residual + plain_product(hidden, w_outer)
    return (
        layer_out,
        normed,
        queries,
        key_rows,
        value_rows,
        bias_table,
        attended,
        log_total,
        residual,
        normed_two,
        inner_act,
        hidden,
    )


def body(
    table,
    row_in_owner,
    send_counts,
    row_order,
    bucket,
    lengths,
    norm1_gain,
    w_query,
    w_key,
    w_value,
    w_output,
    position_bias,
    norm2_gain,
    w_inner,
    w_outer,
    cotangent,
):
    dp_count = lax.axis_size("dp")
    slot_cap = 2 * TOK_DEV // dp_count
    owner_rows = table.shape[0]
    counts_row = send_counts[0]
    send_ends = jnp.cumsum(counts_row, dtype=jnp.int32)
    send_starts = send_ends - counts_row
    places = jnp.arange(TOK_DEV, dtype=jnp.int32)
    owners = jnp.sum(
        (places[:, None] >= send_ends[None, :]).astype(jnp.int32), axis=1, dtype=jnp.int32
    )
    slot_index = places - send_starts[owners]
    requests = jnp.zeros((dp_count, slot_cap), jnp.int32).at[owners, slot_index].set(row_in_owner)
    asked_rows = lax.all_to_all(requests, "dp", split_axis=0, concat_axis=0, tiled=True)
    found_rows = table[asked_rows]
    returned = lax.all_to_all(found_rows, "dp", split_axis=0, concat_axis=0, tiled=True)
    token_order = row_order[0]
    fetched = returned[owners, slot_index]
    embedded = (
        jnp.zeros((TOK_DEV, D), jnp.bfloat16).at[token_order].set(fetched).astype(jnp.float32)
    )
    level_index = bucket[0]
    gathered = (
        lax.all_gather(norm1_gain, ("dp", "fsdp"), axis=0, tiled=True),
        lax.all_gather(w_query, ("dp", "fsdp"), axis=0, tiled=True),
        lax.all_gather(w_key, ("dp", "fsdp"), axis=0, tiled=True),
        lax.all_gather(w_value, ("dp", "fsdp"), axis=0, tiled=True),
        lax.all_gather(w_output, ("dp", "fsdp"), axis=0, tiled=True),
        lax.all_gather(position_bias, ("dp", "fsdp"), axis=0, tiled=True),
        lax.all_gather(norm2_gain, ("dp", "fsdp"), axis=0, tiled=True),
        lax.all_gather(w_inner, ("dp", "fsdp"), axis=0, tiled=True),
        lax.all_gather(w_outer, ("dp", "fsdp"), axis=0, tiled=True),
    )
    (
        layer_out,
        normed,
        queries,
        key_rows,
        value_rows,
        bias_table,
        attended,
        log_total,
        residual,
        normed_two,
        inner_act,
        hidden,
    ) = block_parts(embedded, gathered, level_index, lengths)
    back_weights = (
        lax.all_gather(norm1_gain, ("dp", "fsdp"), axis=0, tiled=True),
        lax.all_gather(w_query, ("dp", "fsdp"), axis=0, tiled=True),
        lax.all_gather(w_key, ("dp", "fsdp"), axis=0, tiled=True),
        lax.all_gather(w_value, ("dp", "fsdp"), axis=0, tiled=True),
        lax.all_gather(w_output, ("dp", "fsdp"), axis=0, tiled=True),
        lax.all_gather(position_bias, ("dp", "fsdp"), axis=0, tiled=True),
        lax.all_gather(norm2_gain, ("dp", "fsdp"), axis=0, tiled=True),
        lax.all_gather(w_inner, ("dp", "fsdp"), axis=0, tiled=True),
        lax.all_gather(w_outer, ("dp", "fsdp"), axis=0, tiled=True),
    )
    gain_one, wq_full, wk_full, wv_full, wo_full, bias_full, gain_two, inner_full, outer_full = (
        back_weights
    )
    grad_out = cotangent.astype(jnp.float32)
    grad_outer = lowered(grad_out)
    grad_w_outer = gram_product(hidden, grad_outer)
    grad_hidden = back_product(grad_outer, outer_full)
    gelu_pull = jax.vjp(lambda pre_act: jax.nn.gelu(pre_act, approximate=True), inner_act)[1]
    grad_inner = lowered(gelu_pull(grad_hidden)[0])
    grad_w_inner = gram_product(normed_two, grad_inner)
    grad_normed_two = back_product(grad_inner, inner_full)
    norm_two_pull = jax.vjp(normalize, residual, gain_two.astype(jnp.float32))[1]
    grad_resid_norm, grad_gain_two = norm_two_pull(grad_normed_two)
    ffn_summed = (
        lax.psum_scatter(grad_gain_two, ("dp", "fsdp"), scatter_dimension=0, tiled=True),
        lax.psum_scatter(grad_w_inner, ("dp", "fsdp"), scatter_dimension=0, tiled=True),
        lax.psum_scatter(grad_w_outer, ("dp", "fsdp"), scatter_dimension=0, tiled=True),
    )
    grad_residual = grad_out + grad_resid_norm
    grad_branch = lowered(grad_residual)
    grad_w_output = gram_product(attended, grad_branch)
    output_summed = lax.psum_scatter(grad_w_output, ("dp", "fsdp"), scatter_dimension=0, tiled=True)
    grad_attended = lowered(back_product(grad_branch, wo_full))
    back_branches = [partial(attend_backward, SHORT * 2**level_num) for level_num in range(4)]
    grad_queries, grad_keys, grad_values, grad_bias = lax.switch(
        level_index,
        back_branches,
        queries,
        key_rows,
        value_rows,
        bias_table,
        lengths,
        log_total,
        grad_attended,
    )
    grad_w_query = gram_product(normed, grad_queries)
    grad_w_key = gram_product(normed, grad_keys)
    grad_w_value = gram_product(normed, grad_values)
    grad_normed = (
        back_product(grad_queries, wq_full)
        + back_product(grad_keys, wk_full)
        + back_product(grad_values, wv_full)
    )
    norm_one_pull = jax.vjp(normalize, embedded, gain_one.astype(jnp.float32))[1]
    grad_embed_norm, grad_gain_one = norm_one_pull(grad_normed)
    input_grad = grad_residual + grad_embed_norm
    attention_summed = (
        lax.psum_scatter(grad_gain_one, ("dp", "fsdp"), scatter_dimension=0, tiled=True),
        lax.psum_scatter(grad_w_query, ("dp", "fsdp"), scatter_dimension=0, tiled=True),
        lax.psum_scatter(grad_w_key, ("dp", "fsdp"), scatter_dimension=0, tiled=True),
        lax.psum_scatter(grad_w_value, ("dp", "fsdp"), scatter_dimension=0, tiled=True),
        lax.psum_scatter(grad_bias.reshape(-1), ("dp", "fsdp"), scatter_dimension=0, tiled=True),
    )
    summed = (
        attention_summed[0],
        attention_summed[1],
        attention_summed[2],
        attention_summed[3],
        output_summed,
        attention_summed[4],
        ffn_summed[0],
        ffn_summed[1],
        ffn_summed[2],
    )
    sent_grads = input_grad[token_order]
    outgoing = (
        jnp.zeros((dp_count, slot_cap, D), jnp.float32).at[owners, slot_index].set(sent_grads)
    )
    incoming = lax.all_to_all(
        outgoing.astype(jnp.bfloat16), "dp", split_axis=0, concat_axis=0, tiled=True
    ).astype(outgoing.dtype)
    local_grad = (
        jnp.zeros((owner_rows, D), jnp.float32)
        .at[asked_rows.reshape(-1)]
        .add(incoming.reshape(-1, D))
    )
    table_grad = lax.psum(local_grad.astype(jnp.bfloat16), "fsdp").astype(jnp.float32)
    return (
        lowered(layer_out),
        input_grad,
        table_grad,
        summed[0],
        summed[1],
        summed[2],
        summed[3],
        summed[4],
        summed[5],
        summed[6],
        summed[7],
        summed[8],
    )


def solution(mesh):
    return jax.shard_map(
        body,
        mesh=mesh,
        in_specs=(
            P("dp", None),
            P(("dp", "fsdp")),
            P(("dp", "fsdp"), None),
            P(("dp", "fsdp"), None),
            P(("dp", "fsdp")),
            P(("dp", "fsdp")),
            P(("dp", "fsdp")),
            P(("dp", "fsdp"), None),
            P(("dp", "fsdp"), None),
            P(("dp", "fsdp"), None),
            P(("dp", "fsdp"), None),
            P(("dp", "fsdp")),
            P(("dp", "fsdp")),
            P(("dp", "fsdp"), None),
            P(("dp", "fsdp"), None),
            P(("dp", "fsdp"), None),
        ),
        out_specs=(
            P(("dp", "fsdp"), None),
            P(("dp", "fsdp"), None),
            P("dp", None),
            P(("dp", "fsdp")),
            P(("dp", "fsdp"), None),
            P(("dp", "fsdp"), None),
            P(("dp", "fsdp"), None),
            P(("dp", "fsdp"), None),
            P(("dp", "fsdp")),
            P(("dp", "fsdp")),
            P(("dp", "fsdp"), None),
            P(("dp", "fsdp"), None),
        ),
        check_vma=False,
    )
```

profile of v0, /device:TPU:0, one launch (start us, length us, event | category | flops | bytes accessed | tf_op | source)
XLA Modules:
  0.0 3196.8 jit_solution(13107335816639540252)
XLA Ops:
  23.9 43.3 %scatter_fusion = s32[16,64]{1,0:T(8,128)S(1)} fusion(s32[16,64]{1,0:T(8,128)S(1)} %broadcast.1725, s32[512]{0:T(512)S(1)} %bitcast.377, s32[512]{0:T(512)} %param.25), kind=kCustom, calls=%fused_computation.11 | custom fusion | bytes 10240 | tf_op jit(solution)/shard_map/scatter | solution.py:194
  67.2 15.4 all_to_all.22
  93.8 60.3 %all-reduce.7 = (bf16[768]{0:T(1024)(128)(2,1)S(1)}, bf16[384]{0:T(512)(128)(2,1)S(1)}, bf16[768]{0:T(1024)(128)(2,1)S(1)}) all-reduce(bf16[768]{0:T(1024)(128)(2,1)S(1)} %dynamic-update-slice, bf16[384]{0:T(512)(128)(2,1)S(1)} %dynamic-update-slice.1, ...), channel_id=1, replica_groups=mesh['dp'=16,'fsdp'=2] {'dp','fsdp'}, use_global_device_ids=true, to_apply=%add | all-reduce | flops 1920 | bytes 7680
  166.5 21.8 all-gather.11.cloned.1.call-done
  190.6 55.1 %conditional.6 = (f32[12,512]{1,0:T(8,128)S(1)}, bf16[512,768]{0,1:T(8,128)(2,1)}) conditional(s32[]{:T(128)} %bitcast.98, (s32[8]{0:T(128)S(1)}, bf16[512,768]{1,0:T(8,128)(2,1)S(1)}, bf16[512,768]{1,0:T(8,128)(2,1)S(1)}, f32[32,12]{1,0:T(8,128)S(1)}, bf16[512,768]{1,0:T(8,128)(2,1)S(1)}) %tuple.196, ...), branch_computations={%region_5.8_spmd, %region_8.11_spmd, %region_11.14_spmd, %region_1... | conditional | flops 839510528 | bytes 165348400
  190.8 14.2 gather_fusion
  249.5 59.9 %all-gather.17.cloned.1.call-done = bf16[3072,768]{1,0:T(8,128)(2,1)} async-done(((bf16[96,768]{1,0:T(8,128)(2,1)}), bf16[3072,768]{1,0:T(8,128)(2,1)}) %all-gather.17.cloned.1.call-update) | async-done | bytes 4718608 | tf_op jit(solution)/shard_map/all_gather | solution.py:213
  317.3 57.3 %all-gather.15.cloned.1.call-done = bf16[768,3072]{1,0:T(8,128)(2,1)} async-done(((bf16[24,3072]{1,0:T(8,128)(2,1)}), bf16[768,3072]{1,0:T(8,128)(2,1)}) %all-gather.15.cloned.1.call-update) | async-done | bytes 4718608 | tf_op jit(solution)/shard_map/all_gather | solution.py:212
  374.6 12.1 fusion.227
  393.1 97.7 %conditional.7 = (f32[32,12]{0,1:T(8,128)S(1)}, bf16[512,768]{0,1:T(8,128)(2,1)}, bf16[512,768]{0,1:T(8,128)(2,1)}, bf16[512,768]{0,1:T(8,128)(2,1)}) conditional(s32[]{:T(128)} %bitcast.98, (s32[8]{0:T(128)S(1)}, bf16[512,768]{1,0:T(8,128)(2,1)S(1)}, bf16[512,768]{1,0:T(8,128)(2,1)S(1)}, f32[32,12]{1,0:T(8,128)S(1)}, ...), branch_computations={%region_19.22_spmd, %region_22.25_spmd, %region_25.28_spmd, %regio... | conditional | flops 2268981760 | bytes 306982048
  404.6 14.1 gather_fusion.3
  504.1 76.1 %scatter_fusion.1 = f32[16,64,768]{2,1,0:T(8,128)} fusion(f32[16,64,768]{2,1,0:T(8,128)} %broadcast_in_dim.130, s32[512]{0:T(512)S(1)} %bitcast.378, f32[512,768]{1,0:T(8,128)} %gather_fusion.9), kind=kCustom, calls=%fused_computation.13 | custom fusion | bytes 4722688 | tf_op jit(solution)/shard_map/scatter | solution.py:306
  583.5 1830.7 %all-to-all-start.2 = ((bf16[16,64,768]{2,1,0:T(8,128)(2,1)}), bf16[16,64,768]{2,1,0:T(8,128)(2,1)S(1)}, u32[]{:S(2)}, u32[]{:S(2)}) async-start(bf16[16,64,768]{2,1,0:T(8,128)(2,1)} %convert_element_type.1093), calls=%async_computation.2 | async-start | bytes 3145728 | tf_op jit(solution)/shard_map/all_to_all | solution.py:308
  2415.5 31.8 all-to-all-done.2
  2447.3 10.7 scatter_custom_fusion.3
  2488.2 9.6 fusion.250
  2498.5 42.2 %all-reduce.6 = (f32[768]{0:T(1024)S(1)}, f32[384]{0:T(512)S(1)}, f32[768]{0:T(1024)S(1)}) all-reduce(f32[768]{0:T(1024)S(1)} %get-tuple-element.356, f32[384]{0:T(512)S(1)} %reshape.1694, f32[768]{0:T(1024)S(1)} %copy-done.58), channel_id=2, replica_groups=mesh['dp'=16,'fsdp'=2] {'dp','fsdp'}, use_global_device_ids=true, to_apply=%region_35.36.clone | all-reduce | flops 1920 | bytes 15360
  2542.4 9.4 add_convert_fusion
  2556.9 36.8 %reduce-scatter.7.cloned.1.call-done = f32[24,768]{1,0:T(8,128)} async-done(((f32[768,768]{1,0:T(8,128)}), f32[24,768]{1,0:T(8,128)}) %reduce-scatter.7.cloned.1.call-update) | async-done | bytes 73744 | tf_op jit(solution)/shard_map/reduce_scatter | solution.py:288
  2593.7 104.8 %reduce-scatter.9.cloned.1.call-done = f32[24,768]{1,0:T(8,128)} async-done(((f32[768,768]{1,0:T(8,128)}), f32[24,768]{1,0:T(8,128)}) %reduce-scatter.9.cloned.1.call-update) | async-done | bytes 73744 | tf_op jit(solution)/shard_map/reduce_scatter | solution.py:289
  2698.5 103.8 %reduce-scatter.11.cloned.1.call-done = f32[24,768]{1,0:T(8,128)} async-done(((f32[768,768]{1,0:T(8,128)}), f32[24,768]{1,0:T(8,128)}) %reduce-scatter.11.cloned.1.call-update) | async-done | bytes 73744 | tf_op jit(solution)/shard_map/reduce_scatter | solution.py:290
  2802.4 104.7 %reduce-scatter.13.cloned.1.call-done = f32[24,768]{1,0:T(8,128)} async-done(((f32[768,768]{1,0:T(8,128)}), f32[24,768]{1,0:T(8,128)}) %reduce-scatter.13.cloned.1.call-update) | async-done | bytes 73744 | tf_op jit(solution)/shard_map/reduce_scatter | solution.py:261
  2907.0 140.9 %reduce-scatter.15.cloned.1.call-done = f32[24,3072]{1,0:T(8,128)} async-done(((f32[768,3072]{1,0:T(8,128)}), f32[24,3072]{1,0:T(8,128)}) %reduce-scatter.15.cloned.1.call-update) | async-done | bytes 294928 | tf_op jit(solution)/shard_map/reduce_scatter | solution.py:255
  3048.0 142.1 %reduce-scatter.17.cloned.1.call-done = f32[96,768]{1,0:T(8,128)} async-done(((f32[3072,768]{1,0:T(8,128)}), f32[96,768]{1,0:T(8,128)}) %reduce-scatter.17.cloned.1.call-update) | async-done | bytes 294928 | tf_op jit(solution)/shard_map/reduce_scatter | solution.py:256
  (230 shorter events, 198.2 us)
Async XLA Ops:
  7.2 76.1 %copy-start = (bf16[2008,768]{1,0:T(8,128)(2,1)S(1)}, bf16[2008,768]{1,0:T(8,128)(2,1)}, u32[]{:S(2)}) copy-start(bf16[2008,768]{1,0:T(8,128)(2,1)} %param.24) | copy-start | bytes 9252868
  7.2 155.0 %all-gather.7.cloned.1.call-start = ((), (), s32[]{:S(2)}) async-start(), calls=%async_computation.9 | async-start | bytes 1216512 | tf_op jit(solution)/shard_map/all_gather | solution.py:206
  7.9 156.4 %all-gather.9.cloned.1.call-start = ((), (), s32[]{:S(2)}) async-start(), calls=%async_computation.10 | async-start | bytes 1216512 | tf_op jit(solution)/shard_map/all_gather | solution.py:207
  8.7 179.6 %all-gather.11.cloned.1.call-start = ((), (), s32[]{:S(2)}) async-start(), calls=%async_computation.11 | async-start | bytes 1216512 | tf_op jit(solution)/shard_map/all_gather | solution.py:208
  9.4 236.3 %all-gather.13.cloned.1.call-start = ((), (), s32[]{:S(2)}) async-start(), calls=%async_computation.12 | async-start | bytes 1216512 | tf_op jit(solution)/shard_map/all_gather | solution.py:209
  10.0 299.4 %all-gather.17.cloned.1.call-start = ((), (), s32[]{:S(2)}) async-start(), calls=%async_computation.14 | async-start | bytes 4866048 | tf_op jit(solution)/shard_map/all_gather | solution.py:213
  10.6 364.0 %all-gather.15.cloned.1.call-start = ((), (), s32[]{:S(2)}) async-start(), calls=%async_computation.13 | async-start | bytes 4866048 | tf_op jit(solution)/shard_map/all_gather | solution.py:212
  23.8 64.6 %copy-start.2 = (s32[512,1]{0,1:T(1,128)}, s32[512,1]{0,1:T(1,128)S(1)}, u32[]{:S(2)}) copy-start(s32[512,1]{0,1:T(1,128)S(1)} %get-tuple-element.373) | copy-start | bytes 6148
  88.5 66.2 %copy-start.59 = (s32[1,512]{1,0:T(1,128)S(1)}, s32[1,512]{1,0:T(1,128)}, u32[]{:S(2)}) copy-start(s32[1,512]{1,0:T(1,128)} %param.27) | copy-start | bytes 6148
  88.5 66.8 %all-to-all-start.1 = ((bf16[16,64,768]{2,1,0:T(8,128)(2,1)}), bf16[16,64,768]{2,1,0:T(8,128)(2,1)S(1)}, u32[]{:S(2)}, u32[]{:S(2)}) async-start(bf16[16,64,768]{2,1,0:T(8,128)(2,1)} %bitcast.404), calls=%async_computation.1 | async-start | bytes 3145728 | tf_op jit(solution)/shard_map/all_to_all | solution.py:197
  154.0 34.2 %copy-start.47 = (f32[768]{0:T(1024)}, f32[768]{0:T(1024)S(1)}, u32[]{:S(2)}) copy-start(f32[768]{0:T(1024)S(1)} %convert_element_type.1080) | copy-start | bytes 9220
  164.3 26.3 copy-start.66
  249.5 140.6 %copy-start.53 = (f32[512]{0:T(512)}, f32[512]{0:T(512)S(1)}, u32[]{:S(2)}) copy-start(f32[512]{0:T(512)S(1)} %fusion.247) | copy-start | bytes 6148
  249.5 125.1 %copy-start.45 = (f32[768]{0:T(1024)S(1)}, f32[768]{0:T(1024)}, u32[]{:S(2)}) copy-start(f32[768]{0:T(1024)} %convert_element_type.1085) | copy-start | bytes 9220
  580.3 1834.5 %copy-start.50 = (s32[16,1,64]{2,1,0:T(1,128)S(1)}, s32[16,1,64]{2,1,0:T(1,128)}, u32[]{:S(2)}) copy-start(s32[16,1,64]{2,1,0:T(1,128)} %copy-done.49) | copy-start | bytes 12292
  583.5 1863.8 %all-to-all-start.2 = ((bf16[16,64,768]{2,1,0:T(8,128)(2,1)}), bf16[16,64,768]{2,1,0:T(8,128)(2,1)S(1)}, u32[]{:S(2)}, u32[]{:S(2)}) async-start(bf16[16,64,768]{2,1,0:T(8,128)(2,1)} %convert_element_type.1093), calls=%async_computation.2 | async-start | bytes 3145728 | tf_op jit(solution)/shard_map/all_to_all | solution.py:308
  2414.2 137.6 %all-reduce.10.cloned.1.call-start = ((), (), s32[]{:S(2)}) async-start(), calls=%async_computation.15 | async-start | bytes 6168576 | tf_op jit(solution)/shard_map/psum | solution.py:316
  2462.8 130.9 %reduce-scatter.7.cloned.1.call-start = ((), (), s32[]{:S(2)}) async-start(), calls=%async_computation.16 | async-start | bytes 2433024 | tf_op jit(solution)/shard_map/reduce_scatter | solution.py:288
  2466.4 232.1 %reduce-scatter.9.cloned.1.call-start = ((), (), s32[]{:S(2)}) async-start(), calls=%async_computation.17 | async-start | bytes 2433024 | tf_op jit(solution)/shard_map/reduce_scatter | solution.py:289
  2470.0 332.3 %reduce-scatter.11.cloned.1.call-start = ((), (), s32[]{:S(2)}) async-start(), calls=%async_computation.18 | async-start | bytes 2433024 | tf_op jit(solution)/shard_map/reduce_scatter | solution.py:290
  2474.0 433.1 %reduce-scatter.13.cloned.1.call-start = ((), (), s32[]{:S(2)}) async-start(), calls=%async_computation.19 | async-start | bytes 2433024 | tf_op jit(solution)/shard_map/reduce_scatter | solution.py:261
  2477.6 570.4 %reduce-scatter.15.cloned.1.call-start = ((), (), s32[]{:S(2)}) async-start(), calls=%async_computation.20 | async-start | bytes 9732096 | tf_op jit(solution)/shard_map/reduce_scatter | solution.py:255
  2487.1 703.0 %reduce-scatter.17.cloned.1.call-start = ((), (), s32[]{:S(2)}) async-start(), calls=%async_computation.21 | async-start | bytes 9732096 | tf_op jit(solution)/shard_map/reduce_scatter | solution.py:256
  2542.4 647.7 %copy-start.1 = (bf16[2008,768]{1,0:T(8,128)(2,1)S(1)}, bf16[2008,768]{1,0:T(8,128)(2,1)}, u32[]{:S(2)}) copy-start(bf16[2008,768]{1,0:T(8,128)(2,1)} %param.24) | copy-start | bytes 9252868
  (35 other events, 164.2 us)
Sparse Core Ops, SparseCore 0:
  10.9 56.7 all-gather.6
  70.6 60.5 all-gather.8
  134.1 54.1 all-gather.10
  191.0 52.9 all-gather.12
  246.8 62.5 all-gather.16
  312.1 62.4 all-gather.14
  2462.9 24.5 all-reduce.9
  2493.4 100.2 reduce-scatter.6
  2600.4 98.0 reduce-scatter.8
  2704.2 98.0 reduce-scatter.10
  2809.1 97.9 reduce-scatter.12
  2913.4 134.5 reduce-scatter.14
  3055.5 134.5 reduce-scatter.16
where the time goes:
time: 3230 us; the launch traced here: 3200 us
  starting transfers between devices  1840 us (57%)
  waiting for transfers between devices  808 us (25%)
  local copies, waits for them, and re-layouts  225 us (7%)
  blocking collectives  118 us (4%)
  matrix products  114 us (4%)
  loops' own time  41.3 us (1%)
  other arithmetic  40.2 us (1%)
    all_to_all x1, starting transfers between devices, body(): lax.all_to_all(outgoing.astype(jnp.bfloat16), 'dp', split_axis=0, concat_...  1830 us
    reduce_scatter x1, waiting for transfers between devices, body(): lax.psum_scatter(grad_w_outer, ('dp', 'fsdp'), scatter_dimension=0, tiled...  142 us
    reduce_scatter x1, waiting for transfers between devices, body(): lax.psum_scatter(grad_w_inner, ('dp', 'fsdp'), scatter_dimension=0, tiled...  141 us
    reduce_scatter x1, waiting for transfers between devices, body(): lax.psum_scatter(grad_w_key, ('dp', 'fsdp'), scatter_dimension=0, tiled=T...  105 us
    reduce_scatter x1, waiting for transfers between devices, body(): lax.psum_scatter(grad_w_output, ('dp', 'fsdp'), scatter_dimension=0, tile...  105 us
    reduce_scatter x1, waiting for transfers between devices, body(): lax.psum_scatter(grad_w_value, ('dp', 'fsdp'), scatter_dimension=0, tiled...  104 us
    unnamed x2, blocking collectives  102 us
    scatter x1, local copies, waits for them, and re-layouts, body(): jnp.zeros((dp_count, slot_cap, D), jnp.float32).at[owners, slot_index]  76.1 us
  transfers between devices with their start and end apart: 15, of which 10 were waited for; matrix products, arithmetic and copies ran while one was open for 6% of the time, Pallas kernels for 0%

commit v1 on v0

v1 whole, which is shorter than its diff:
```python
from functools import partial

import jax
import jax.numpy as jnp
from jax import lax
from jax.experimental import pallas as pl
from jax.experimental.pallas import tpu as pltpu
from jax.sharding import PartitionSpec as P

D = 768
HEADS = 12
HEAD_DIM = 64
NB = 32
SHORT = 64
TOK_DEV = 512
TILE = 128
BIG = 1e9

EPSILON = 1e-06
THRESHOLDS = (12, 16, 23, 32, 46, 64, 91)
MESH = pl.DeviceIdType.MESH
F32 = jnp.float32
BF16 = jnp.bfloat16
ANY = pl.BlockSpec(memory_space=pl.ANY)
VMEM = pl.BlockSpec(memory_space=pltpu.VMEM)
SMEM = pl.BlockSpec(memory_space=pltpu.SMEM)
ALL = slice(None)


def relative_bucket(offset):
    distance = jnp.abs(offset)
    far_bucket = 8 + sum(((distance >= threshold).astype(jnp.int32) for threshold in THRESHOLDS))
    near_far = jnp.where(distance < 8, distance, jnp.minimum(far_bucket, 15))
    return near_far + 16 * (offset > 0).astype(jnp.int32)


def normalize(activations, gains):
    return (
        activations
        * lax.rsqrt(jnp.mean(activations * activations, axis=-1, keepdims=True) + EPSILON)
        * gains
    )


def lowered(array_in):
    return array_in.astype(BF16)


def plain_product(left_side, right_side):
    return jnp.dot(left_side, right_side, preferred_element_type=F32)


def gram_product(left_side, right_side):
    return lax.dot_general(
        left_side, right_side, (((0,), (0,)), ((), ())), preferred_element_type=F32
    )


def back_product(left_side, right_side):
    return lax.dot_general(
        left_side, right_side, (((1,), (1,)), ((), ())), preferred_element_type=F32
    )


def chip_grid(chips):
    depth = 4 if chips % 4 == 0 else 1
    rest = chips // depth
    tall = max(part for part in range(1, rest + 1) if rest % part == 0 and part * part <= rest)
    return depth, tall, rest // tall


class Place:
    def __init__(self, dims):
        self.dims = dims
        self.count = dims[0] * dims[1] * dims[2]
        self.dp = lax.axis_index("dp")
        self.core = lax.axis_index("fsdp")
        self.at = (
            self.dp // (dims[1] * dims[2]),
            (self.dp // dims[2]) % dims[1],
            self.dp % dims[2],
        )

    def peer(self, axis, step):
        spot = list(self.at)
        spot[axis] = (spot[axis] + step) % self.dims[axis]
        return spot[axis], ((spot[0] * self.dims[1] + spot[1]) * self.dims[2] + spot[2], self.core)

    def other(self, step):
        return (self.dp + step) % self.count, ((self.dp + step) % self.count, self.core)

    def sibling(self):
        return (self.dp, 1 - self.core)


def remote(source, target, send, recv, device):
    return pltpu.make_async_remote_copy(
        src_ref=source,
        dst_ref=target,
        send_sem=send,
        recv_sem=recv,
        device_id=device,
        device_id_type=MESH,
    )


def enter(place):
    barrier = pltpu.get_barrier_semaphore()

    def greet(step, carry):
        pl.semaphore_signal(barrier, inc=1, device_id=place.other(step)[1], device_id_type=MESH)
        return carry

    lax.fori_loop(1, place.count, greet, 0)
    pl.semaphore_signal(barrier, inc=1, device_id=place.sibling(), device_id_type=MESH)
    pl.semaphore_wait(barrier, place.count)


def pieces_of(square, inner, outer):
    found = []

    def columns(ref, width, shift, span):
        def view(z, y, x, core):
            start = pl.multiple_of(core * span + shift, TILE)
            return ref.at[z, y, x, :, pl.ds(start, width)]

        return view

    def rows(ref, width, shift):
        def view(z, y, x, core):
            return ref.at[z, y, x, core, :, pl.ds(shift, width)]

        return view

    for half in range(2):
        width = outer.shape[-1] // 2
        found.append((rows(outer, width, half * width), half, (outer.shape[-2], width)))
    for half in range(2):
        width = inner.shape[-1] // 4
        view = columns(inner, width, half * width, 2 * width)
        found.append((view, half, (inner.shape[-2], width)))
    for number, ref in enumerate(square):
        width = ref.shape[-1] // 2
        view = columns(ref, width, 0, width)
        found.append((view, number % 2, (ref.shape[-2], width)))
    return found


GATHER_ORDER = ((0, 1, 2), (0, 2, 1))
REDUCE_ORDER = ((2, 1, 0), (1, 2, 0))


def fetch_kernel(
    dims,
    cap,
    asks,
    table,
    w_query,
    w_key,
    w_value,
    w_output,
    w_inner,
    w_outer,
    small,
    rows_out,
    asked_out,
    full_query,
    full_key,
    full_value,
    full_output,
    full_inner,
    full_outer,
    full_small,
    got,
    near_square,
    near_inner,
    block_square,
    block_inner,
    ids_turned,
    one_hot,
    found,
    ask_send,
    ask_recv,
    row_send,
    row_recv,
    pair_send,
    pair_recv,
    local_sem,
    axis_send,
    axis_recv,
    core_send,
    core_recv,
):
    place = Place(dims)
    me, core = place.dp, place.core
    count = place.count
    enter(place)

    def ask_copy(step):
        peer, device = place.other(step)
        return remote(
            asks.at[peer], got.at[me], ask_send.at[step - 1], ask_recv.at[step - 1], device
        )

    def send_ask(step, carry):
        ask_copy(step).start()
        return carry

    lax.fori_loop(1, count, send_ask, 0)
    got[pl.ds(me, 1)] = asks[pl.ds(me, 1)]

    squares = (w_query, w_key, w_value, w_output)
    pair_copies = [
        remote(ref, near_square.at[number], pair_send.at[number], pair_recv.at[number], place.sibling())
        for number, ref in enumerate(squares)
    ]
    pair_copies.append(remote(w_inner, near_inner, pair_send.at[4], pair_recv.at[4], place.sibling()))
    for copy in pair_copies:
        copy.start()

    pieces = pieces_of((full_query, full_key, full_value, full_output), full_inner, full_outer)
    pieces.append((lambda z, y, x, c: full_small.at[z, y, x, c], 0, small.shape))
    half_outer = w_outer.shape[-1] // 2
    half_inner = block_inner.shape[-1] // 2
    sources = [w_outer.at[:, pl.ds(half * half_outer, half_outer)] for half in range(2)]
    sources += [block_inner.at[:, pl.ds(half * half_inner, half_inner)] for half in range(2)]
    sources += [block_square.at[number] for number in range(4)]
    sources += [small]

    def axis_copies(piece, phase):
        view, order, _ = pieces[piece]
        order = GATHER_ORDER[order]
        axis = order[phase]
        pick = [ALL if a in order[:phase] else place.at[a] for a in range(3)]
        here = view(*pick, core)
        source = sources[piece] if phase == 0 else here
        return [
            remote(
                source,
                here,
                axis_send.at[piece, phase, step - 1],
                axis_recv.at[piece, phase, step - 1],
                place.peer(axis, step)[1],
            )
            for step in range(1, dims[axis])
        ]

    def core_copy(piece):
        here = pieces[piece][0](ALL, ALL, ALL, core)
        return remote(here, here, core_send.at[piece], core_recv.at[piece], place.sibling())

    def keep_copy(piece):
        return pltpu.make_async_copy(
            sources[piece], pieces[piece][0](*place.at, core), local_sem.at[piece]
        )

    def begin(piece):
        keep_copy(piece).start()
        for copy in axis_copies(piece, 0):
            copy.start()

    for piece in (0, 1, 8):
        begin(piece)

    for copy in pair_copies:
        copy.wait()

    def joined(mine, theirs):
        mine, theirs = mine.astype(F32), theirs.astype(F32)
        both = jnp.concatenate(
            [jnp.where(core == 0, mine, theirs), jnp.where(core == 0, theirs, mine)], axis=0
        )
        half = both.shape[1] // 2
        return lowered(jnp.where(core == 0, both[:, :half], both[:, half:]))

    for number, ref in enumerate(squares):
        block_square[number] = joined(ref[...], near_square[number])
    block_inner[...] = joined(w_inner[...], near_inner[...])

    def wait_ask(step, carry):
        ask_copy(step).wait()
        return carry

    lax.fori_loop(1, count, wait_ask, 0)

    turned_rows = jnp.zeros((TILE, TILE), F32)
    ids_turned[...] = turned_rows
    ids_turned[pl.ds(0, count)] = got[:, 0, :].astype(F32)
    ids_turned[...] = jnp.transpose(ids_turned[...])
    table_rows = table.shape[0]
    group = max(1, min(count, 256 // cap))

    def find_group(number, carry):
        lanes = lax.broadcasted_iota(jnp.int32, (cap, TILE), 1)
        spots = lax.broadcasted_iota(jnp.int32, (cap, table_rows), 1)
        for inside in range(group):
            block = number * group + inside
            ids = jnp.sum(
                jnp.where(lanes == block, ids_turned[0:cap, :], 0.0), axis=1, keepdims=True
            ).astype(jnp.int32)
            one_hot[inside * cap : (inside + 1) * cap, :] = (spots == ids).astype(F32).astype(BF16)
        rows = lowered(plain_product(one_hot[...], table[...]))
        for inside in range(group):
            block = number * group + inside
            found[pl.ds(block, 1)] = rows[inside * cap : (inside + 1) * cap][None]

            @pl.when(block != me)
            def _():
                row_copy(block).start()

        return carry

    def row_copy(block):
        return remote(
            found.at[block], rows_out.at[me], row_send.at[block], row_recv.at[me], (block, core)
        )

    def row_arrival(block):
        return remote(
            found.at[block], rows_out.at[block], row_send.at[block], row_recv.at[block], (block, core)
        )

    lax.fori_loop(0, count // group, find_group, 0)
    own_rows = pltpu.make_async_copy(found.at[me], rows_out.at[me], local_sem.at[9])
    own_rows.start()
    own_asks = pltpu.make_async_copy(got, asked_out.at[core], local_sem.at[10])
    own_asks.start()
    asks_across = remote(got, asked_out.at[core], pair_send.at[5], pair_recv.at[5], place.sibling())
    asks_across.start()

    for piece in range(2, 8):
        begin(piece)

    total = len(pieces)
    for turn in range(total + 3):
        for phase in (3, 2, 1):
            piece = turn + 1 - phase
            if not 0 <= piece < total:
                continue
            for copy in axis_copies(piece, phase - 1):
                copy.wait_recv()
            if phase == 1:
                keep_copy(piece).wait()
            if phase < 3:
                for copy in axis_copies(piece, phase):
                    copy.start()
            else:
                core_copy(piece).start()

    def wait_row(block, carry):
        @pl.when(block != me)
        def _():
            row_copy(block).wait_send()
            row_arrival(block).wait_recv()

        return carry

    lax.fori_loop(0, count, wait_row, 0)
    own_rows.wait()
    own_asks.wait()
    asks_across.wait()
    for piece in range(total):
        for phase in range(3):
            for copy in axis_copies(piece, phase):
                copy.wait_send()
        core_copy(piece).wait()


def fetch(dims, asks, table, squares, w_inner, w_outer, small):
    count = dims[0] * dims[1] * dims[2]
    cap = 2 * TOK_DEV // count
    rows = 2 * squares[0].shape[0]
    shapes = (
        [((count, cap, D), BF16), ((2, *asks.shape), jnp.int32)]
        + [((*dims, rows, D), BF16)] * 4
        + [
            ((*dims, rows, w_inner.shape[1]), BF16),
            ((*dims, 2, *w_outer.shape), BF16),
            ((*dims, 2, *small.shape), BF16),
        ]
    )
    steps = max(dims) - 1
    dma = pltpu.SemaphoreType.DMA
    return pl.pallas_call(
        partial(fetch_kernel, dims, cap),
        out_shape=[jax.ShapeDtypeStruct(*shape) for shape in shapes],
        in_specs=[VMEM] * 9,
        out_specs=[ANY] * 9,
        scratch_shapes=[
            pltpu.VMEM(asks.shape, jnp.int32),
            pltpu.VMEM((4, *squares[0].shape), BF16),
            pltpu.VMEM(w_inner.shape, BF16),
            pltpu.VMEM((4, rows, D // 2), BF16),
            pltpu.VMEM((rows, w_inner.shape[1] // 2), BF16),
            pltpu.VMEM((TILE, TILE), F32),
            pltpu.VMEM((max(1, min(count, 256 // cap)) * cap, table.shape[0]), BF16),
            pltpu.VMEM((count, cap, D), BF16),
            dma((count - 1,)),
            dma((count - 1,)),
            dma((count,)),
            dma((count,)),
            dma((6,)),
            dma((6,)),
            dma((11,)),
            dma((9, 3, steps)),
            dma((9, 3, steps)),
            dma((9,)),
            dma((9,)),
        ],
        compiler_params=pltpu.CompilerParams(
            collective_id=1, has_side_effects=True, vmem_limit_bytes=40 * 2**20
        ),
        name="fetch",
    )(asks, table, *squares, w_inner, w_outer, small)


def reduce_kernel(
    dims,
    grad_query,
    grad_key,
    grad_value,
    grad_output,
    grad_inner,
    grad_outer,
    small,
    leaving,
    out_query,
    out_key,
    out_value,
    out_output,
    out_inner,
    out_outer,
    out_small,
    incoming,
    *scratch,
):
    place = Place(dims)
    me, core = place.dp, place.core
    count = place.count
    scratch = list(scratch)
    held = [scratch.pop(0) for _ in range(8)]
    across = [scratch.pop(0) for _ in range(8)]
    arrived = [[scratch.pop(0) for _ in range(3)] for _ in range(8)]
    final = [scratch.pop(0) for _ in range(8)]
    small_in, small_sum, small_pair = (scratch.pop(0) for _ in range(3))
    (
        row_send,
        row_recv,
        over_send,
        over_recv,
        small_send,
        small_recv,
        pair_send,
        pair_recv,
        local_sem,
        axis_send,
        axis_recv,
        end_send,
        end_recv,
    ) = scratch
    enter(place)

    def row_copy(step):
        peer, device = place.other(step)
        return remote(
            leaving.at[peer], incoming.at[core, me], row_send.at[step], row_recv.at[step], device
        )

    def over_copy(step):
        owner = (me - step + count) % count
        here = incoming.at[core, owner]
        return remote(here, here, over_send.at[step], over_recv.at[step], place.sibling())

    def send_row(step, carry):
        row_copy(step).start()
        return carry

    lax.fori_loop(1, count, send_row, 0)
    own_row = pltpu.make_async_copy(leaving.at[me], incoming.at[core, me], local_sem.at[8])
    own_row.start()

    def small_copy(step):
        peer, device = place.other(step)
        return remote(
            small.at[peer], small_in.at[me], small_send.at[step - 1], small_recv.at[step - 1], device
        )

    def send_small(step, carry):
        small_copy(step).start()
        return carry

    lax.fori_loop(1, count, send_small, 0)
    small_in[pl.ds(me, 1)] = small[pl.ds(me, 1)]

    pieces = pieces_of((grad_query, grad_key, grad_value, grad_output), grad_inner, grad_outer)
    total = len(pieces)

    def pair_copy(piece):
        theirs = pieces[piece][0](ALL, ALL, ALL, 1 - core)
        return remote(theirs, across[piece], pair_send.at[piece], pair_recv.at[piece], place.sibling())

    def load_copy(piece):
        mine = pieces[piece][0](ALL, ALL, ALL, core)
        return pltpu.make_async_copy(mine, held[piece], local_sem.at[piece])

    def axis_copies(piece, phase):
        order = REDUCE_ORDER[pieces[piece][1]]
        axis = order[phase]
        copies = []
        for step in range(1, dims[axis]):
            spot, device = place.peer(axis, step)
            pick = [
                spot if a == axis else (place.at[a] if a in order[:phase] else ALL)
                for a in range(3)
            ]
            copies.append(
                remote(
                    held[piece].at[pick[0], pick[1], pick[2]],
                    arrived[piece][phase].at[step - 1],
                    axis_send.at[piece, phase, step - 1],
                    axis_recv.at[piece, phase, step - 1],
                    device,
                )
            )
        return copies

    def add_across(piece):
        def one(index, carry):
            z, y, x = index // (dims[1] * dims[2]), (index // dims[2]) % dims[1], index % dims[2]
            held[piece][z, y, x] = held[piece][z, y, x] + across[piece][z, y, x]
            return carry

        lax.fori_loop(0, count, one, 0)

    def add_arrived(piece, phase):
        order = REDUCE_ORDER[pieces[piece][1]]
        free = [a for a in range(3) if a not in order[: phase + 1]]
        amount = 1
        for a in free:
            amount *= dims[a]

        def one(index, carry):
            spot = list(place.at)
            inner_spot = []
            rest = index
            for a in reversed(free):
                spot[a] = rest % dims[a]
                inner_spot.insert(0, rest % dims[a])
                rest = rest // dims[a]
            value = held[piece][tuple(spot)]
            for step in range(dims[order[phase]] - 1):
                value = value + arrived[piece][phase][(step, *inner_spot)]
            held[piece][tuple(spot)] = value
            return carry

        lax.fori_loop(0, amount, one, 0)

    outs = [out_outer, out_outer, out_inner, out_inner, out_query, out_key, out_value, out_output]

    def end_copies(piece):
        rows, width = pieces[piece][2]
        out = outs[piece]
        if piece < 2:
            half = pl.ds((piece % 2) * width, width)
            return [pltpu.make_async_copy(final[piece], out.at[:, half], end_send.at[piece])]
        span = 2 * width if piece < 4 else width
        shift = (piece % 2) * width if piece < 4 else 0
        part = out.at[:, pl.ds(pl.multiple_of(core * span + shift, TILE), width)]
        return [
            pltpu.make_async_copy(final[piece].at[core], part, local_sem.at[9 + piece]),
            remote(
                final[piece].at[1 - core],
                part,
                end_send.at[piece],
                end_recv.at[piece],
                place.sibling(),
            ),
        ]

    def finish(piece):
        value = held[piece][place.at].astype(F32)
        for step in range(dims[0] - 1):
            value = value + arrived[piece][2][step].astype(F32)
        if piece < 2:
            final[piece][...] = value
        else:
            half = value.shape[0] // 2
            final[piece][0] = value[:half]
            final[piece][1] = value[half:]
        for copy in end_copies(piece):
            copy.start()

    for piece in range(total):
        load_copy(piece).start()
        pair_copy(piece).start()

    for turn in range(total + 3):
        for phase in (3, 2, 1, 0):
            piece = turn - phase
            if not 0 <= piece < total:
                continue
            if phase == 0:
                load_copy(piece).wait()
                pair_copy(piece).wait_recv()
                add_across(piece)
            else:
                for copy in axis_copies(piece, phase - 1):
                    copy.wait_recv()
                if phase < 3:
                    add_arrived(piece, phase - 1)
            if phase < 3:
                for copy in axis_copies(piece, phase):
                    copy.start()
            else:
                finish(piece)

    def pass_over(step, carry):
        row_copy(step).wait()
        over_copy(step).start()
        return carry

    own_row.wait()
    over_copy(0).start()
    lax.fori_loop(1, count, pass_over, 0)

    def wait_small(step, carry):
        small_copy(step).wait()
        return carry

    lax.fori_loop(1, count, wait_small, 0)
    small_sum[...] = jnp.sum(small_in[...], axis=0)
    small_across = remote(
        small_sum, small_pair, pair_send.at[total], pair_recv.at[total], place.sibling()
    )
    small_across.start()
    small_across.wait()
    out_small[...] = small_sum[...] + small_pair[...]

    def wait_over(step, carry):
        over_copy(step).wait()
        return carry

    lax.fori_loop(0, count, wait_over, 0)
    for piece in range(total):
        pair_copy(piece).wait_send()
        for phase in range(3):
            for copy in axis_copies(piece, phase):
                copy.wait_send()
        for copy in end_copies(piece):
            copy.wait()


def reduce_grads(dims, squares, inner, outer, small, leaving):
    count = dims[0] * dims[1] * dims[2]
    rows, width = squares[0].shape[3], squares[0].shape[4]
    blocks = [(outer.shape[4], outer.shape[5] // 2)] * 2
    blocks += [(rows, inner.shape[4] // 4)] * 2
    blocks += [(rows, width // 2)] * 4
    orders = [0, 1, 0, 1, 0, 1, 0, 1]
    scratch = [pltpu.VMEM((*dims, *block), BF16) for block in blocks] * 2
    for block, order in zip(blocks, orders):
        order = REDUCE_ORDER[order]
        for phase in range(3):
            free = [dims[a] for a in range(3) if a not in order[: phase + 1]]
            scratch.append(pltpu.VMEM((dims[order[phase]] - 1, *free, *block), BF16))
    for number, (high, wide) in enumerate(blocks):
        scratch.append(
            pltpu.VMEM((high, wide) if number < 2 else (2, high // 2, wide), F32)
        )
    scratch += [pltpu.VMEM(small.shape, F32)] + [pltpu.VMEM(small.shape[1:], F32)] * 2
    steps = max(dims) - 1
    dma = pltpu.SemaphoreType.DMA
    scratch += [
        dma((count,)),
        dma((count,)),
        dma((count,)),
        dma((count,)),
        dma((count - 1,)),
        dma((count - 1,)),
        dma((9,)),
        dma((9,)),
        dma((17,)),
        dma((8, 3, steps)),
        dma((8, 3, steps)),
        dma((8,)),
        dma((8,)),
    ]
    shapes = [((rows // 2, width), F32)] * 4 + [
        ((rows // 2, inner.shape[4]), F32),
        ((outer.shape[4], outer.shape[5]), F32),
        (small.shape[1:], F32),
        ((2, *leaving.shape), BF16),
    ]
    return pl.pallas_call(
        partial(reduce_kernel, dims),
        out_shape=[jax.ShapeDtypeStruct(*shape) for shape in shapes],
        in_specs=[ANY] * 6 + [VMEM, ANY],
        out_specs=[ANY] * 6 + [VMEM, ANY],
        scratch_shapes=scratch,
        compiler_params=pltpu.CompilerParams(
            collective_id=2, has_side_effects=True, vmem_limit_bytes=48 * 2**20
        ),
        name="reduce",
    )(*squares, inner, outer, small, leaving)


def near_tile(row):
    wide = jnp.broadcast_to(row, (TILE, 2 * TILE))
    return pltpu.roll(wide, 0, 1, stride=1, stride_axis=0)[:, :TILE]


def diagonal_sums(tile):
    wide = jnp.concatenate([tile, jnp.zeros((TILE, TILE), F32)], axis=1)
    group = wide[:8]
    for first in range(8, TILE, 8):
        group = group + pltpu.roll(wide[first : first + 8], 2 * TILE - first, 1)
    line = group[:1]
    for row in range(1, 8):
        line = line + pltpu.roll(group[row : row + 1], 2 * TILE - row, 1)
    return line


def pair_mask(shape, axis, head):
    place = lax.broadcasted_iota(jnp.int32, shape, axis)
    return (place // HEAD_DIM) == head


def attend_kernel(far, key, query_t, value_t, feature_k, feature_q, near, attended_t, prob):
    pair = pl.program_id(0)
    tiles = TOK_DEV // TILE
    for head in range(2):
        number = pair * 2 + head
        ahead = far[31 * HEADS + number]
        behind = far[15 * HEADS + number]
        lane = lax.broadcasted_iota(jnp.int32, (TOK_DEV, TILE), 1) - 8
        key_tile = lax.broadcasted_iota(jnp.int32, (TOK_DEV, TILE), 0) // TILE
        inside = (lane >= 0) & (lane < tiles)
        extra = jnp.where(
            inside & (key_tile - lane >= 2),
            ahead,
            jnp.where(inside & (key_tile - lane <= -2), behind, 0.0),
        )
        feature = lowered(feature_k[...].astype(F32) + extra)
        masked_key = jnp.where(pair_mask((TOK_DEV, TILE), 1, head), key[...].astype(F32), 0.0)
        left = jnp.concatenate([lowered(masked_key), feature], axis=1)
        bias = [near_tile(near[head, kind : kind + 1, :]) for kind in range(3)]
        for strip in range(2):
            lanes = slice(strip * 256, (strip + 1) * 256)
            right = jnp.concatenate([query_t[:, lanes], feature_q[:, lanes]], axis=0)
            scores = plain_product(left, right)
            rows = []
            for key_block in range(tiles):
                parts = []
                for inner in range(2):
                    query_block = strip * 2 + inner
                    part = scores[
                        key_block * TILE : (key_block + 1) * TILE, inner * TILE : (inner + 1) * TILE
                    ]
                    gap = key_block - query_block
                    if abs(gap) <= 1:
                        part = part + bias[gap + 1]
                    parts.append(part)
                rows.append(jnp.concatenate(parts, axis=1))
            scores = jnp.concatenate(rows, axis=0)
            peak = jnp.max(scores, axis=0, keepdims=True)
            powers = jnp.exp(scores - peak)
            share = 1.0 / jnp.sum(powers, axis=0, keepdims=True)
            weights = lowered(powers * share)
            prob[head, :, lanes] = weights
            attended_t[head * HEAD_DIM : (head + 1) * HEAD_DIM, lanes] = lowered(
                plain_product(value_t[head * HEAD_DIM : (head + 1) * HEAD_DIM, :], weights)
            )


def attend(far, key, query_t, value_t, feature_k, feature_q, near):
    wide = pl.BlockSpec((TOK_DEV, TILE), lambda pair: (0, pair))
    tall = pl.BlockSpec((TILE, TOK_DEV), lambda pair: (pair, 0))
    return pl.pallas_call(
        attend_kernel,
        grid=(HEADS // 2,),
        in_specs=[
            SMEM,
            wide,
            tall,
            tall,
            pl.BlockSpec((TOK_DEV, TILE), lambda pair: (0, 0)),
            pl.BlockSpec((TILE, TOK_DEV), lambda pair: (0, 0)),
            pl.BlockSpec((2, 3, 2 * TILE), lambda pair: (pair, 0, 0)),
        ],
        out_specs=[tall, pl.BlockSpec((2, TOK_DEV, TOK_DEV), lambda pair: (pair, 0, 0))],
        out_shape=[
            jax.ShapeDtypeStruct((D, TOK_DEV), BF16),
            jax.ShapeDtypeStruct((HEADS, TOK_DEV, TOK_DEV), BF16),
        ],
        compiler_params=pltpu.CompilerParams(vmem_limit_bytes=40 * 2**20),
        name="attend",
    )(far, key, query_t, value_t, feature_k, feature_q, near)


def attend_back_kernel(
    prob, value, grad_t, attended_t, grad, query, key_t, grad_value, grad_key, grad_query_t, bias_sums
):
    tiles = TOK_DEV // TILE
    value_sum = jnp.zeros((TOK_DEV, TILE), F32)
    key_sum = jnp.zeros((TOK_DEV, TILE), F32)
    for head in range(2):
        own = slice(head * HEAD_DIM, (head + 1) * HEAD_DIM)
        mask = pair_mask((TOK_DEV, TILE), 1, head)
        masked = [
            lowered(jnp.where(mask, ref[...].astype(F32), 0.0)) for ref in (value, grad, query)
        ]
        inner = jnp.sum(
            grad_t[own, :].astype(F32) * attended_t[own, :].astype(F32), axis=0, keepdims=True
        )
        strips = []
        near_sums = [jnp.zeros((TILE, TILE), F32) for _ in range(3)]
        far_sums = [jnp.zeros((TILE, TILE), F32) for _ in range(2)]
        for strip in range(2):
            lanes = slice(strip * 256, (strip + 1) * 256)
            grad_prob = plain_product(masked[0], grad_t[:, lanes])
            scores = lowered(prob[head, :, lanes].astype(F32) * (grad_prob - inner[:, lanes]))
            strips.append(scores)
            wide = scores.astype(F32)
            for key_block in range(tiles):
                for part in range(2):
                    gap = key_block - (strip * 2 + part)
                    tile = wide[
                        key_block * TILE : (key_block + 1) * TILE, part * TILE : (part + 1) * TILE
                    ]
                    if abs(gap) <= 1:
                        near_sums[gap + 1] = near_sums[gap + 1] + tile
                    else:
                        far_sums[gap > 0] = far_sums[gap > 0] + tile
        scores = jnp.concatenate(strips, axis=1)
        value_sum = value_sum + plain_product(prob[head], masked[1])
        key_sum = key_sum + plain_product(scores, masked[2])
        grad_query_t[own, :] = lowered(plain_product(key_t[own, :], scores))
        rows = []
        for tile in near_sums:
            rows.append(diagonal_sums(tile))
        for tile in far_sums:
            line = jnp.sum(tile, axis=0, keepdims=True)
            rows.append(jnp.concatenate([line, jnp.zeros((1, TILE), F32)], axis=1))
        rows.append(jnp.zeros((3, 2 * TILE), F32))
        bias_sums[head] = jnp.concatenate(rows, axis=0)
    grad_value[...] = lowered(value_sum)
    grad_key[...] = lowered(key_sum)


def attend_back(prob, value, grad_t, attended_t, grad, query, key_t):
    wide = pl.BlockSpec((TOK_DEV, TILE), lambda pair: (0, pair))
    tall = pl.BlockSpec((TILE, TOK_DEV), lambda pair: (pair, 0))
    return pl.pallas_call(
        attend_back_kernel,
        grid=(HEADS // 2,),
        in_specs=[
            pl.BlockSpec((2, TOK_DEV, TOK_DEV), lambda pair: (pair, 0, 0)),
            wide,
            tall,
            tall,
            wide,
            wide,
            tall,
        ],
        out_specs=[wide, wide, tall, pl.BlockSpec((2, 8, 2 * TILE), lambda pair: (pair, 0, 0))],
        out_shape=[
            jax.ShapeDtypeStruct((TOK_DEV, D), BF16),
            jax.ShapeDtypeStruct((TOK_DEV, D), BF16),
            jax.ShapeDtypeStruct((D, TOK_DEV), BF16),
            jax.ShapeDtypeStruct((HEADS, 8, 2 * TILE), F32),
        ],
        compiler_params=pltpu.CompilerParams(vmem_limit_bytes=40 * 2**20),
        name="attend_back",
    )(prob, value, grad_t, attended_t, grad, query, key_t)


def collect_kernel(ids, incoming, out):
    high = out.shape[0]
    first = pl.program_id(0) * high
    rows = lax.broadcasted_iota(jnp.int32, (high, ids.shape[1]), 0) + first
    picked = (rows == ids[...]).astype(F32).astype(BF16)
    out[...] = plain_product(picked, incoming[...])


def collect(ids, incoming, owner_rows):
    high = 256
    return pl.pallas_call(
        collect_kernel,
        grid=(-(-owner_rows // high),),
        in_specs=[
            pl.BlockSpec(ids.shape, lambda step: (0, 0)),
            pl.BlockSpec(incoming.shape, lambda step: (0, 0)),
        ],
        out_specs=pl.BlockSpec((high, D), lambda step: (step, 0)),
        out_shape=jax.ShapeDtypeStruct((owner_rows, D), F32),
        compiler_params=pltpu.CompilerParams(vmem_limit_bytes=40 * 2**20),
        name="collect",
    )(ids, incoming)


def near_places():
    lane = jnp.arange(2 * TILE, dtype=jnp.int32)
    gap = jnp.where(lane < TILE, lane, lane - 2 * TILE)
    kinds = jnp.arange(3, dtype=jnp.int32)[:, None] - 1
    return relative_bucket(kinds * TILE - gap[None, :])


def body(
    dims,
    table,
    row_in_owner,
    send_counts,
    row_order,
    bucket,
    lengths,
    norm1_gain,
    w_query,
    w_key,
    w_value,
    w_output,
    position_bias,
    norm2_gain,
    w_inner,
    w_outer,
    cotangent,
):
    dp_count = dims[0] * dims[1] * dims[2]
    cap = 2 * TOK_DEV // dp_count
    owner_rows = table.shape[0]
    core = lax.axis_index("fsdp")
    counts_row = send_counts[0]
    owner_ids = jnp.arange(dp_count, dtype=jnp.int32)
    send_ends = jnp.sum(
        jnp.where(owner_ids[None, :] <= owner_ids[:, None], counts_row[None, :], 0), axis=1
    )
    send_starts = send_ends - counts_row
    places = jnp.arange(TOK_DEV, dtype=jnp.int32)
    lanes = jnp.arange(TILE, dtype=jnp.int32)
    wanted = send_starts[:, None] + lanes[None, :]
    asks = jnp.sum(
        jnp.where(wanted[:, :, None] == places[None, None, :], row_in_owner[None, None, :], 0), axis=2
    )
    asks = jnp.where((lanes[None, :] < counts_row[:, None]) & (lanes[None, :] < cap), asks, -1)
    asks = jnp.broadcast_to(asks[:, None, :], (dp_count, 8, TILE))
    past = (places[:, None] >= send_ends[None, :]).astype(jnp.int32)
    owners = jnp.sum(past, axis=1, dtype=jnp.int32)
    owner_start = jnp.sum(past * counts_row[None, :], axis=1, dtype=jnp.int32)
    slots = owners * cap + places - owner_start
    token_slot = jnp.sum(jnp.where(row_order[0][None, :] == places[:, None], slots[None, :], 0), axis=1)
    all_slots = jnp.arange(dp_count * cap, dtype=jnp.int32)
    spread = (token_slot[:, None] == all_slots[None, :]).astype(BF16)
    spread_t = (all_slots[:, None] == token_slot[None, :]).astype(BF16)

    shard = norm1_gain.shape[0]
    bias_shard = position_bias.shape[0]
    small = jnp.zeros((16, TILE), BF16)
    small = small.at[0, :shard].set(norm1_gain).at[1, :shard].set(norm2_gain)
    small = small.at[2, :bias_shard].set(position_bias)
    rows, asked, *gathered = fetch(
        dims, asks, table, (w_query, w_key, w_value, w_output), w_inner, w_outer, small
    )
    wq_full, wk_full, wv_full, wo_full = (part.reshape(D, D) for part in gathered[:4])
    inner_full = gathered[4].reshape(D, -1)
    outer_full = gathered[5].reshape(-1, D)
    small_full = gathered[6].reshape(2 * dp_count, 16, TILE)
    gain_one = small_full[:, 0, :shard].reshape(1, D).astype(F32)
    gain_two = small_full[:, 1, :shard].reshape(1, D).astype(F32)
    bias_flat = small_full[:, 2, :bias_shard].reshape(NB * HEADS)
    bias_table = bias_flat.reshape(NB, HEADS)

    embedded = plain_product(spread, rows.reshape(dp_count * cap, D))
    normed = lowered(normalize(embedded, gain_one))

    span_shift = 6 + bucket[0]
    document = places >> span_shift
    within = places - (document << span_shift)
    doc_ids = jnp.arange(8, dtype=jnp.int32)
    doc_length = jnp.sum(jnp.where(document[:, None] == doc_ids[None, :], lengths[None, :], 0), axis=1)
    usable = (document[:, None] == doc_ids[None, :]) & (within < doc_length)[:, None]
    feature_k = jnp.pad(jnp.where(usable, 0.0, -BIG).astype(BF16), ((0, 0), (0, TILE - 8)))
    feature_q = jnp.concatenate(
        [
            (doc_ids[:, None] == document[None, :]).astype(BF16),
            (jnp.arange(8, dtype=jnp.int32)[:, None] == (places // TILE)[None, :]).astype(BF16),
            jnp.zeros((TILE - 16, TOK_DEV), BF16),
        ],
        axis=0,
    )
    near_hot = (near_places().reshape(-1)[None, :] == jnp.arange(NB, dtype=jnp.int32)[:, None]).astype(BF16)
    near = gram_product(bias_table, near_hot).reshape(HEADS, 3, 2 * TILE)

    queries = lowered(plain_product(normed, wq_full))
    key_rows = lowered(plain_product(normed, wk_full))
    value_rows = lowered(plain_product(normed, wv_full))
    attended_t, prob = attend(
        bias_flat.astype(F32), key_rows, queries.T, value_rows.T, feature_k, feature_q, near
    )
    attended = attended_t.T
    residual = embedded + plain_product(attended, wo_full)
    normed_two = lowered(normalize(residual, gain_two))
    inner_act = plain_product(normed_two, inner_full)
    hidden = lowered(jax.nn.gelu(inner_act, approximate=True))
    layer_out = residual + plain_product(hidden, outer_full)

    grad_out = cotangent.astype(F32)
    grad_w_outer = lowered(gram_product(hidden, cotangent))
    grad_hidden = back_product(cotangent, outer_full)
    gelu_pull = jax.vjp(lambda pre_act: jax.nn.gelu(pre_act, approximate=True), inner_act)[1]
    grad_inner = lowered(gelu_pull(grad_hidden)[0])
    grad_w_inner = lowered(gram_product(normed_two, grad_inner))
    grad_normed_two = back_product(grad_inner, inner_full)
    norm_two_pull = jax.vjp(normalize, residual, gain_two)[1]
    grad_resid_norm, grad_gain_two = norm_two_pull(grad_normed_two)
    grad_residual = grad_out + grad_resid_norm
    grad_branch = lowered(grad_residual)
    grad_w_output = lowered(gram_product(attended, grad_branch))
    grad_attended = lowered(back_product(grad_branch, wo_full))
    grad_values, grad_keys, grad_queries_t, bias_sums = attend_back(
        prob, value_rows, grad_attended.T, attended_t, grad_attended, queries, key_rows.T
    )
    grad_queries = grad_queries_t.T
    near_sums = lax.dot_general(
        bias_sums[:, :3].reshape(HEADS, 6 * TILE),
        near_hot.astype(F32),
        (((1,), (1,)), ((), ())),
        precision=lax.Precision.HIGHEST,
        preferred_element_type=F32,
    )
    far_behind = jnp.sum(bias_sums[:, 3], axis=1)
    far_ahead = jnp.sum(bias_sums[:, 4], axis=1)
    grad_bias = near_sums.T.at[15].add(far_behind).at[31].add(far_ahead)
    grad_w_query = lowered(gram_product(normed, grad_queries))
    grad_w_key = lowered(gram_product(normed, grad_keys))
    grad_w_value = lowered(gram_product(normed, grad_values))
    grad_normed = (
        back_product(grad_queries, wq_full)
        + back_product(grad_keys, wk_full)
        + back_product(grad_values, wv_full)
    )
    norm_one_pull = jax.vjp(normalize, embedded, gain_one)[1]
    grad_embed_norm, grad_gain_one = norm_one_pull(grad_normed)
    input_grad = grad_residual + grad_embed_norm

    chip_rows = 2 * shard
    small_grads = jnp.zeros((dp_count, 8, TILE), F32)
    small_grads = small_grads.at[:, 0, :chip_rows].set(grad_gain_one.reshape(dp_count, chip_rows))
    small_grads = small_grads.at[:, 1, :chip_rows].set(grad_gain_two.reshape(dp_count, chip_rows))
    small_grads = small_grads.at[:, 2, : 2 * bias_shard].set(
        grad_bias.reshape(dp_count, 2 * bias_shard)
    )
    leaving = lowered(plain_product(spread_t, lowered(input_grad))).reshape(dp_count, cap, D)
    square = (*dims, chip_rows, D)
    sum_query, sum_key, sum_value, sum_output, sum_inner, sum_outer, sum_small, incoming = reduce_grads(
        dims,
        [g.reshape(square) for g in (grad_w_query, grad_w_key, grad_w_value, grad_w_output)],
        grad_w_inner.reshape(*dims, chip_rows, -1),
        grad_w_outer.reshape(*dims, 2, -1, D),
        small_grads,
        leaving,
    )
    ids = asked[:, :, 0, :cap].reshape(1, 2 * dp_count * cap)
    table_grad = collect(ids, incoming.reshape(2 * dp_count * cap, D), owner_rows)
    gain_one_sum = lax.dynamic_slice(sum_small[0], (core * shard,), (shard,))
    gain_two_sum = lax.dynamic_slice(sum_small[1], (core * shard,), (shard,))
    bias_sum = lax.dynamic_slice(sum_small[2], (core * bias_shard,), (bias_shard,))
    return (
        lowered(layer_out),
        input_grad,
        table_grad,
        gain_one_sum,
        sum_query,
        sum_key,
        sum_value,
        sum_output,
        bias_sum,
        gain_two_sum,
        sum_inner,
        sum_outer,
    )


def solution(mesh):
    both = ("dp", "fsdp")
    flat, tall = P(both), P(both, None)
    return jax.shard_map(
        partial(body, chip_grid(mesh.shape["dp"])),
        mesh=mesh,
        in_specs=(
            P("dp", None), flat, tall, tall, flat, flat, flat, tall, tall, tall, tall, flat, flat,
            tall, tall, tall,
        ),
        out_specs=(
            tall, tall, P("dp", None), flat, tall, tall, tall, tall, flat, flat, tall, tall,
        ),
        check_vma=False,
    )
```

time: 3230 us -> 442 us (0.14); the launches traced: 3200 us -> 441 us
  starting transfers between devices: 1840 us -> 0 us
  waiting for transfers between devices: 808 us -> 0 us
  Pallas kernels: 0 us -> 341 us
  local copies, waits for them, and re-layouts: 225 us -> 38.6 us
  blocking collectives: 118 us -> 0 us
  matrix products: 114 us -> 49 us
  loops' own time: 41.3 us -> 0 us
    all_to_all x2 -> x0, starting transfers between devices: 1830 us -> none  [the longest x1 1830 us: body(): lax.all_to_all(outgoing.astype(jnp.bfloat16), 'dp', split_axis=0, concat_...]
    reduce_scatter x6 -> x0, waiting for transfers between devices: 633 us -> none  [the longest x1 142 us: body(): lax.psum_scatter(grad_w_outer, ('dp', 'fsdp'), scatter_dimension=0, tiled...]
    pallas_call x0 -> x5, Pallas kernels: none -> 341 us  [the longest x1 156 us: reduce_grads(): pl.pallas_call(partial(reduce_kernel, dims), out_shape=[jax.ShapeDtypeStr...]
    all_gather x6 -> x0, waiting for transfers between devices: 139 us -> none  [the longest x1 59.9 us: body(): lax.all_gather(w_outer, ('dp', 'fsdp'), axis=0, tiled=True)]
    scatter x3 -> x6, local copies, waits for them, and re-layouts: 126 us -> 2.97 us  [the longest x2 1.43 us: body(): small = small.at[0, :shard].set(norm1_gain).at[1, :shard].set(norm2_gain)]
    unnamed x2 -> x0, blocking collectives: 102 us -> none
    gather x7 -> x0, local copies, waits for them, and re-layouts: 42.2 us -> none  [the longest x4 33.7 us: attention_scores(): position_term = jnp.transpose(bias_table[span_buckets(doc_span)], (2, 0, 1))]
    dot_general x14 -> x9, matrix products: 60.8 us -> 19.4 us  [the longest x8 19.3 us: plain_product(): return jnp.dot(left_side, right_side, preferred_element_type=F32)]
  transfers between devices with their start and end apart: 15 -> 0, of which waited for: 10 -> 0; matrix products, arithmetic and copies ran while one was open for 6% -> 0% of each run, Pallas kernels for 0% -> 0%
where the time goes in v1:
time: 442 us; the launch traced here: 441 us
  Pallas kernels  341 us (77%)
  matrix products  49 us (11%)
  local copies, waits for them, and re-layouts  38.6 us (9%)
  other arithmetic  10.8 us (2%)
    pallas_call x1, Pallas kernels, reduce_grads(): pl.pallas_call(partial(reduce_kernel, dims), out_shape=[jax.ShapeDtypeStr...  156 us
    pallas_call x1, Pallas kernels, fetch(): pl.pallas_call(partial(fetch_kernel, dims, cap), out_shape=[jax.ShapeDtyp...  154 us
    unnamed x101, local copies, waits for them, and re-layouts  29.1 us
    dot_general x8, matrix products, plain_product(): return jnp.dot(left_side, right_side, preferred_element_type=F32)  19.3 us
    dot_general x6, matrix products, back_product(): lax.dot_general(left_side, right_side, (((1,), (1,)), ((), ())), preferre...  15.3 us
    dot_general x7, matrix products, gram_product(): lax.dot_general(left_side, right_side, (((0,), (0,)), ((), ())), preferre...  14.3 us
    pallas_call x1, Pallas kernels, attend(): pl.pallas_call(attend_kernel, grid=(HEADS // 2,), in_specs=[SMEM, wide, t...  13.4 us

profile of v1, /device:TPU:0, one launch (start us, length us, event | category | flops | bytes accessed | tf_op | source)
XLA Modules:
  0.0 441.3 jit_solution(12521692832850646320)
XLA Ops:
  7.7 1.6 select_reduce_fusion
  10.5 1.9 copy-done.11
  17.3 154.3 %fetch.1 = (bf16[16,64,768]{2,1,0:T(8,128)(2,1)S(1)}, s32[2,16,8,128]{3,2,1,0:T(8,128)S(1)}, bf16[4,2,2,48,768]{4,3,2,1,0:T(8,128)(2,1)S(1)}, bf16[4,2,2,48,768]...) custom-call(s32[16,8,128]{2,1,0:T(8,128)S(1)} %broadcast_in_dim.78.a, ...), custom_call_target="tpu_custom_call" | custom-call | tf_op jit(solution)/shard_map/fetch/pallas_call | solution.py:384
  171.6 2.7 multiply_reduce_fusion.5
  175.1 1.6 multiply_convert_fusion.2
  182.2 13.4 %attend.1 = (bf16[768,512]{1,0:T(8,128)(2,1)S(1)}, bf16[12,512,512]{2,1,0:T(8,128)(2,1)S(1)}) custom-call(f32[384]{0:T(512)S(1)} %reshape.593.far, bf16[512,768]{1,0:T(8,128)(2,1)S(1)} %copy.58.key, bf16[768,512]{1,0:T(8,128)(2,1)S(1)} %copy.59.query_t, bf16[768,512]{1,0:T(8,128)(2,1)S(1)} %copy.60.value_t, bf16[512,128]{1,0:T(8,128)(2,1)S(1)} %pad.32.feature_k, ...), custom_call_target="tpu_custom_call" | custom-call | tf_op jit(solution)/shard_map/attend/pallas_call | solution.py:778
  195.6 2.7 copy-done
  198.3 2.5 multiply_reduce_fusion.4
  200.8 4.6 %fusion.50 = f32[512,3072]{1,0:T(8,128)S(1)} fusion(bf16[768,3072]{1,0:T(8,128)(2,1)} %bitcast.119, f32[512,768]{1,0:T(8,128)S(1)} %get-tuple-element.173, f32[768]{0:T(1024)S(1)} %reshape.595, f32[512]{0:T(512)S(1)} %fusion.46), kind=kOutput, calls=%fused_computation.127 | convolution fusion | flops 2417098752 | bytes 12588032 | tf_op jit(solution)/shard_map/dot_general | solution.py:50
  205.5 4.9 %add_convert_fusion = bf16[512,768]{1,0:T(8,128)(2,1)} fusion(f32[512,768]{1,0:T(8,128)S(1)} %get-tuple-element.173, bf16[3072,768]{1,0:T(8,128)(2,1)S(1)} %bitcast.138, f32[512,3072]{1,0:T(8,128)S(1)} %fusion.50), kind=kOutput, calls=%fused_computation.33 | convolution fusion | flops 2430861312 | bytes 13369344 | tf_op jit(solution)/shard_map/dot_general | solution.py:50
  210.4 6.1 %fusion.6 = bf16[512,3072]{1,0:T(8,128)(2,1)S(1)} fusion(f32[512,3072]{1,0:T(8,128)S(1)} %fusion.50, bf16[3072,768]{1,0:T(8,128)(2,1)S(1)} %bitcast.139, bf16[512,768]{1,0:T(8,128)(2,1)S(1)} %copy-done.41), kind=kOutput, calls=%fused_computation.8 | convolution fusion | flops 2447376384 | bytes 14942208 | tf_op jit(solution)/shard_map/dot_general | solution.py:60
  216.6 2.9 multiply_reduce_fusion
  219.4 5.0 %convolution_convert_fusion = bf16[3072,768]{1,0:T(8,128)(2,1)} fusion(bf16[512,768]{1,0:T(8,128)(2,1)S(1)} %copy-done.41, f32[512,3072]{1,0:T(8,128)S(1)} %fusion.50), kind=kOutput, calls=%fused_computation.15 | convolution fusion | flops 2432434176 | bytes 11796480 | tf_op jit(solution)/shard_map/dot_general | solution.py:54
  226.0 1.8 convolution_convert_fusion.6.grad
  227.8 4.5 %convolution_convert_fusion.1 = bf16[768,3072]{1,0:T(8,128)(2,1)} fusion(bf16[512,3072]{1,0:T(8,128)(2,1)S(1)} %fusion.6, f32[512,768]{1,0:T(8,128)S(1)} %get-tuple-element.173, f32[768]{0:T(1024)S(1)} %reshape.595, f32[512]{0:T(512)S(1)} %fusion.46), kind=kOutput, calls=%fused_computation.16 | convolution fusion | flops 2419458048 | bytes 9442304 | tf_op jit(solution)/shard_map/dot_general | solution.py:54
  232.4 2.4 copy.64.grad_t
  234.8 2.8 copy-done.1
  239.9 8.1 %attend_back.1 = (bf16[512,768]{1,0:T(8,128)(2,1)S(1)}, bf16[512,768]{1,0:T(8,128)(2,1)S(1)}, bf16[768,512]{1,0:T(8,128)(2,1)S(1)}, f32[12,8,256]{2,1,0:T(8,128)S(1)}) custom-call(bf16[12,512,512]{2,1,0:T(8,128)(2,1)S(1)} %copy-done.1, bf16[512,768]{1,0:T(8,128)(2,1)S(1)} %copy-done.4, bf16[768,512]{1,0:T(8,128)(2,1)S(1)} %copy-done.10, ...), custom_call_target="tpu_custom_call" | custom-call | tf_op jit(solution)/shard_map/attend_back/pallas_call | solution.py:853
  252.0 2.5 fusion.53
  262.6 2.3 convolution_convert_fusion.3
  266.3 2.2 fusion.12
  268.5 156.4 %reduce.23 = (f32[24,768]{1,0:T(8,128)S(1)}, f32[24,768]{1,0:T(8,128)S(1)}, f32[24,768]{1,0:T(8,128)S(1)}, f32[24,768]{1,0:T(8,128)S(1)}, f32[24,3072]{1,0:T(8,1...) custom-call(bf16[4,2,2,48,768]{4,3,2,1,0:T(8,128)(2,1)S(1)} %bitcast.107, ...), custom_call_target="tpu_custom_call" | custom-call | tf_op jit(solution)/shard_map/reduce/pallas_call | solution.py:694
  426.7 1.9 copy-done.2
  428.6 8.7 %collect.1 = f32[2008,768]{1,0:T(8,128)} custom-call(s32[1,2048]{1,0:T(1,128)S(1)} %reshape_squeeze.2.ids, bf16[2048,768]{1,0:T(8,128)(2,1)S(1)} %bitcast.98), custom_call_target="tpu_custom_call" | custom-call | tf_op jit(solution)/shard_map/collect/pallas_call | solution.py:887
  (175 shorter events, 41.7 us)
Async XLA Ops:
  10.5 1.9 copy-start.11
  171.6 2.7 copy-start.14
  171.6 2.7 copy-start.24
  171.6 2.7 copy-start.27
  171.6 5.1 %copy-start.12 = (bf16[4,2,2,48,768]{4,3,2,1,0:T(8,128)(2,1)}, bf16[4,2,2,48,768]{4,3,2,1,0:T(8,128)(2,1)S(1)}, u32[]{:S(2)}) copy-start(bf16[4,2,2,48,768]{4,3,2,1,0:T(8,128)(2,1)S(1)} %get-tuple-element.135) | copy-start | bytes 3538948
  176.8 2.4 copy-start.38
  177.6 4.3 copy-start.3
  182.2 16.1 %copy-start.15 = (bf16[4,2,2,48,768]{4,3,2,1,0:T(8,128)(2,1)S(1)}, bf16[4,2,2,48,768]{4,3,2,1,0:T(8,128)(2,1)}, u32[]{:S(2)}) copy-start(bf16[4,2,2,48,768]{4,3,2,1,0:T(8,128)(2,1)} %copy-done.14) | copy-start | bytes 3538948
  195.6 2.7 copy-start
  198.3 7.1 %slice-start.2 = ((s8[4718592]{0:T(1024)(128)(4,1)}), s8[4194304]{0:T(1024)(128)(4,1)S(1)}, s32[]{:S(2)}) async-start(s8[4718592]{0:T(1024)(128)(4,1)} %bitcast.136), calls=%async_computation.2 | async-start | bytes 8388608
  200.8 4.7 %slice-start.3 = ((s8[4718592]{0:T(1024)(128)(4,1)}), s8[524288]{0:T(1024)(128)(4,1)S(1)}, s32[]{:S(2)}) async-start(s8[4718592]{0:T(1024)(128)(4,1)} %bitcast.136), calls=%async_computation.3 | async-start | bytes 1048576
  205.5 4.9 %copy-start.41 = (bf16[512,768]{1,0:T(8,128)(2,1)S(1)}, bf16[512,768]{1,0:T(8,128)(2,1)}, u32[]{:S(2)}) copy-start(bf16[512,768]{1,0:T(8,128)(2,1)} %param.47) | copy-start | bytes 2359300
  205.5 11.0 %slice-start = ((s8[4718592]{0:T(1024)(128)(4,1)}), s8[4194304]{0:T(1024)(128)(4,1)S(1)}, s32[]{:S(2)}) async-start(s8[4718592]{0:T(1024)(128)(4,1)} %bitcast.120), calls=%async_computation | async-start | bytes 8388608
  210.4 6.1 %slice-start.1 = ((s8[4718592]{0:T(1024)(128)(4,1)}), s8[524288]{0:T(1024)(128)(4,1)S(1)}, s32[]{:S(2)}) async-start(s8[4718592]{0:T(1024)(128)(4,1)} %bitcast.120), calls=%async_computation.1 | async-start | bytes 1048576
  227.8 7.0 %copy-start.8 = (bf16[512,768]{0,1:T(8,128)(2,1)S(1)}, bf16[512,768]{0,1:T(8,128)(2,1)}, u32[]{:S(2)}) copy-start(bf16[512,768]{0,1:T(8,128)(2,1)} %copy-done.7) | copy-start | bytes 2359300
  232.3 2.5 copy-start.4
  232.3 2.5 copy-start.6
  234.8 2.8 copy-start.1
  252.0 2.5 copy-start.33
  252.0 2.5 copy-start.39
  256.0 2.0 copy-start.34
  262.6 2.3 copy-start.31
  262.6 2.3 copy-start.40
  426.7 1.9 copy-start.2
  (22 other events, 24.7 us)

commit v2 on v1

--- a/solution.py
+++ b/solution.py
@@ -275,6 +275,8 @@
 
     for number, ref in enumerate(squares):
         block_square[number] = joined(ref[...], near_square[number])
+    for piece in range(4, 8):
+        begin(piece)
     block_inner[...] = joined(w_inner[...], near_inner[...])
 
     def wait_ask(step, carry):
@@ -328,24 +330,25 @@
     asks_across = remote(got, asked_out.at[core], pair_send.at[5], pair_recv.at[5], place.sibling())
     asks_across.start()
 
-    for piece in range(2, 8):
-        begin(piece)
-
     total = len(pieces)
-    for turn in range(total + 3):
+    pairs = ((0, 1), (4, 5), (6, 7, 8), (2, 3))
+    for turn in range(len(pairs) + 2):
         for phase in (3, 2, 1):
-            piece = turn + 1 - phase
-            if not 0 <= piece < total:
+            if not 0 <= turn + 1 - phase < len(pairs):
                 continue
-            for copy in axis_copies(piece, phase - 1):
-                copy.wait_recv()
-            if phase == 1:
-                keep_copy(piece).wait()
-            if phase < 3:
-                for copy in axis_copies(piece, phase):
-                    copy.start()
-            else:
-                core_copy(piece).start()
+            for piece in pairs[turn + 1 - phase]:
+                for copy in axis_copies(piece, phase - 1):
+                    copy.wait_recv()
+                if phase == 1:
+                    keep_copy(piece).wait()
+                if phase < 3:
+                    for copy in axis_copies(piece, phase):
+                        copy.start()
+                else:
+                    core_copy(piece).start()
+        if turn == 0:
+            for piece in (2, 3):
+                begin(piece)
 
     def wait_row(block, carry):
         @pl.when(block != me)
@@ -594,25 +597,26 @@
         load_copy(piece).start()
         pair_copy(piece).start()
 
-    for turn in range(total + 3):
+    pairs = ((0, 1), (2, 3), (4, 5), (6, 7))
+    for turn in range(len(pairs) + 3):
         for phase in (3, 2, 1, 0):
-            piece = turn - phase
-            if not 0 <= piece < total:
+            if not 0 <= turn - phase < len(pairs):
                 continue
-            if phase == 0:
-                load_copy(piece).wait()
-                pair_copy(piece).wait_recv()
-                add_across(piece)
-            else:
-                for copy in axis_copies(piece, phase - 1):
-                    copy.wait_recv()
+            for piece in pairs[turn - phase]:
+                if phase == 0:
+                    load_copy(piece).wait()
+                    pair_copy(piece).wait_recv()
+                    add_across(piece)
+                else:
+                    for copy in axis_copies(piece, phase - 1):
+                        copy.wait_recv()
+                    if phase < 3:
+                        add_arrived(piece, phase - 1)
                 if phase < 3:
-                    add_arrived(piece, phase - 1)
-            if phase < 3:
-                for copy in axis_copies(piece, phase):
-                    copy.start()
-            else:
-                finish(piece)
+                    for copy in axis_copies(piece, phase):
+                        copy.start()
+                else:
+                    finish(piece)
 
     def pass_over(step, carry):
         row_copy(step).wait()

time: 442 us -> 347 us (0.79)
  Pallas kernels: 341 us -> 243 us
    pallas_call x1, Pallas kernels: 156 us -> 106 us  [reduce_grads(): pl.pallas_call(partial(reduce_kernel, dims), out_shape=[jax.ShapeDtypeStr...]
    pallas_call x1, Pallas kernels: 154 us -> 108 us  [fetch(): pl.pallas_call(partial(fetch_kernel, dims, cap), out_shape=[jax.ShapeDtyp...]
where the time goes in v2:
time: 347 us; the launch traced here: 344 us
  Pallas kernels  243 us (70%)
  matrix products  49 us (14%)
  local copies, waits for them, and re-layouts  38.6 us (11%)
  other arithmetic  10.8 us (3%)
    pallas_call x1, Pallas kernels, fetch(): pl.pallas_call(partial(fetch_kernel, dims, cap), out_shape=[jax.ShapeDtyp...  108 us
    pallas_call x1, Pallas kernels, reduce_grads(): pl.pallas_call(partial(reduce_kernel, dims), out_shape=[jax.ShapeDtypeStr...  106 us
    unnamed x101, local copies, waits for them, and re-layouts  29.1 us
    dot_general x8, matrix products, plain_product(): return jnp.dot(left_side, right_side, preferred_element_type=F32)  19.3 us
    dot_general x6, matrix products, back_product(): lax.dot_general(left_side, right_side, (((1,), (1,)), ((), ())), preferre...  15.3 us
    dot_general x7, matrix products, gram_product(): lax.dot_general(left_side, right_side, (((0,), (0,)), ((), ())), preferre...  14.3 us
    pallas_call x1, Pallas kernels, attend(): pl.pallas_call(attend_kernel, grid=(HEADS // 2,), in_specs=[SMEM, wide, t...  13.4 us
    pallas_call x1, Pallas kernels, collect(): pl.pallas_call(collect_kernel, grid=(-(-owner_rows // high),), in_specs=[...  8.75 us

profile of v2, /device:TPU:0, one launch (start us, length us, event | category | flops | bytes accessed | tf_op | source)
XLA Modules:
  0.0 343.8 jit_solution(15841469197952226855)
XLA Ops:
  7.7 1.6 select_reduce_fusion
  10.5 1.9 copy-done.11
  17.3 107.5 %fetch.1 = (bf16[16,64,768]{2,1,0:T(8,128)(2,1)S(1)}, s32[2,16,8,128]{3,2,1,0:T(8,128)S(1)}, bf16[4,2,2,48,768]{4,3,2,1,0:T(8,128)(2,1)S(1)}, bf16[4,2,2,48,768]...) custom-call(s32[16,8,128]{2,1,0:T(8,128)S(1)} %broadcast_in_dim.78.a, ...), custom_call_target="tpu_custom_call" | custom-call | tf_op jit(solution)/shard_map/fetch/pallas_call | solution.py:387
  124.8 2.7 multiply_reduce_fusion.5
  128.4 1.6 multiply_convert_fusion.2
  135.4 13.4 %attend.1 = (bf16[768,512]{1,0:T(8,128)(2,1)S(1)}, bf16[12,512,512]{2,1,0:T(8,128)(2,1)S(1)}) custom-call(f32[384]{0:T(512)S(1)} %reshape.593.far, bf16[512,768]{1,0:T(8,128)(2,1)S(1)} %copy.58.key, bf16[768,512]{1,0:T(8,128)(2,1)S(1)} %copy.59.query_t, bf16[768,512]{1,0:T(8,128)(2,1)S(1)} %copy.60.value_t, bf16[512,128]{1,0:T(8,128)(2,1)S(1)} %pad.32.feature_k, ...), custom_call_target="tpu_custom_call" | custom-call | tf_op jit(solution)/shard_map/attend/pallas_call | solution.py:782
  148.9 2.7 copy-done
  151.5 2.5 multiply_reduce_fusion.4
  154.0 4.6 %fusion.50 = f32[512,3072]{1,0:T(8,128)S(1)} fusion(bf16[768,3072]{1,0:T(8,128)(2,1)} %bitcast.119, f32[512,768]{1,0:T(8,128)S(1)} %get-tuple-element.173, f32[768]{0:T(1024)S(1)} %reshape.595, f32[512]{0:T(512)S(1)} %fusion.46), kind=kOutput, calls=%fused_computation.127 | convolution fusion | flops 2417098752 | bytes 12588032 | tf_op jit(solution)/shard_map/dot_general | solution.py:50
  158.7 4.9 %add_convert_fusion = bf16[512,768]{1,0:T(8,128)(2,1)} fusion(f32[512,768]{1,0:T(8,128)S(1)} %get-tuple-element.173, bf16[3072,768]{1,0:T(8,128)(2,1)S(1)} %bitcast.138, f32[512,3072]{1,0:T(8,128)S(1)} %fusion.50), kind=kOutput, calls=%fused_computation.33 | convolution fusion | flops 2430861312 | bytes 13369344 | tf_op jit(solution)/shard_map/dot_general | solution.py:50
  163.6 6.1 %fusion.6 = bf16[512,3072]{1,0:T(8,128)(2,1)S(1)} fusion(f32[512,3072]{1,0:T(8,128)S(1)} %fusion.50, bf16[3072,768]{1,0:T(8,128)(2,1)S(1)} %bitcast.139, bf16[512,768]{1,0:T(8,128)(2,1)S(1)} %copy-done.41), kind=kOutput, calls=%fused_computation.8 | convolution fusion | flops 2447376384 | bytes 14942208 | tf_op jit(solution)/shard_map/dot_general | solution.py:60
  169.8 2.9 multiply_reduce_fusion
  172.6 5.0 %convolution_convert_fusion = bf16[3072,768]{1,0:T(8,128)(2,1)} fusion(bf16[512,768]{1,0:T(8,128)(2,1)S(1)} %copy-done.41, f32[512,3072]{1,0:T(8,128)S(1)} %fusion.50), kind=kOutput, calls=%fused_computation.15 | convolution fusion | flops 2432434176 | bytes 11796480 | tf_op jit(solution)/shard_map/dot_general | solution.py:54
  179.3 1.8 convolution_convert_fusion.6.grad
  181.0 4.5 %convolution_convert_fusion.1 = bf16[768,3072]{1,0:T(8,128)(2,1)} fusion(bf16[512,3072]{1,0:T(8,128)(2,1)S(1)} %fusion.6, f32[512,768]{1,0:T(8,128)S(1)} %get-tuple-element.173, f32[768]{0:T(1024)S(1)} %reshape.595, f32[512]{0:T(512)S(1)} %fusion.46), kind=kOutput, calls=%fused_computation.16 | convolution fusion | flops 2419458048 | bytes 9442304 | tf_op jit(solution)/shard_map/dot_general | solution.py:54
  185.6 2.4 copy.64.grad_t
  188.0 2.8 copy-done.1
  193.1 8.1 %attend_back.1 = (bf16[512,768]{1,0:T(8,128)(2,1)S(1)}, bf16[512,768]{1,0:T(8,128)(2,1)S(1)}, bf16[768,512]{1,0:T(8,128)(2,1)S(1)}, f32[12,8,256]{2,1,0:T(8,128)S(1)}) custom-call(bf16[12,512,512]{2,1,0:T(8,128)(2,1)S(1)} %copy-done.1, bf16[512,768]{1,0:T(8,128)(2,1)S(1)} %copy-done.4, bf16[768,512]{1,0:T(8,128)(2,1)S(1)} %copy-done.10, ...), custom_call_target="tpu_custom_call" | custom-call | tf_op jit(solution)/shard_map/attend_back/pallas_call | solution.py:857
  205.2 2.5 fusion.53
  215.8 2.3 convolution_convert_fusion.3
  219.5 2.2 fusion.12
  221.8 105.7 %reduce.23 = (f32[24,768]{1,0:T(8,128)S(1)}, f32[24,768]{1,0:T(8,128)S(1)}, f32[24,768]{1,0:T(8,128)S(1)}, f32[24,768]{1,0:T(8,128)S(1)}, f32[24,3072]{1,0:T(8,1...) custom-call(bf16[4,2,2,48,768]{4,3,2,1,0:T(8,128)(2,1)S(1)} %bitcast.107, ...), custom_call_target="tpu_custom_call" | custom-call | tf_op jit(solution)/shard_map/reduce/pallas_call | solution.py:698
  329.2 1.9 copy-done.2
  331.1 8.8 %collect.1 = f32[2008,768]{1,0:T(8,128)} custom-call(s32[1,2048]{1,0:T(1,128)S(1)} %reshape_squeeze.2.ids, bf16[2048,768]{1,0:T(8,128)(2,1)S(1)} %bitcast.98), custom_call_target="tpu_custom_call" | custom-call | tf_op jit(solution)/shard_map/collect/pallas_call | solution.py:891
  (175 shorter events, 41.7 us)
Async XLA Ops:
  10.5 1.9 copy-start.11
  124.8 2.7 copy-start.14
  124.8 2.7 copy-start.24
  124.8 2.7 copy-start.27
  124.8 5.1 %copy-start.12 = (bf16[4,2,2,48,768]{4,3,2,1,0:T(8,128)(2,1)}, bf16[4,2,2,48,768]{4,3,2,1,0:T(8,128)(2,1)S(1)}, u32[]{:S(2)}) copy-start(bf16[4,2,2,48,768]{4,3,2,1,0:T(8,128)(2,1)S(1)} %get-tuple-element.135) | copy-start | bytes 3538948
  130.0 2.4 copy-start.38
  130.8 4.3 %copy-start.3 = (bf16[512,768]{1,0:T(8,128)(2,1)}, bf16[512,768]{1,0:T(8,128)(2,1)S(1)}, u32[]{:S(2)}) copy-start(bf16[512,768]{1,0:T(8,128)(2,1)S(1)} %convolution_convert_fusion.7.value) | copy-start | bytes 2359300
  135.4 16.1 %copy-start.15 = (bf16[4,2,2,48,768]{4,3,2,1,0:T(8,128)(2,1)S(1)}, bf16[4,2,2,48,768]{4,3,2,1,0:T(8,128)(2,1)}, u32[]{:S(2)}) copy-start(bf16[4,2,2,48,768]{4,3,2,1,0:T(8,128)(2,1)} %copy-done.14) | copy-start | bytes 3538948
  148.9 2.7 copy-start
  151.5 7.1 %slice-start.2 = ((s8[4718592]{0:T(1024)(128)(4,1)}), s8[4194304]{0:T(1024)(128)(4,1)S(1)}, s32[]{:S(2)}) async-start(s8[4718592]{0:T(1024)(128)(4,1)} %bitcast.136), calls=%async_computation.2 | async-start | bytes 8388608
  154.0 4.7 %slice-start.3 = ((s8[4718592]{0:T(1024)(128)(4,1)}), s8[524288]{0:T(1024)(128)(4,1)S(1)}, s32[]{:S(2)}) async-start(s8[4718592]{0:T(1024)(128)(4,1)} %bitcast.136), calls=%async_computation.3 | async-start | bytes 1048576
  158.7 4.9 %copy-start.41 = (bf16[512,768]{1,0:T(8,128)(2,1)S(1)}, bf16[512,768]{1,0:T(8,128)(2,1)}, u32[]{:S(2)}) copy-start(bf16[512,768]{1,0:T(8,128)(2,1)} %param.47) | copy-start | bytes 2359300
  158.7 11.0 %slice-start = ((s8[4718592]{0:T(1024)(128)(4,1)}), s8[4194304]{0:T(1024)(128)(4,1)S(1)}, s32[]{:S(2)}) async-start(s8[4718592]{0:T(1024)(128)(4,1)} %bitcast.120), calls=%async_computation | async-start | bytes 8388608
  163.6 6.1 %slice-start.1 = ((s8[4718592]{0:T(1024)(128)(4,1)}), s8[524288]{0:T(1024)(128)(4,1)S(1)}, s32[]{:S(2)}) async-start(s8[4718592]{0:T(1024)(128)(4,1)} %bitcast.120), calls=%async_computation.1 | async-start | bytes 1048576
  181.0 7.0 %copy-start.8 = (bf16[512,768]{0,1:T(8,128)(2,1)S(1)}, bf16[512,768]{0,1:T(8,128)(2,1)}, u32[]{:S(2)}) copy-start(bf16[512,768]{0,1:T(8,128)(2,1)} %copy-done.7) | copy-start | bytes 2359300
  185.5 2.5 copy-start.4
  185.5 2.5 copy-start.6
  188.0 2.8 copy-start.1
  205.2 2.5 copy-start.33
  205.2 2.5 copy-start.39
  209.2 2.0 copy-start.34
  215.8 2.3 copy-start.31
  215.8 2.3 copy-start.40
  329.2 1.9 copy-start.2
  (22 other events, 24.7 us)

commit v3 on v2

--- a/solution.py
+++ b/solution.py
@@ -1,4 +1,6 @@
 from functools import partial
+from types import SimpleNamespace
+from typing import Any, NamedTuple
 
 import jax
 import jax.numpy as jnp
@@ -18,6 +20,8 @@
 
 EPSILON = 1e-06
 THRESHOLDS = (12, 16, 23, 32, 46, 64, 91)
+GELU_A = 0.7978845608028654
+GELU_B = 0.044715
 MESH = pl.DeviceIdType.MESH
 F32 = jnp.float32
 BF16 = jnp.bfloat16
@@ -104,16 +108,24 @@
     )
 
 
-def enter(place):
+def greet(place):
     barrier = pltpu.get_barrier_semaphore()
 
-    def greet(step, carry):
+    def one(step, carry):
         pl.semaphore_signal(barrier, inc=1, device_id=place.other(step)[1], device_id_type=MESH)
         return carry
 
-    lax.fori_loop(1, place.count, greet, 0)
+    lax.fori_loop(1, place.count, one, 0)
     pl.semaphore_signal(barrier, inc=1, device_id=place.sibling(), device_id_type=MESH)
-    pl.semaphore_wait(barrier, place.count)
+
+
+def meet(place):
+    pl.semaphore_wait(pltpu.get_barrier_semaphore(), place.count)
+
+
+def enter(place):
+    greet(place)
+    meet(place)
 
 
 def pieces_of(square, inner, outer):
@@ -878,28 +890,1781 @@
     )(prob, value, grad_t, attended_t, grad, query, key_t)
 
 
-def collect_kernel(ids, incoming, out):
+def collect_kernel(cap, sizes, asked, small, incoming, *refs):
+    ready, (out, gain_one, gain_two, bias), refs = refs[:8], refs[8:12], refs[12:]
+    placed, held, (ids, rows, load_sem, pass_sem) = refs[:8], refs[8:16], refs[16:]
+    step = pl.program_id(0)
+    core = lax.axis_index("fsdp")
+    count = asked.shape[1]
+    load = pltpu.make_async_copy(incoming, rows, load_sem)
+    takes = [
+        pltpu.make_async_copy(source, target, pass_sem.at[number])
+        for number, (source, target) in enumerate(zip(ready, held))
+    ]
+    passes = [
+        pltpu.make_async_copy(source, target, pass_sem.at[number])
+        for number, (source, target) in enumerate(zip(held, placed))
+    ]
+
+    @pl.when(step == 0)
+    def _():
+        load.start()
+        for copy in takes:
+            copy.start()
+        together = TILE // cap
+        lane = lax.broadcasted_iota(jnp.int32, (1, TILE), 1)
+        for side in range(2):
+            for group in range(count // together):
+                line = asked[side, group * together, 0:1, :]
+                for inside in range(1, together):
+                    moved = pltpu.roll(asked[side, group * together + inside, 0:1, :], inside * cap, 1)
+                    line = jnp.where(lane < inside * cap, line, moved)
+                first = (side * count + group * together) * cap
+                ids[:, first : first + TILE] = line
+        for row, (target, size) in enumerate(zip((gain_one, gain_two, bias), sizes)):
+            line = small[row : row + 1, :]
+            moved = pltpu.roll(line, TILE - size, 1)
+            target[...] = jnp.where(core == 0, line, moved)[:, :size]
+        load.wait()
+
+    @pl.when(step == 1)
+    def _():
+        for copy in takes:
+            copy.wait()
+        for copy in passes:
+            copy.start()
+
     high = out.shape[0]
-    first = pl.program_id(0) * high
-    rows = lax.broadcasted_iota(jnp.int32, (high, ids.shape[1]), 0) + first
-    picked = (rows == ids[...]).astype(F32).astype(BF16)
-    out[...] = plain_product(picked, incoming[...])
-
-
-def collect(ids, incoming, owner_rows):
+    spots = lax.broadcasted_iota(jnp.int32, (high, ids.shape[1]), 0) + step * high
+    picked = lowered((spots == ids[...]).astype(F32))
+    out[...] = plain_product(picked, rows[...].reshape(ids.shape[1], D))
+
+    @pl.when(step == pl.num_programs(0) - 1)
+    def _():
+        for copy in passes:
+            copy.wait()
+
+
+def collect(asked, small, incoming, ready, owner_rows, sizes):
     high = 256
+    cap = incoming.shape[2]
+    slots = incoming.shape[0] * incoming.shape[1] * cap
+    lines = [jax.ShapeDtypeStruct((1, size), F32) for size in sizes]
     return pl.pallas_call(
-        collect_kernel,
+        partial(collect_kernel, cap, sizes),
         grid=(-(-owner_rows // high),),
-        in_specs=[
-            pl.BlockSpec(ids.shape, lambda step: (0, 0)),
-            pl.BlockSpec(incoming.shape, lambda step: (0, 0)),
+        in_specs=[VMEM, VMEM] + [ANY] * 9,
+        out_specs=[pl.BlockSpec((high, D), lambda step: (step, 0))] + [VMEM] * 3 + [ANY] * 8,
+        out_shape=[jax.ShapeDtypeStruct((owner_rows, D), F32)]
+        + lines
+        + [jax.ShapeDtypeStruct(part.shape, part.dtype) for part in ready],
+        scratch_shapes=[pltpu.VMEM(part.shape, part.dtype) for part in ready]
+        + [
+            pltpu.VMEM((1, slots), jnp.int32),
+            pltpu.VMEM(incoming.shape, BF16),
+            pltpu.SemaphoreType.DMA,
+            pltpu.SemaphoreType.DMA((8,)),
         ],
-        out_specs=pl.BlockSpec((high, D), lambda step: (step, 0)),
-        out_shape=jax.ShapeDtypeStruct((owner_rows, D), F32),
-        compiler_params=pltpu.CompilerParams(vmem_limit_bytes=40 * 2**20),
+        compiler_params=pltpu.CompilerParams(vmem_limit_bytes=60 * 2**20),
         name="collect",
-    )(ids, incoming)
+    )(asked, small, incoming, *ready)
+
+
+OUTER, INNER, SQUARE, SMALL = (0, 1, 2, 3), (4, 5, 6, 7), (8, 9, 10, 11), 12
+
+
+def piece_columns(hidden):
+    quarter = hidden // 8
+    return (
+        [(0, 256), (256, 256), (512, TILE), (512 + TILE, TILE)]
+        + [(number * quarter, quarter) for number in range(4)]
+        + [(0, D // 2)] * 4
+    )
+
+
+def divided(numbers, by):
+    return ((numbers.astype(F32) + 0.5) * (1.0 / by)).astype(jnp.int32)
+
+
+def gather_columns(rows, per, width):
+    count = rows.shape[0]
+    column = lax.broadcasted_iota(jnp.int32, (TILE, width), 1)
+    lane = lax.broadcasted_iota(jnp.int32, (TILE, width), 0)
+    hot = lowered((column - divided(column, per) * per == lane).astype(F32))
+    spread = plain_product(rows, hot)
+    owner = divided(lax.broadcasted_iota(jnp.int32, (count, width), 1), per)
+    mine = owner == lax.broadcasted_iota(jnp.int32, (count, width), 0)
+    return jnp.sum(jnp.where(mine, spread, 0.0), axis=0, keepdims=True)
+
+
+def near_hot_columns():
+    column = lax.broadcasted_iota(jnp.int32, (NB * HEADS, 6 * TILE), 1)
+    kind = divided(column, 2 * TILE)
+    lane = column - kind * 2 * TILE
+    gap = jnp.where(lane < TILE, lane, lane - 2 * TILE)
+    bucket = relative_bucket((kind - 1) * TILE - gap)
+    entry = divided(lax.broadcasted_iota(jnp.int32, (NB * HEADS, 6 * TILE), 0), HEADS)
+    return lowered((entry == bucket).astype(F32))
+
+
+class ForwardIn(NamedTuple):
+    counts: Any
+    bucket: Any
+    lengths: Any
+    asked_rows: Any
+    order: Any
+    table: Any
+    w_query: Any
+    w_key: Any
+    w_value: Any
+    w_output: Any
+    w_inner: Any
+    w_outer: Any
+    small: Any
+
+
+class ForwardOut(NamedTuple):
+    full_query: Any
+    full_key: Any
+    full_value: Any
+    full_output: Any
+    full_inner: Any
+    full_outer: Any
+    asked: Any
+    slots: Any
+    gains: Any
+    block_out: Any
+    embedded: Any
+    normed: Any
+    query: Any
+    value: Any
+    key_t: Any
+    attended: Any
+    attended_t: Any
+    prob: Any
+    residual: Any
+    normed_two: Any
+    hidden: Any
+    slope: Any
+
+
+class ForwardScratch(NamedTuple):
+    full_small: Any
+    asks: Any
+    got: Any
+    table_v: Any
+    shard_square: Any
+    shard_inner: Any
+    near_square: Any
+    near_inner: Any
+    block_square: Any
+    block_inner: Any
+    turned: Any
+    one_hot: Any
+    found: Any
+    landed: Any
+    spread: Any
+    feature_k: Any
+    feature_q: Any
+    near_rows: Any
+    far_rows: Any
+    gain_rows: Any
+    small_v: Any
+    query_w: Any
+    key_w: Any
+    value_w: Any
+    output_w: Any
+    inner_w: Any
+    outer_w: Any
+    embedded_v: Any
+    normed_v: Any
+    query_v: Any
+    query_tv: Any
+    key_v: Any
+    key_tv: Any
+    value_v: Any
+    value_tv: Any
+    attended_tv: Any
+    attended_v: Any
+    residual_v: Any
+    normed_two_v: Any
+    hidden_v: Any
+    slope_v: Any
+    block_v: Any
+    prob_v: Any
+    slots_v: Any
+    ask_send: Any
+    ask_recv: Any
+    row_send: Any
+    row_recv: Any
+    pair_send: Any
+    pair_recv: Any
+    local_sem: Any
+    load_sem: Any
+    keep_sem: Any
+    prob_sem: Any
+    chain_send: Any
+    chain_recv: Any
+    first_send: Any
+    first_recv: Any
+    second_send: Any
+    second_recv: Any
+    core_send: Any
+    core_recv: Any
+
+
+def merged(refs, *kinds):
+    found, start = {}, 0
+    for kind in kinds:
+        end = start + len(kind._fields)
+        found.update(kind(*refs[start:end])._asdict())
+        start = end
+    return SimpleNamespace(**found)
+
+
+def forward_plan(k):
+    k.begin(SMALL)
+    k.squares()
+    k.begin(8, 9, 10, 11)
+    k.inner()
+    k.begin(4, 5, 6, 7)
+    k.places()
+    k.rise(1, SMALL, 8, 9, 10, 11)
+    k.ids()
+    k.rise(1, 4, 5, 6, 7)
+    k.rise(2, SMALL, 8, 9, 10, 11)
+    k.rise(2, 4, 5, 6, 7)
+    k.rise(3, SMALL, 8, 9, 10, 11)
+    k.rows(0, 4)
+    k.hand()
+    k.rise(3, 4, 5, 6, 7)
+    k.begin(0, 1, 2, 3)
+    k.features()
+    k.move(2, SMALL, 8, 9)
+    k.rise(1, 0, 1, 2, 3)
+    k.move(2, 10, 11)
+    k.move(3, SMALL, 8, 9)
+    k.rise(2, 0, 1, 2, 3)
+    k.move(2, 4, 5)
+    k.small()
+    k.move(3, 10, 11)
+    k.rise(3, 0, 1, 2, 3)
+    k.move(2, 6, 7)
+    k.embed()
+    k.load(0, 1)
+    k.project(0)
+    k.project(1)
+    k.load(2, 3)
+    k.project(2)
+    k.move(3, 4, 5)
+    k.move(2, 0, 1, 2, 3)
+    k.attend(0, 2)
+    k.move(3, 6, 7)
+    k.attend(2, 4)
+    k.move(3, 0, 1)
+    k.attend(4, 6)
+    k.branch()
+    k.load(4)
+    k.move(3, 2, 3)
+    k.widen()
+    k.load(5)
+    k.narrow()
+
+
+def forward_kernel(dims, cap, plan, *refs):
+    r = merged(refs, ForwardIn, ForwardOut, ForwardScratch)
+    place = Place(dims)
+    me, core = place.dp, place.core
+    count = place.count
+    squares = (r.w_query, r.w_key, r.w_value, r.w_output)
+
+    loads = [
+        pltpu.make_async_copy(ref, r.shard_square.at[number], r.load_sem.at[number])
+        for number, ref in enumerate(squares)
+    ]
+    loads.append(pltpu.make_async_copy(r.w_inner, r.shard_inner, r.load_sem.at[4]))
+    table_load = pltpu.make_async_copy(r.table, r.table_v, r.load_sem.at[7])
+    for copy in loads:
+        copy.start()
+    table_load.start()
+    greet(place)
+
+    wide = jnp.broadcast_to(r.asked_rows[...].astype(F32), (TILE, TOK_DEV))
+    columns = jnp.concatenate(
+        [jnp.transpose(wide[:, first : first + TILE]) for first in range(0, TOK_DEV, TILE)], axis=0
+    )
+    spots = lax.broadcasted_iota(jnp.int32, (TOK_DEV, TILE), 0)
+    lanes = lax.broadcasted_iota(jnp.int32, (TOK_DEV, TILE), 1)
+    lane_row = lax.broadcasted_iota(jnp.int32, (1, TILE), 1)
+
+    def fill_ask(owner, start):
+        amount = r.counts[0, owner]
+        values = jnp.sum(
+            jnp.where(spots - start == lanes, columns, 0.0), axis=0, keepdims=True
+        ).astype(jnp.int32)
+        values = jnp.where((lane_row < amount) & (lane_row < cap), values, -1)
+        r.asks[pl.ds(owner, 1)] = jnp.broadcast_to(values[None], (1, 8, TILE))
+        return start + amount
+
+    lax.fori_loop(0, count, fill_ask, jnp.int32(0))
+    meet(place)
+
+    def ask_copy(step):
+        peer, device = place.other(step)
+        return remote(
+            r.asks.at[peer], r.got.at[me], r.ask_send.at[step - 1], r.ask_recv.at[step - 1], device
+        )
+
+    def send_ask(step, carry):
+        ask_copy(step).start()
+        return carry
+
+    lax.fori_loop(1, count, send_ask, 0)
+    r.got[pl.ds(me, 1)] = r.asks[pl.ds(me, 1)]
+
+    pair_copies = [
+        remote(
+            squares[number],
+            r.near_square.at[number],
+            r.pair_send.at[number],
+            r.pair_recv.at[number],
+            place.sibling(),
+        )
+        for number in range(4)
+    ]
+    pair_copies.append(
+        remote(r.w_inner, r.near_inner, r.pair_send.at[4], r.pair_recv.at[4], place.sibling())
+    )
+    for copy in pair_copies:
+        copy.start()
+
+    spans = piece_columns(r.full_inner.shape[-1])
+    squares_full = (r.full_query, r.full_key, r.full_value, r.full_output)
+    total = len(spans) + 1
+
+    def view(piece, z, y, x):
+        if piece == SMALL:
+            return r.full_small.at[z, y, x, core]
+        first, width = spans[piece]
+        if piece in OUTER:
+            return r.full_outer.at[z, y, x, core, :, pl.ds(first, width)]
+        full = r.full_inner if piece in INNER else squares_full[piece - 8]
+        first = pl.multiple_of(core * (full.shape[-1] // 2) + first, TILE)
+        return full.at[z, y, x, :, pl.ds(first, width)]
+
+    def source(piece):
+        if piece == SMALL:
+            return r.small
+        first, width = spans[piece]
+        if piece in SQUARE:
+            return r.block_square.at[piece - 8]
+        held = r.w_outer if piece in OUTER else r.block_inner
+        return held.at[:, pl.ds(first, width)]
+
+    depth = place.at[0]
+    rounds = dims[0] - 1
+
+    def chain(act, piece, turn, arrival):
+        for way, sign in enumerate((1, -1)):
+            if arrival:
+                block = depth - sign * turn
+                valid = block >= 0 if sign == 1 else block < dims[0]
+            else:
+                block = depth - sign * (turn - 1)
+                valid = (block >= 0) & (depth + 1 < dims[0]) if sign == 1 else (block < dims[0]) & (depth > 0)
+
+            @pl.when(valid)
+            def _():
+                here = view(piece, block, place.at[1], place.at[2])
+                start = source(piece) if turn == 1 and not arrival else here
+                copy = remote(
+                    start,
+                    here,
+                    r.chain_send.at[piece, way, turn - 1],
+                    r.chain_recv.at[piece, way, turn - 1],
+                    place.peer(0, sign)[1],
+                )
+                act(copy, block)
+
+    def first_copies(piece, block, start=None):
+        axis = GATHER_ORDER[piece % 2][1]
+        here = view(piece, block, place.at[1], place.at[2])
+        return [
+            remote(
+                here if start is None else start,
+                here,
+                r.first_send.at[piece, block, step - 1],
+                r.first_recv.at[piece, block, step - 1],
+                place.peer(axis, step)[1],
+            )
+            for step in range(1, dims[axis])
+        ]
+
+    def second_copies(piece, column):
+        _, first, second = GATHER_ORDER[piece % 2]
+        pick = [ALL, place.at[1], place.at[2]]
+        pick[first] = (pick[first] - column + dims[first]) % dims[first]
+        here = view(piece, *pick)
+        return [
+            remote(
+                here,
+                here,
+                r.second_send.at[piece, column, step - 1],
+                r.second_recv.at[piece, column, step - 1],
+                place.peer(second, step)[1],
+            )
+            for step in range(1, dims[second])
+        ]
+
+    def core_copy(piece):
+        here = view(piece, ALL, ALL, ALL)
+        return remote(here, here, r.core_send.at[piece], r.core_recv.at[piece], place.sibling())
+
+    def keep_copy(piece):
+        return pltpu.make_async_copy(source(piece), view(piece, *place.at), r.keep_sem.at[piece])
+
+    def begin(*chosen):
+        for piece in chosen:
+            chain(lambda copy, block: copy.start(), piece, 1, False)
+            for copy in first_copies(piece, depth, source(piece)):
+                copy.start()
+            keep_copy(piece).start()
+
+    def rise(turn, *chosen):
+        for piece in chosen:
+
+            def pass_on(copy, block):
+                copy.wait_recv()
+                for other in first_copies(piece, block):
+                    other.start()
+
+            chain(pass_on, piece, turn, True)
+            if turn < rounds:
+                chain(lambda copy, block: copy.start(), piece, turn + 1, False)
+            else:
+                keep_copy(piece).wait()
+                for copy in second_copies(piece, 0):
+                    copy.start()
+
+    def move(phase, *chosen):
+        for piece in chosen:
+            first = GATHER_ORDER[piece % 2][1]
+            for column in range(1 if phase == 2 else 0, dims[first]):
+                if phase == 2:
+                    for block in range(dims[0]):
+                        first_copies(piece, block)[column - 1].wait_recv()
+                    for copy in second_copies(piece, column):
+                        copy.start()
+                else:
+                    for copy in second_copies(piece, column):
+                        copy.wait_recv()
+            if phase == 3:
+                core_copy(piece).start()
+
+    saved = []
+    waits, base, landed = {}, [], []
+
+    def save(source, target):
+        copy = pltpu.make_async_copy(source, target, r.local_sem.at[2 + len(saved)])
+        copy.start()
+        saved.append(copy)
+
+    def find_places():
+        token = lax.broadcasted_iota(jnp.int32, (1, TOK_DEV), 1)
+
+        def find_slot(owner, carry):
+            end, owners, begun = carry
+            amount = r.counts[0, owner]
+            end = end + amount
+            past = token >= end
+            return end, owners + past.astype(jnp.int32), begun + jnp.where(past, amount, 0)
+
+        zero = jnp.zeros((1, TOK_DEV), jnp.int32)
+        _, owners, begun = lax.fori_loop(0, count, find_slot, (jnp.int32(0), zero, zero))
+        slot = (owners * cap + token - begun).astype(F32)
+        order = r.order[...]
+        for first in range(0, TOK_DEV, TILE):
+            ids = lax.broadcasted_iota(jnp.int32, (TILE, TOK_DEV), 0) + first
+            own_slot = jnp.sum(jnp.where(ids == order, slot, 0.0), axis=1, keepdims=True)
+            own_slot = jnp.broadcast_to(own_slot, (TILE, TILE))
+            r.slots_v[:, first : first + TILE] = jnp.transpose(own_slot)[:8].astype(jnp.int32)
+            wanted = lax.broadcasted_iota(jnp.int32, (TILE, count * cap), 1)
+            hot = wanted == own_slot[:, :1].astype(jnp.int32)
+            r.spread[first : first + TILE, :] = lowered(hot.astype(F32))
+
+        save(r.slots_v, r.slots)
+
+    def joined(mine, theirs):
+        mine, theirs = mine.astype(F32), theirs.astype(F32)
+        both = jnp.concatenate(
+            [jnp.where(core == 0, mine, theirs), jnp.where(core == 0, theirs, mine)], axis=0
+        )
+        half = both.shape[1] // 2
+        return lowered(jnp.where(core == 0, both[:, :half], both[:, half:]))
+
+    def join_squares():
+        for number in range(4):
+            loads[number].wait()
+            pair_copies[number].wait()
+            r.block_square[number] = joined(r.shard_square[number], r.near_square[number])
+
+    def join_inner():
+        loads[4].wait()
+        pair_copies[4].wait()
+        r.block_inner[...] = joined(r.shard_inner[...], r.near_inner[...])
+
+    def wait_ask(step, carry):
+        ask_copy(step).wait()
+        return carry
+
+    def turn_ids():
+        lax.fori_loop(1, count, wait_ask, 0)
+        table_load.wait()
+        r.turned[...] = jnp.zeros((TILE, TILE), F32)
+        r.turned[pl.ds(0, count)] = r.got[:, 0, :].astype(F32)
+        r.turned[...] = jnp.transpose(r.turned[...])
+
+    table_rows = r.table_v.shape[0]
+    group = max(1, min(count, 256 // cap))
+
+    def row_copy(block):
+        return remote(
+            r.found.at[block], r.landed.at[me], r.row_send.at[block], r.row_recv.at[me], (block, core)
+        )
+
+    def row_arrival(block):
+        return remote(
+            r.found.at[block],
+            r.landed.at[block],
+            r.row_send.at[block],
+            r.row_recv.at[block],
+            (block, core),
+        )
+
+    def find_group(number, carry):
+        lane = lax.broadcasted_iota(jnp.int32, (cap, TILE), 1)
+        spot = lax.broadcasted_iota(jnp.int32, (cap, table_rows), 1)
+        for inside in range(group):
+            block = number * group + inside
+            ids = jnp.sum(
+                jnp.where(lane == block, r.turned[0:cap, :], 0.0), axis=1, keepdims=True
+            ).astype(jnp.int32)
+            r.one_hot[inside * cap : (inside + 1) * cap, :] = lowered((spot == ids).astype(F32))
+        rows = lowered(plain_product(r.one_hot[...], r.table_v[...]))
+        for inside in range(group):
+            block = number * group + inside
+            r.found[pl.ds(block, 1)] = rows[inside * cap : (inside + 1) * cap][None]
+
+            @pl.when(block != me)
+            def _():
+                row_copy(block).start()
+
+        return carry
+
+    def look_up(first, last):
+        groups = count // group
+        lax.fori_loop(first * groups // 4, last * groups // 4, find_group, 0)
+
+    own_rows = pltpu.make_async_copy(r.found.at[me], r.landed.at[me], r.local_sem.at[0])
+    own_asks = pltpu.make_async_copy(r.got, r.asked.at[core], r.local_sem.at[1])
+    asks_across = remote(
+        r.got, r.asked.at[core], r.pair_send.at[5], r.pair_recv.at[5], place.sibling()
+    )
+    row_extras = (own_asks, asks_across)
+
+    def hand_on():
+        for copy in (own_rows, *row_extras):
+            copy.start()
+
+    shift = 6 + r.bucket[0]
+    key_spot = lax.broadcasted_iota(jnp.int32, (TOK_DEV, TILE), 0)
+    key_lane = lax.broadcasted_iota(jnp.int32, (TOK_DEV, TILE), 1)
+    document = key_spot >> shift
+
+    def find_features():
+        length = jnp.zeros((1, TILE), jnp.int32)
+        for number in range(TOK_DEV // SHORT):
+            length = jnp.where(lane_row == number, r.lengths[number], length)
+        usable = (document == key_lane) & (key_spot - (document << shift) < length)
+        base.append(jnp.where(usable | (key_lane >= 8), 0.0, -BIG))
+        row = lax.broadcasted_iota(jnp.int32, (TILE, TOK_DEV), 0)
+        query_spot = lax.broadcasted_iota(jnp.int32, (TILE, TOK_DEV), 1)
+        wanted_row = jnp.where(row < 8, query_spot >> shift, query_spot // TILE + 8)
+        r.feature_q[...] = lowered((row == wanted_row).astype(F32))
+
+
+    def spread_small():
+        core_copy(SMALL).wait()
+        small_load = pltpu.make_async_copy(r.full_small, r.small_v, r.load_sem.at[0])
+        small_load.start()
+        small_load.wait()
+        shards = r.small_v.shape[0] * r.small_v.shape[1] * r.small_v.shape[2] * 2
+        small_rows = r.small_v[...].reshape(shards, 16, TILE)
+        gain_one = gather_columns(small_rows[:, 0, :], D // shards, D)
+        gain_two = gather_columns(small_rows[:, 1, :], D // shards, D)
+        bias = gather_columns(small_rows[:, 2, :], NB * HEADS // shards, NB * HEADS)
+        r.gain_rows[...] = jnp.concatenate([gain_one, gain_two, jnp.zeros((6, D), F32)], axis=0)
+        save(r.gain_rows, r.gains)
+        entry = lax.broadcasted_iota(jnp.int32, (16, NB * HEADS), 1)
+        entry_bucket = divided(entry, HEADS)
+        own_head = entry - entry_bucket * HEADS == lax.broadcasted_iota(
+            jnp.int32, (16, NB * HEADS), 0
+        )
+        by_head = jnp.where(own_head, bias, 0.0)
+        r.near_rows[...] = plain_product(lowered(by_head), near_hot_columns())
+        ahead = jnp.sum(jnp.where(entry_bucket == 31, by_head, 0.0), axis=1, keepdims=True)
+        behind = jnp.sum(jnp.where(entry_bucket == 15, by_head, 0.0), axis=1, keepdims=True)
+        key_tile = key_spot // TILE
+        lane_tile = key_lane - 8
+        inside = (lane_tile >= 0) & (lane_tile < TOK_DEV // TILE)
+        far_after = inside & (key_tile - lane_tile >= 2)
+        far_before = inside & (key_tile - lane_tile <= -2)
+        r.far_rows[0] = jnp.broadcast_to(ahead, (16, TILE))
+        r.far_rows[1] = jnp.broadcast_to(behind, (16, TILE))
+
+        def fill_feature(head, carry):
+            extra = jnp.where(
+                far_after,
+                r.far_rows[0, pl.ds(head, 1), :],
+                jnp.where(far_before, r.far_rows[1, pl.ds(head, 1), :], 0.0),
+            )
+            r.feature_k[pl.ds(head, 1)] = lowered(base[0] + extra)[None]
+            return carry
+
+        lax.fori_loop(0, HEADS, fill_feature, 0)
+
+    def wait_row(block, carry):
+        @pl.when(block != me)
+        def _():
+            row_copy(block).wait_send()
+            row_arrival(block).wait_recv()
+
+        return carry
+
+    def embed(part, carry):
+        rows = pl.ds(part * 256, 256)
+        values = plain_product(r.spread[rows, :], landed[0])
+        r.embedded_v[rows, :] = values
+        scale = lax.rsqrt(jnp.mean(values * values, axis=1, keepdims=True) + EPSILON)
+        r.normed_v[rows, :] = lowered(values * scale * r.gain_rows[0:1, :])
+        return carry
+
+    def embed_rows():
+        lax.fori_loop(0, count, wait_row, 0)
+        own_rows.wait()
+        landed.append(r.landed[...].reshape(count * cap, D))
+        lax.fori_loop(0, TOK_DEV // 256, embed, 0)
+        save(r.embedded_v, r.embedded)
+        save(r.normed_v, r.normed)
+
+    def load_weight(number, full, held, *needs):
+        for piece in needs:
+            core_copy(piece).wait_recv()
+        shape = held.shape
+        copy = pltpu.make_async_copy(full.reshape(*shape), held, r.load_sem.at[number])
+        copy.start()
+        return copy
+
+    def project(weight, rows_ref, turned_ref):
+        def tile(number, carry):
+            span = pl.ds(pl.multiple_of(number * 256, 256), 256)
+            values = lowered(plain_product(r.normed_v[...], weight[:, span]))
+            rows_ref[:, span] = values
+            turned_ref[span, :] = jnp.transpose(values)
+            return carry
+
+        lax.fori_loop(0, D // 256, tile, 0)
+
+    weights = (
+        (r.full_query, r.query_w, 8),
+        (r.full_key, r.key_w, 9),
+        (r.full_value, r.value_w, 10),
+        (r.full_output, r.output_w, 11),
+        (r.full_inner, r.inner_w, *INNER),
+        (r.full_outer, r.outer_w, *OUTER),
+    )
+
+    def load(*numbers):
+        for number in numbers:
+            waits[number] = load_weight(number + 1, *weights[number])
+
+    def project_one(number):
+        held, rows_ref, turned_ref, source, target = (
+            (r.query_w, r.query_v, r.query_tv, r.query_v, r.query),
+            (r.key_w, r.key_v, r.key_tv, r.key_tv, r.key_t),
+            (r.value_w, r.value_v, r.value_tv, r.value_v, r.value),
+        )[number]
+        waits[number].wait()
+        project(held, rows_ref, turned_ref)
+        save(source, target)
+
+    tiles = TOK_DEV // TILE
+
+    def prob_copy(pair):
+        return pltpu.make_async_copy(
+            r.prob_v.at[pair % 2], r.prob.at[pl.ds(pair * 2, 2)], r.prob_sem.at[pair % 2]
+        )
+
+    def attend_pair(pair, carry):
+        @pl.when(pair >= 2)
+        def _():
+            prob_copy(pair - 2).wait()
+
+        span = pl.ds(pl.multiple_of(pair * TILE, TILE), TILE)
+        slot = pair % 2
+        for head in range(2):
+            number = pair * 2 + head
+            mask = pair_mask((TOK_DEV, TILE), 1, head)
+            masked_key = lowered(jnp.where(mask, r.key_v[:, span].astype(F32), 0.0))
+            left = jnp.concatenate([masked_key, r.feature_k[number]], axis=1)
+            near = r.near_rows[pl.ds(number, 1), :]
+            bias_tiles = [
+                near_tile(near[:, kind * 2 * TILE : (kind + 1) * 2 * TILE]) for kind in range(3)
+            ]
+            values = r.value_tv[pl.ds(pl.multiple_of(number * HEAD_DIM, HEAD_DIM), HEAD_DIM), :]
+            for strip in range(2):
+                cols = slice(strip * 256, (strip + 1) * 256)
+                right = jnp.concatenate([r.query_tv[span, cols], r.feature_q[:, cols]], axis=0)
+                scores = plain_product(left, right)
+                rows = []
+                for key_block in range(tiles):
+                    parts = []
+                    for inner in range(2):
+                        gap = key_block - (strip * 2 + inner)
+                        part = scores[
+                            key_block * TILE : (key_block + 1) * TILE,
+                            inner * TILE : (inner + 1) * TILE,
+                        ]
+                        parts.append(part + bias_tiles[gap + 1] if abs(gap) <= 1 else part)
+                    rows.append(jnp.concatenate(parts, axis=1))
+                scores = jnp.concatenate(rows, axis=0)
+                peak = jnp.max(scores, axis=0, keepdims=True)
+                powers = jnp.exp(scores - peak)
+                share = 1.0 / jnp.sum(powers, axis=0, keepdims=True)
+                weights = lowered(powers * share)
+                r.prob_v[slot, head, :, cols] = weights
+                r.attended_tv[
+                    pl.ds(pl.multiple_of(number * HEAD_DIM, HEAD_DIM), HEAD_DIM), cols
+                ] = lowered(plain_product(values, weights))
+        r.attended_v[:, span] = jnp.transpose(r.attended_tv[span, :])
+        prob_copy(pair).start()
+        return carry
+
+    pairs = HEADS // 2
+
+    def attend_some(first, last):
+        lax.fori_loop(first, last, attend_pair, 0)
+
+    def add_branch(part, carry):
+        rows = pl.ds(part * 256, 256)
+        values = r.embedded_v[rows, :] + plain_product(r.attended_v[rows, :], r.output_w[...])
+        r.residual_v[rows, :] = values
+        scale = lax.rsqrt(jnp.mean(values * values, axis=1, keepdims=True) + EPSILON)
+        r.normed_two_v[rows, :] = lowered(values * scale * r.gain_rows[1:2, :])
+        return carry
+
+    def branch_out():
+        save(r.attended_tv, r.attended_t)
+        save(r.attended_v, r.attended)
+        waits[3].wait()
+        lax.fori_loop(0, TOK_DEV // 256, add_branch, 0)
+        save(r.residual_v, r.residual)
+        save(r.normed_two_v, r.normed_two)
+
+    def widen(number, carry):
+        span = pl.ds(pl.multiple_of(number * 256, 256), 256)
+        values = plain_product(r.normed_two_v[...], r.inner_w[:, span])
+        square = values * values
+        curve = jnp.tanh(values * (GELU_A + GELU_A * GELU_B * square))
+        half = 0.5 * (1.0 + curve)
+        r.hidden_v[:, span] = lowered(values * half)
+        r.slope_v[:, span] = lowered(
+            half
+            + 0.5 * values * (1.0 - curve * curve) * (GELU_A + 3.0 * GELU_A * GELU_B * square)
+        )
+        return carry
+
+    def widen_all():
+        waits[4].wait()
+        lax.fori_loop(0, r.hidden_v.shape[1] // 256, widen, 0)
+        save(r.hidden_v, r.hidden)
+        save(r.slope_v, r.slope)
+
+    def narrow(number, carry):
+        span = pl.ds(pl.multiple_of(number * 256, 256), 256)
+        values = r.residual_v[:, span] + plain_product(r.hidden_v[...], r.outer_w[:, span])
+        r.block_v[:, span] = lowered(values)
+        return carry
+
+    def narrow_all():
+        waits[5].wait()
+        lax.fori_loop(0, D // 256, narrow, 0)
+        save(r.block_v, r.block_out)
+
+    steps = SimpleNamespace(
+        begin=begin,
+        rise=rise,
+        move=move,
+        places=find_places,
+        squares=join_squares,
+        inner=join_inner,
+        ids=turn_ids,
+        rows=look_up,
+        hand=hand_on,
+        features=find_features,
+        small=spread_small,
+        embed=embed_rows,
+        load=load,
+        project=project_one,
+        attend=attend_some,
+        branch=branch_out,
+        widen=widen_all,
+        narrow=narrow_all,
+    )
+    plan(steps)
+
+    for copy in row_extras:
+        copy.wait()
+    prob_copy(pairs - 2).wait()
+    prob_copy(pairs - 1).wait()
+    for copy in saved:
+        copy.wait()
+    for piece in range(total):
+        for turn in range(1, rounds + 1):
+            chain(lambda copy, block: copy.wait_send(), piece, turn, False)
+        for block in range(dims[0]):
+            for copy in first_copies(piece, block):
+                copy.wait_send()
+        for column in range(dims[GATHER_ORDER[piece % 2][1]]):
+            for copy in second_copies(piece, column):
+                copy.wait_send()
+        if piece != SMALL:
+            core_copy(piece).wait_send()
+
+
+def forward(dims, counts, bucket, lengths, asked_rows, order, table, squares, w_inner, w_outer, small):
+    count = dims[0] * dims[1] * dims[2]
+    cap = 2 * TOK_DEV // count
+    rows = 2 * squares[0].shape[0]
+    hidden = w_inner.shape[1]
+    tokens, turned = (TOK_DEV, D), (D, TOK_DEV)
+    square = ((*dims, rows, D), BF16)
+    outer = (*dims, 2, *w_outer.shape)
+    shapes = ForwardOut(
+        full_query=square,
+        full_key=square,
+        full_value=square,
+        full_output=square,
+        full_inner=((*dims, rows, hidden), BF16),
+        full_outer=(outer, BF16),
+        asked=((2, count, 8, TILE), jnp.int32),
+        slots=((8, TOK_DEV), jnp.int32),
+        gains=((8, D), F32),
+        block_out=(tokens, BF16),
+        embedded=(tokens, F32),
+        normed=(tokens, BF16),
+        query=(tokens, BF16),
+        value=(tokens, BF16),
+        key_t=(turned, BF16),
+        attended=(tokens, BF16),
+        attended_t=(turned, BF16),
+        prob=((HEADS, TOK_DEV, TOK_DEV), BF16),
+        residual=(tokens, F32),
+        normed_two=(tokens, BF16),
+        hidden=((TOK_DEV, hidden), BF16),
+        slope=((TOK_DEV, hidden), BF16),
+    )
+    steps = max(dims[1:]) - 1
+    dma, vmem = pltpu.SemaphoreType.DMA, pltpu.VMEM
+    whole = vmem((D, D), BF16)
+    scratch = ForwardScratch(
+        full_small=vmem((*dims, 2, *small.shape), BF16),
+        asks=vmem((count, 8, TILE), jnp.int32),
+        got=vmem((count, 8, TILE), jnp.int32),
+        table_v=vmem(table.shape, BF16),
+        shard_square=vmem((4, *squares[0].shape), BF16),
+        shard_inner=vmem(w_inner.shape, BF16),
+        near_square=vmem((4, *squares[0].shape), BF16),
+        near_inner=vmem(w_inner.shape, BF16),
+        block_square=vmem((4, rows, D // 2), BF16),
+        block_inner=vmem((rows, hidden // 2), BF16),
+        turned=vmem((TILE, TILE), F32),
+        one_hot=vmem((max(1, min(count, 256 // cap)) * cap, table.shape[0]), BF16),
+        found=vmem((count, cap, D), BF16),
+        landed=vmem((count, cap, D), BF16),
+        spread=vmem((TOK_DEV, count * cap), BF16),
+        feature_k=vmem((HEADS, TOK_DEV, TILE), BF16),
+        feature_q=vmem((TILE, TOK_DEV), BF16),
+        near_rows=vmem((16, 6 * TILE), F32),
+        far_rows=vmem((2, 16, TILE), F32),
+        gain_rows=vmem((8, D), F32),
+        small_v=vmem((*dims, 2, *small.shape), BF16),
+        query_w=whole,
+        key_w=whole,
+        value_w=whole,
+        output_w=whole,
+        inner_w=vmem((D, hidden), BF16),
+        outer_w=vmem((hidden, D), BF16),
+        embedded_v=vmem(tokens, F32),
+        normed_v=vmem(tokens, BF16),
+        query_v=vmem(tokens, BF16),
+        query_tv=vmem(turned, BF16),
+        key_v=vmem(tokens, BF16),
+        key_tv=vmem(turned, BF16),
+        value_v=vmem(tokens, BF16),
+        value_tv=vmem(turned, BF16),
+        attended_tv=vmem(turned, BF16),
+        attended_v=vmem(tokens, BF16),
+        residual_v=vmem(tokens, F32),
+        normed_two_v=vmem(tokens, BF16),
+        hidden_v=vmem((TOK_DEV, hidden), BF16),
+        slope_v=vmem((TOK_DEV, hidden), BF16),
+        block_v=vmem(tokens, BF16),
+        prob_v=vmem((2, 2, TOK_DEV, TOK_DEV), BF16),
+        slots_v=vmem((8, TOK_DEV), jnp.int32),
+        ask_send=dma((count - 1,)),
+        ask_recv=dma((count - 1,)),
+        row_send=dma((count,)),
+        row_recv=dma((count,)),
+        pair_send=dma((6,)),
+        pair_recv=dma((6,)),
+        local_sem=dma((18,)),
+        load_sem=dma((8,)),
+        keep_sem=dma((13,)),
+        prob_sem=dma((2,)),
+        chain_send=dma((13, 2, dims[0] - 1)),
+        chain_recv=dma((13, 2, dims[0] - 1)),
+        first_send=dma((13, dims[0], steps)),
+        first_recv=dma((13, dims[0], steps)),
+        second_send=dma((13, steps + 1, steps)),
+        second_recv=dma((13, steps + 1, steps)),
+        core_send=dma((13,)),
+        core_recv=dma((13,)),
+    )
+    found = pl.pallas_call(
+        partial(forward_kernel, dims, cap, forward_plan),
+        out_shape=[jax.ShapeDtypeStruct(*shape) for shape in shapes],
+        in_specs=[SMEM] * 3 + [VMEM] * 2 + [ANY] * 8,
+        out_specs=[ANY] * len(shapes),
+        scratch_shapes=list(scratch),
+        compiler_params=pltpu.CompilerParams(
+            collective_id=3, has_side_effects=True, vmem_limit_bytes=60 * 2**20
+        ),
+        name="forward",
+    )(counts, bucket, lengths, asked_rows, order, table, *squares, w_inner, w_outer, small)
+    return ForwardOut(*found)
+
+
+def split_product(left_side, right_side, product):
+    high = lowered(left_side)
+    rest = left_side - high.astype(F32)
+    middle = lowered(rest)
+    low = lowered(rest - middle.astype(F32))
+    return product(high, right_side) + product(middle, right_side) + product(low, right_side)
+
+
+def scatter_columns(flat, per, count):
+    width = flat.shape[1]
+    column = lax.broadcasted_iota(jnp.int32, (count, width), 1)
+    owner = divided(column, per)
+    picked = jnp.where(owner == lax.broadcasted_iota(jnp.int32, (count, width), 0), flat, 0.0)
+    row = lax.broadcasted_iota(jnp.int32, (width, TILE), 0)
+    lane = lax.broadcasted_iota(jnp.int32, (width, TILE), 1)
+    hot = lowered((row - divided(row, per) * per == lane).astype(F32))
+    return split_product(picked, hot, plain_product)
+
+
+class BackwardIn(NamedTuple):
+    full_query: Any
+    full_key: Any
+    full_value: Any
+    full_output: Any
+    full_inner: Any
+    full_outer: Any
+    slots: Any
+    gains: Any
+    embedded: Any
+    normed: Any
+    query: Any
+    value: Any
+    key_t: Any
+    attended_t: Any
+    prob: Any
+    residual: Any
+    normed_two: Any
+    hidden: Any
+    slope: Any
+    cotangent: Any
+
+
+class BackwardOut(NamedTuple):
+    out_query: Any
+    out_key: Any
+    out_value: Any
+    out_output: Any
+    out_inner: Any
+    out_outer: Any
+    out_small: Any
+    incoming: Any
+    input_grad: Any
+
+
+class BackwardScratch(NamedTuple):
+    stage_outer: Any
+    stage_square: Any
+    small_v: Any
+    small_in: Any
+    small_sum: Any
+    small_pair: Any
+    outer_w: Any
+    inner_w: Any
+    output_w: Any
+    hidden_v: Any
+    slope_v: Any
+    cot_v: Any
+    turned_v: Any
+    residual_v: Any
+    grad_v: Any
+    attended_tv: Any
+    value_v: Any
+    query_v: Any
+    key_tv: Any
+    branch_v: Any
+    branch_tv: Any
+    merged_v: Any
+    leaving: Any
+    slots_v: Any
+    gains_v: Any
+    near_sums: Any
+    far_sums: Any
+    gain_sums: Any
+    load_sem: Any
+    prob_sem: Any
+    row_send: Any
+    row_recv: Any
+    over_send: Any
+    over_recv: Any
+    small_send: Any
+    small_recv: Any
+    pair_send: Any
+    pair_recv: Any
+    local_sem: Any
+    chain_send: Any
+    chain_recv: Any
+    axis_send: Any
+    axis_recv: Any
+    end_send: Any
+    end_recv: Any
+
+
+def backward_plan(k):
+    k.outer()
+    k.back()
+    k.move(0, 0, 1, 2, 3)
+    k.inner()
+    k.two()
+    k.move(0, 4, 5, 6, 7)
+    k.branch()
+    k.square(11)
+    k.attend(0, 2)
+    k.move(1, 0, 1, 2, 3)
+    k.attend(2, 6)
+    k.move(2, 0, 1, 2, 3)
+    k.one()
+    k.move(1, 4, 5, 6, 7)
+    k.sink(1, 0, 1, 2, 3)
+    k.leave(0, 4)
+    k.own()
+    k.sink(2, 0, 1, 2, 3)
+    k.square(8)
+    k.square(9)
+    k.square(10)
+    k.move(2, 4, 5, 6, 7)
+    k.move(0, 8, 9, 10, 11)
+    k.finish(0, 1, 2, 3)
+    k.sink(1, 4, 5, 6, 7)
+    k.small()
+    k.move(1, 8, 9, 10, 11)
+    k.sink(2, 4, 5, 6, 7)
+    k.move(2, 8, 9, 10, 11)
+    k.finish(4, 5, 6, 7)
+    k.sink(1, 8, 9, 10, 11)
+    k.over(0, 4)
+    k.sink(2, 8, 9, 10, 11)
+    k.finish(8, 9, 10, 11)
+    k.end()
+
+
+def backward_kernel(dims, cap, plan, *refs):
+    apart = len(BackwardIn._fields) + len(BackwardOut._fields)
+    r = merged((*refs[:apart], *refs[apart + 72 :]), BackwardIn, BackwardOut, BackwardScratch)
+    place = Place(dims)
+    me, core = place.dp, place.core
+    count = place.count
+    held, across, first_in, second_in, risen, final = (
+        refs[apart + 12 * number : apart + 12 * number + 12] for number in range(6)
+    )
+    arrived = list(zip(first_in, second_in))
+    started = []
+
+    def load(source, target):
+        copy = pltpu.make_async_copy(source, target, r.load_sem.at[len(started)])
+        copy.start()
+        started.append(copy)
+        return copy
+
+    outer_rows = r.outer_w.shape[0]
+    hidden_load = load(r.hidden, r.hidden_v)
+    cot_load = load(r.cotangent, r.cot_v)
+    outer_load = load(r.full_outer.reshape(outer_rows, D), r.outer_w)
+    slope_load = load(r.slope, r.slope_v)
+    two_load = load(r.normed_two, r.branch_v)
+    inner_load = load(r.full_inner.reshape(D, outer_rows), r.inner_w)
+    residual_load = load(r.residual, r.residual_v)
+    gains_load = load(r.gains, r.gains_v)
+    output_load = load(r.full_output.reshape(D, D), r.output_w)
+    attended_load = load(r.attended_t, r.attended_tv)
+    value_load = load(r.value, r.value_v)
+    query_load = load(r.query, r.query_v)
+    key_load = load(r.key_t, r.key_tv)
+    slots_load = load(r.slots, r.slots_v)
+    enter(place)
+
+    blocks = dims[0] * dims[1] * dims[2]
+
+    def spot_of(chip):
+        return chip // (dims[1] * dims[2]), (chip // dims[2]) % dims[1], chip % dims[2]
+
+    spans = piece_columns(outer_rows)
+    depth = place.at[0]
+    rounds = dims[0] - 1
+
+    def stage(piece):
+        first, width = spans[piece]
+        if piece in OUTER:
+            return r.stage_outer.at[:, :, :, :, pl.ds(first, width)]
+        if piece in SQUARE:
+            return r.stage_square.at[piece - 8]
+        half = (piece - 4) // 2
+        rows = r.outer_w.at[pl.ds(half * D, D), :].reshape(*dims, D // blocks, D)
+        return rows.at[:, :, :, :, pl.ds((piece % 2) * width, width)]
+
+    def pair_copy(piece):
+        return remote(
+            stage(piece), across[piece], r.pair_send.at[piece], r.pair_recv.at[piece], place.sibling()
+        )
+
+    def axis_copies(piece, phase):
+        order = REDUCE_ORDER[piece % 2]
+        axis = order[phase]
+        copies = []
+        for step in range(1, dims[axis]):
+            spot, device = place.peer(axis, step)
+            pick = [
+                spot if a == axis else (place.at[a] if a in order[:phase] else ALL)
+                for a in range(3)
+            ]
+            copies.append(
+                remote(
+                    held[piece].at[pick[0], pick[1], pick[2]],
+                    arrived[piece][phase].at[step - 1],
+                    r.axis_send.at[piece, phase, step - 1],
+                    r.axis_recv.at[piece, phase, step - 1],
+                    device,
+                )
+            )
+        return copies
+
+    def chain(act, piece, turn, arrival):
+        for way, sign in enumerate((1, -1)):
+            block = depth + sign * (rounds - turn if arrival else rounds + 1 - turn)
+            near = depth - sign if arrival else depth + sign
+            valid = (block >= 0) & (block < dims[0]) & (near >= 0) & (near < dims[0])
+
+            @pl.when(valid)
+            def _():
+                copy = remote(
+                    held[piece].at[block, place.at[1], place.at[2]],
+                    risen[piece].at[way, turn - 1],
+                    r.chain_send.at[piece, way, turn - 1],
+                    r.chain_recv.at[piece, way, turn - 1],
+                    place.peer(0, sign)[1],
+                )
+                act(copy, block, way)
+
+    def add_across(piece):
+        def one(index, carry):
+            spot = spot_of(index)
+            held[piece][spot] = held[piece][spot] + across[piece][spot]
+            return carry
+
+        lax.fori_loop(0, blocks, one, 0)
+
+    def add_arrived(piece, phase):
+        order = REDUCE_ORDER[piece % 2]
+        free = [a for a in range(3) if a not in order[: phase + 1]]
+        amount = 1
+        for a in free:
+            amount *= dims[a]
+
+        def one(index, carry):
+            spot = list(place.at)
+            inner_spot = []
+            rest = index
+            for a in reversed(free):
+                spot[a] = rest % dims[a]
+                inner_spot.insert(0, rest % dims[a])
+                rest = rest // dims[a]
+            value = held[piece][tuple(spot)]
+            for step in range(dims[order[phase]] - 1):
+                value = value + arrived[piece][phase][(step, *inner_spot)]
+            held[piece][tuple(spot)] = value
+            return carry
+
+        lax.fori_loop(0, amount, one, 0)
+
+    outs = (r.out_query, r.out_key, r.out_value, r.out_output)
+
+    def end_copies(piece):
+        first, width = spans[piece]
+        if piece in OUTER:
+            part = r.out_outer.at[:, pl.ds(first, width)]
+            return [pltpu.make_async_copy(final[piece], part, r.end_send.at[piece])]
+        out = r.out_inner if piece in INNER else outs[piece - 8]
+        first = pl.multiple_of(core * (out.shape[-1] // 2) + first, TILE)
+        part = out.at[:, pl.ds(first, width)]
+        return [
+            pltpu.make_async_copy(final[piece].at[core], part, r.local_sem.at[piece]),
+            remote(
+                final[piece].at[1 - core],
+                part,
+                r.end_send.at[piece],
+                r.end_recv.at[piece],
+                place.sibling(),
+            ),
+        ]
+
+    def add_final(piece, value, fresh):
+        if piece in OUTER:
+            final[piece][...] = value if fresh else final[piece][...] + value
+            return
+        half = value.shape[0] // 2
+        for number in range(2):
+            part = value[number * half : (number + 1) * half]
+            final[piece][number] = part if fresh else final[piece][number] + part
+
+    def move(phase, *chosen):
+        for piece in chosen:
+            if phase == 0:
+                pair_copy(piece).wait_recv()
+                add_across(piece)
+            else:
+                for copy in axis_copies(piece, phase - 1):
+                    copy.wait_recv()
+                add_arrived(piece, phase - 1)
+            if phase < 2:
+                for copy in axis_copies(piece, phase):
+                    copy.start()
+            else:
+                chain(lambda copy, block, way: copy.start(), piece, 1, False)
+
+    def sink(turn, *chosen):
+        for piece in chosen:
+
+            def add(copy, block, way):
+                copy.wait_recv()
+                spot = (block, place.at[1], place.at[2])
+                held[piece][spot] = held[piece][spot] + risen[piece][way, turn - 1]
+
+            chain(add, piece, turn, True)
+            chain(lambda copy, block, way: copy.start(), piece, turn + 1, False)
+
+    def finish(*chosen):
+        for piece in chosen:
+            add_final(piece, held[piece][place.at].astype(F32), True)
+
+            def add(copy, block, way):
+                copy.wait_recv()
+                add_final(piece, risen[piece][way, rounds - 1].astype(F32), False)
+
+            chain(add, piece, rounds, True)
+            for copy in end_copies(piece):
+                copy.start()
+
+    high = held[0].shape[3]
+
+    def outer_tile(number, carry):
+        span = pl.ds(pl.multiple_of(number * 4 * high, 4 * high), 4 * high)
+        values = lowered(gram_product(r.hidden_v[:, span], r.cot_v[...]))
+        for inside in range(2):
+            spot = spot_of(number * 2 + inside)
+            first = values[2 * inside * high : (2 * inside + 1) * high]
+            second = values[(2 * inside + 1) * high : (2 * inside + 2) * high]
+            mine = jnp.where(core == 0, first, second)
+            r.stage_outer[spot] = jnp.where(core == 0, second, first)
+            for piece in OUTER:
+                begun, width = spans[piece]
+                held[piece][spot] = mine[:, begun : begun + width]
+        return carry
+
+    def prob_slot(slot, head):
+        return pl.ds(pl.multiple_of((slot * 2 + head) * TOK_DEV, TOK_DEV), TOK_DEV)
+
+    def prob_load(pair, head):
+        return pltpu.make_async_copy(
+            r.prob.at[pair * 2 + head],
+            r.hidden_v.at[:, prob_slot(pair % 2, head)],
+            r.prob_sem.at[pair % 2, head],
+        )
+
+    def outer_grad():
+        hidden_load.wait()
+        cot_load.wait()
+        lax.fori_loop(0, blocks // 2, outer_tile, 0)
+        for piece in OUTER:
+            pair_copy(piece).start()
+        for pair in range(2):
+            for head in range(2):
+                prob_load(pair, head).start()
+
+    def turn_rows(copy):
+        copy.wait()
+        for first in range(0, D, 256):
+            r.turned_v[first : first + 256, :] = jnp.transpose(r.branch_v[:, first : first + 256])
+
+    def inner_tile(number, carry):
+        span = pl.ds(pl.multiple_of(number * 256, 256), 256)
+        values = back_product(r.cot_v[...], r.outer_w[span, :])
+        r.slope_v[:, span] = lowered(values * r.slope_v[:, span].astype(F32))
+        return carry
+
+    def inner_back():
+        outer_load.wait()
+        slope_load.wait()
+        lax.fori_loop(0, outer_rows // 256, inner_tile, 0)
+
+    rows = held[8].shape[3]
+    together = 384 // rows
+
+    def inner_grad():
+        turn_rows(two_load)
+        width = spans[4][1]
+        for half in range(2):
+
+            def tile(number, carry):
+                part = pl.ds(pl.multiple_of(number * 384, 384), 384)
+                for side in (core, 1 - core):
+                    start = pl.multiple_of((side * 2 + half) * 2 * width, TILE)
+                    values = lowered(
+                        plain_product(r.turned_v[part, :], r.slope_v[:, pl.ds(start, 2 * width)])
+                    )
+                    for inside in range(together):
+                        spot = spot_of(number * together + inside)
+                        block = values[inside * rows : (inside + 1) * rows]
+                        for quarter in range(2):
+                            piece = 4 + half * 2 + quarter
+                            target = held[piece] if side is core else stage(piece)
+                            target[spot] = block[:, quarter * width : (quarter + 1) * width]
+                return carry
+
+            lax.fori_loop(0, D // 384, tile, 0)
+            for quarter in range(2):
+                pair_copy(4 + half * 2 + quarter).start()
+
+    def square_grad(piece):
+        left, right, first = (
+            (r.attended_tv, r.cot_v, 0) if piece == 11 else (r.turned_v, r.merged_v, (piece - 8) * D)
+        )
+
+        def tile(number, carry):
+            part = pl.ds(pl.multiple_of(number * 384, 384), 384)
+            values = lowered(plain_product(left[part, :], right[:, first : first + D]))
+            for inside in range(together):
+                spot = spot_of(number * together + inside)
+                block = values[inside * rows : (inside + 1) * rows]
+                low, top = block[:, : D // 2], block[:, D // 2 :]
+                held[piece][spot] = jnp.where(core == 0, low, top)
+                r.stage_square[(piece - 8, *spot)] = jnp.where(core == 0, top, low)
+            return carry
+
+        lax.fori_loop(0, D // 384, tile, 0)
+        pair_copy(piece).start()
+
+    late = []
+
+    def norm_back(number, values, spread):
+        gain = r.gains_v[number : number + 1, :]
+        scale = lax.rsqrt(jnp.mean(values * values, axis=1, keepdims=True) + EPSILON)
+        sums = jnp.sum(spread * values * scale, axis=0, keepdims=True)
+        r.gain_sums[number : number + 1, :] = r.gain_sums[number : number + 1, :] + sums
+        scaled = spread * gain
+        inner = jnp.mean(scaled * values, axis=1, keepdims=True)
+        return scale * scaled - values * (scale * scale * scale * inner)
+
+    def two_back(part, carry):
+        rows = pl.ds(part * 256, 256)
+        spread = back_product(r.slope_v[rows, :], r.inner_w[...])
+        values = r.cot_v[rows, :].astype(F32) + norm_back(1, r.residual_v[rows, :], spread)
+        r.grad_v[rows, :] = values
+        r.cot_v[rows, :] = lowered(values)
+        return carry
+
+    def two_grad():
+        inner_load.wait()
+        residual_load.wait()
+        gains_load.wait()
+        r.gain_sums[...] = jnp.zeros(r.gain_sums.shape, F32)
+        lax.fori_loop(0, TOK_DEV // 256, two_back, 0)
+        for number, full in enumerate((r.full_query, r.full_key, r.full_value)):
+            late.append(load(full.reshape(D, D), r.inner_w.at[:, pl.ds(number * D, D)]))
+        late.append(load(r.embedded, r.residual_v))
+        turn_rows(load(r.normed, r.branch_v))
+
+    def branch_tile(number, carry):
+        span = pl.ds(pl.multiple_of(number * 256, 256), 256)
+        values = lowered(back_product(r.cot_v[...], r.output_w[span, :]))
+        r.branch_v[:, span] = values
+        r.branch_tv[span, :] = jnp.transpose(values)
+        return carry
+
+    def branch_grad():
+        output_load.wait()
+        attended_load.wait()
+        lax.fori_loop(0, D // 256, branch_tile, 0)
+        for copy in (value_load, query_load, key_load):
+            copy.wait()
+        r.near_sums[...] = jnp.zeros(r.near_sums.shape, F32)
+        r.far_sums[...] = jnp.zeros(r.far_sums.shape, F32)
+
+    tiles = TOK_DEV // TILE
+
+    def attend_pair(pair, carry):
+        span = pl.ds(pl.multiple_of(pair * TILE, TILE), TILE)
+        slot = pair % 2
+        value_sum = jnp.zeros((TOK_DEV, TILE), F32)
+        key_sum = jnp.zeros((TOK_DEV, TILE), F32)
+        turned = []
+        for head in range(2):
+            number = pair * 2 + head
+            own = pl.ds(pl.multiple_of(number * HEAD_DIM, HEAD_DIM), HEAD_DIM)
+            prob_load(pair, head).wait()
+            prob = r.hidden_v[:, prob_slot(slot, head)]
+            mask = pair_mask((TOK_DEV, TILE), 1, head)
+            masked = [
+                lowered(jnp.where(mask, ref[:, span].astype(F32), 0.0))
+                for ref in (r.value_v, r.branch_v, r.query_v)
+            ]
+            inner = jnp.sum(
+                r.branch_tv[own, :].astype(F32) * r.attended_tv[own, :].astype(F32),
+                axis=0,
+                keepdims=True,
+            )
+            strips = []
+            near_sums = [jnp.zeros((TILE, TILE), F32) for _ in range(3)]
+            far_sums = [jnp.zeros((TILE, TILE), F32) for _ in range(2)]
+            for strip in range(2):
+                lanes = slice(strip * 256, (strip + 1) * 256)
+                grad_prob = plain_product(masked[0], r.branch_tv[span, lanes])
+                scores = lowered(prob[:, lanes].astype(F32) * (grad_prob - inner[:, lanes]))
+                strips.append(scores)
+                values = scores.astype(F32)
+                for key_block in range(tiles):
+                    for part in range(2):
+                        gap = key_block - (strip * 2 + part)
+                        tile = values[
+                            key_block * TILE : (key_block + 1) * TILE,
+                            part * TILE : (part + 1) * TILE,
+                        ]
+                        if abs(gap) <= 1:
+                            near_sums[gap + 1] = near_sums[gap + 1] + tile
+                        else:
+                            far_sums[gap > 0] = far_sums[gap > 0] + tile
+            scores = jnp.concatenate(strips, axis=1)
+            value_sum = value_sum + plain_product(prob, masked[1])
+            key_sum = key_sum + plain_product(scores, masked[2])
+            turned.append(plain_product(r.key_tv[own, :], scores))
+            for kind, tile in enumerate(near_sums):
+                lanes = slice(kind * 2 * TILE, (kind + 1) * 2 * TILE)
+                r.near_sums[number, :, lanes] = diagonal_sums(tile)
+            for kind, tile in enumerate(far_sums):
+                lanes = slice(kind * TILE, (kind + 1) * TILE)
+                r.far_sums[number, :, lanes] = jnp.sum(tile, axis=0, keepdims=True)
+        query_sum = jnp.transpose(jnp.concatenate(turned, axis=0))
+        for number, values in enumerate((query_sum, key_sum, value_sum)):
+            where = pl.ds(pl.multiple_of(number * D + pair * TILE, TILE), TILE)
+            r.merged_v[:, where] = lowered(values)
+
+        @pl.when(pair + 2 < HEADS // 2)
+        def _():
+            for head in range(2):
+                prob_load(pair + 2, head).start()
+
+        return carry
+
+    def attend_some(first, last):
+        lax.fori_loop(first, last, attend_pair, 0)
+
+    def one_back(part, carry):
+        rows = pl.ds(part * 256, 256)
+        spread = back_product(r.merged_v[rows, :], r.inner_w[:, 0 : 3 * D])
+        values = r.grad_v[rows, :] + norm_back(0, r.residual_v[rows, :], spread)
+        r.grad_v[rows, :] = values
+        r.cot_v[rows, :] = lowered(values)
+        return carry
+
+    grad_save = pltpu.make_async_copy(r.grad_v, r.input_grad, r.local_sem.at[12])
+
+    def one_grad():
+        for copy in (*late, slots_load):
+            copy.wait()
+        lax.fori_loop(0, TOK_DEV // 256, one_back, 0)
+        grad_save.start()
+
+    def row_copy(owner):
+        return remote(
+            r.leaving.at[owner],
+            r.incoming.at[core, me],
+            r.row_send.at[owner],
+            r.row_recv.at[me],
+            (owner, core),
+        )
+
+    def row_arrival(owner):
+        return remote(
+            r.leaving.at[owner],
+            r.incoming.at[core, owner],
+            r.row_send.at[owner],
+            r.row_recv.at[owner],
+            (owner, core),
+        )
+
+    def over_copy(owner):
+        here = r.incoming.at[core, owner]
+        return remote(here, here, r.over_send.at[owner], r.over_recv.at[owner], place.sibling())
+
+    group = max(1, min(count, 256 // cap))
+
+    def leave(number, carry):
+        slot = lax.broadcasted_iota(jnp.int32, (group * cap, TOK_DEV), 0) + number * group * cap
+        hot = lowered((slot == r.slots_v[0:1, :]).astype(F32))
+        rows = lowered(plain_product(hot, r.cot_v[...]))
+        for inside in range(group):
+            owner = number * group + inside
+            r.leaving[pl.ds(owner, 1)] = rows[inside * cap : (inside + 1) * cap][None]
+
+            @pl.when(owner != me)
+            def _():
+                row_copy(owner).start()
+
+        return carry
+
+    own_row = pltpu.make_async_copy(r.leaving.at[me], r.incoming.at[core, me], r.local_sem.at[13])
+
+    def leave_some(first, last):
+        groups = count // group
+        lax.fori_loop(first * groups // 4, last * groups // 4, leave, 0)
+
+    def small_copy(step):
+        peer, device = place.other(step)
+        return remote(
+            r.small_v.at[peer],
+            r.small_in.at[me],
+            r.small_send.at[step - 1],
+            r.small_recv.at[step - 1],
+            device,
+        )
+
+    def send_small(step, carry):
+        small_copy(step).start()
+        return carry
+
+    def small_grad():
+        entry = lax.broadcasted_iota(jnp.int32, (16, NB * HEADS), 1)
+        entry_bucket = divided(entry, HEADS)
+        own_head = entry - entry_bucket * HEADS == lax.broadcasted_iota(
+            jnp.int32, (16, NB * HEADS), 0
+        )
+        totals = split_product(r.near_sums[:, 0, :], near_hot_columns(), back_product)
+        behind = jnp.sum(r.far_sums[:, 0, 0:TILE], axis=1, keepdims=True)
+        ahead = jnp.sum(r.far_sums[:, 0, TILE : 2 * TILE], axis=1, keepdims=True)
+        totals = totals + jnp.where(entry_bucket == 31, ahead, 0.0)
+        totals = totals + jnp.where(entry_bucket == 15, behind, 0.0)
+        bias = jnp.sum(jnp.where(own_head, totals, 0.0), axis=0, keepdims=True)
+        chip_rows = held[4].shape[3]
+        r.small_v[...] = jnp.zeros(r.small_v.shape, F32)
+        r.small_v[:, 0, :] = scatter_columns(r.gain_sums[0:1, :], chip_rows, count)
+        r.small_v[:, 1, :] = scatter_columns(r.gain_sums[1:2, :], chip_rows, count)
+        r.small_v[:, 2, :] = scatter_columns(bias, NB * HEADS // count, count)
+
+        lax.fori_loop(1, count, send_small, 0)
+        r.small_in[pl.ds(me, 1)] = r.small_v[pl.ds(me, 1)]
+
+    def pass_over(owner, carry):
+        @pl.when(owner != me)
+        def _():
+            row_copy(owner).wait_send()
+            row_arrival(owner).wait_recv()
+            over_copy(owner).start()
+
+        return carry
+
+    def hand_own():
+        own_row.start()
+        own_row.wait()
+        over_copy(me).start()
+
+    def hand_over(first, last):
+        lax.fori_loop(first * count // 4, last * count // 4, pass_over, 0)
+
+    def wait_small(step, carry):
+        small_copy(step).wait()
+        return carry
+
+    small_across = remote(
+        r.small_sum, r.small_pair, r.pair_send.at[12], r.pair_recv.at[12], place.sibling()
+    )
+    small_save = pltpu.make_async_copy(r.small_sum, r.out_small, r.local_sem.at[14])
+
+    def small_end():
+        lax.fori_loop(1, count, wait_small, 0)
+        r.small_sum[...] = jnp.sum(r.small_in[...], axis=0)
+        small_across.start()
+        small_across.wait()
+        r.small_sum[...] = r.small_sum[...] + r.small_pair[...]
+        small_save.start()
+
+    steps = SimpleNamespace(
+        outer=outer_grad,
+        back=inner_back,
+        inner=inner_grad,
+        square=square_grad,
+        two=two_grad,
+        branch=branch_grad,
+        attend=attend_some,
+        one=one_grad,
+        leave=leave_some,
+        own=hand_own,
+        over=hand_over,
+        small=small_grad,
+        end=small_end,
+        move=move,
+        sink=sink,
+        finish=finish,
+    )
+    plan(steps)
+
+    def wait_over(owner, carry):
+        over_copy(owner).wait()
+        return carry
+
+    lax.fori_loop(0, count, wait_over, 0)
+    for piece in range(len(spans)):
+        pair_copy(piece).wait_send()
+        for phase in range(2):
+            for copy in axis_copies(piece, phase):
+                copy.wait_send()
+        for turn in range(1, rounds + 1):
+            chain(lambda copy, block, way: copy.wait_send(), piece, turn, False)
+        for copy in end_copies(piece):
+            copy.wait()
+    grad_save.wait()
+    small_save.wait()
+
+
+def backward(dims, f, cotangent):
+    count = dims[0] * dims[1] * dims[2]
+    cap = 2 * TOK_DEV // count
+    rows = f.full_query.shape[3]
+    hidden = f.full_inner.shape[4]
+    high = f.full_outer.shape[4]
+    dma, vmem = pltpu.SemaphoreType.DMA, pltpu.VMEM
+    spans = piece_columns(hidden)
+    lists = [[] for _ in range(6)]
+    for number, (_, width) in enumerate(spans):
+        block = (high if number in OUTER else rows, width)
+        order = REDUCE_ORDER[number % 2]
+        lists[0].append(vmem((*dims, *block), BF16))
+        lists[1].append(vmem((*dims, *block), BF16))
+        for phase in range(2):
+            free = [dims[a] for a in range(3) if a not in order[: phase + 1]]
+            lists[2 + phase].append(vmem((dims[order[phase]] - 1, *free, *block), BF16))
+        lists[4].append(vmem((2, dims[0] - 1, *block), BF16))
+        lists[5].append(vmem(block if number in OUTER else (2, block[0] // 2, width), F32))
+    tokens, turned = (TOK_DEV, D), (D, TOK_DEV)
+    steps = max(dims) - 1
+    scratch = BackwardScratch(
+        stage_outer=vmem((*dims, high, D), BF16),
+        stage_square=vmem((4, *dims, rows, D // 2), BF16),
+        small_v=vmem((count, 8, TILE), F32),
+        small_in=vmem((count, 8, TILE), F32),
+        small_sum=vmem((8, TILE), F32),
+        small_pair=vmem((8, TILE), F32),
+        outer_w=vmem((hidden, D), BF16),
+        inner_w=vmem((D, hidden), BF16),
+        output_w=vmem((D, D), BF16),
+        hidden_v=vmem((TOK_DEV, hidden), BF16),
+        slope_v=vmem((TOK_DEV, hidden), BF16),
+        cot_v=vmem(tokens, BF16),
+        turned_v=vmem(turned, BF16),
+        residual_v=vmem(tokens, F32),
+        grad_v=vmem(tokens, F32),
+        attended_tv=vmem(turned, BF16),
+        value_v=vmem(tokens, BF16),
+        query_v=vmem(tokens, BF16),
+        key_tv=vmem(turned, BF16),
+        branch_v=vmem(tokens, BF16),
+        branch_tv=vmem(turned, BF16),
+        merged_v=vmem((TOK_DEV, 3 * D), BF16),
+        leaving=vmem((count, cap, D), BF16),
+        slots_v=vmem((8, TOK_DEV), jnp.int32),
+        gains_v=vmem((8, D), F32),
+        near_sums=vmem((16, 1, 6 * TILE), F32),
+        far_sums=vmem((16, 1, 2 * TILE), F32),
+        gain_sums=vmem((8, D), F32),
+        load_sem=dma((19,)),
+        prob_sem=dma((2, 2)),
+        row_send=dma((count,)),
+        row_recv=dma((count,)),
+        over_send=dma((count,)),
+        over_recv=dma((count,)),
+        small_send=dma((count - 1,)),
+        small_recv=dma((count - 1,)),
+        pair_send=dma((13,)),
+        pair_recv=dma((13,)),
+        local_sem=dma((15,)),
+        chain_send=dma((12, 2, dims[0] - 1)),
+        chain_recv=dma((12, 2, dims[0] - 1)),
+        axis_send=dma((12, 2, steps)),
+        axis_recv=dma((12, 2, steps)),
+        end_send=dma((12,)),
+        end_recv=dma((12,)),
+    )
+    half = rows // 2
+    shapes = BackwardOut(
+        out_query=((half, D), F32),
+        out_key=((half, D), F32),
+        out_value=((half, D), F32),
+        out_output=((half, D), F32),
+        out_inner=((half, hidden), F32),
+        out_outer=((high, D), F32),
+        out_small=((8, TILE), F32),
+        incoming=((2, count, cap, D), BF16),
+        input_grad=(tokens, F32),
+    )
+    used = {name: part for name, part in f._asdict().items() if name in BackwardIn._fields}
+    given = BackwardIn(**used, cotangent=cotangent)
+    found = pl.pallas_call(
+        partial(backward_kernel, dims, cap, backward_plan),
+        out_shape=[jax.ShapeDtypeStruct(*shape) for shape in shapes],
+        in_specs=[ANY] * len(given),
+        out_specs=[ANY] * len(shapes),
+        scratch_shapes=[*sum(lists, []), *scratch],
+        compiler_params=pltpu.CompilerParams(
+            collective_id=4, has_side_effects=True, vmem_limit_bytes=62 * 2**20
+        ),
+        name="backward",
+    )(*given)
+    return BackwardOut(*found)
 
 
 def near_places():
@@ -907,6 +2672,187 @@
     gap = jnp.where(lane < TILE, lane, lane - 2 * TILE)
     kinds = jnp.arange(3, dtype=jnp.int32)[:, None] - 1
     return relative_bucket(kinds * TILE - gap[None, :])
+
+
+def pack_small(norm1_gain, norm2_gain, position_bias):
+    rows = [jnp.pad(part, (0, TILE - part.shape[0])) for part in (norm1_gain, norm2_gain, position_bias)]
+    return jnp.pad(jnp.stack(rows), ((0, 13), (0, 0)))
+
+
+def forward_apart(
+    dims, send_counts, bucket, lengths, asked_rows, order, table, squares, w_inner, w_outer, small
+):
+    dp_count = dims[0] * dims[1] * dims[2]
+    cap = 2 * TOK_DEV // dp_count
+    counts_row = send_counts[0]
+    row_in_owner = asked_rows[0]
+    owner_ids = jnp.arange(dp_count, dtype=jnp.int32)
+    send_ends = jnp.sum(
+        jnp.where(owner_ids[None, :] <= owner_ids[:, None], counts_row[None, :], 0), axis=1
+    )
+    send_starts = send_ends - counts_row
+    places = jnp.arange(TOK_DEV, dtype=jnp.int32)
+    lanes = jnp.arange(TILE, dtype=jnp.int32)
+    wanted = send_starts[:, None] + lanes[None, :]
+    asks = jnp.sum(
+        jnp.where(wanted[:, :, None] == places[None, None, :], row_in_owner[None, None, :], 0), axis=2
+    )
+    asks = jnp.where((lanes[None, :] < counts_row[:, None]) & (lanes[None, :] < cap), asks, -1)
+    asks = jnp.broadcast_to(asks[:, None, :], (dp_count, 8, TILE))
+    past = (places[:, None] >= send_ends[None, :]).astype(jnp.int32)
+    owners = jnp.sum(past, axis=1, dtype=jnp.int32)
+    owner_start = jnp.sum(past * counts_row[None, :], axis=1, dtype=jnp.int32)
+    slots = owners * cap + places - owner_start
+    token_slot = jnp.sum(jnp.where(order[0][None, :] == places[:, None], slots[None, :], 0), axis=1)
+    all_slots = jnp.arange(dp_count * cap, dtype=jnp.int32)
+    spread = (token_slot[:, None] == all_slots[None, :]).astype(BF16)
+
+    shard = squares[0].shape[0]
+    bias_shard = NB * HEADS * shard // D
+    rows, asked, *gathered = fetch(
+        dims, asks, table, squares, w_inner, w_outer, small
+    )
+    wq_full, wk_full, wv_full, wo_full = (part.reshape(D, D) for part in gathered[:4])
+    inner_full = gathered[4].reshape(D, -1)
+    outer_full = gathered[5].reshape(-1, D)
+    small_full = gathered[6].reshape(2 * dp_count, 16, TILE)
+    gain_one = small_full[:, 0, :shard].reshape(1, D).astype(F32)
+    gain_two = small_full[:, 1, :shard].reshape(1, D).astype(F32)
+    bias_flat = small_full[:, 2, :bias_shard].reshape(NB * HEADS)
+    bias_table = bias_flat.reshape(NB, HEADS)
+
+    embedded = plain_product(spread, rows.reshape(dp_count * cap, D))
+    normed = lowered(normalize(embedded, gain_one))
+
+    span_shift = 6 + bucket[0]
+    document = places >> span_shift
+    within = places - (document << span_shift)
+    doc_ids = jnp.arange(8, dtype=jnp.int32)
+    doc_length = jnp.sum(jnp.where(document[:, None] == doc_ids[None, :], lengths[None, :], 0), axis=1)
+    usable = (document[:, None] == doc_ids[None, :]) & (within < doc_length)[:, None]
+    feature_k = jnp.pad(jnp.where(usable, 0.0, -BIG).astype(BF16), ((0, 0), (0, TILE - 8)))
+    feature_q = jnp.concatenate(
+        [
+            (doc_ids[:, None] == document[None, :]).astype(BF16),
+            (jnp.arange(8, dtype=jnp.int32)[:, None] == (places // TILE)[None, :]).astype(BF16),
+            jnp.zeros((TILE - 16, TOK_DEV), BF16),
+        ],
+        axis=0,
+    )
+    near_hot = (near_places().reshape(-1)[None, :] == jnp.arange(NB, dtype=jnp.int32)[:, None]).astype(BF16)
+    near = gram_product(bias_table, near_hot).reshape(HEADS, 3, 2 * TILE)
+
+    queries = lowered(plain_product(normed, wq_full))
+    key_rows = lowered(plain_product(normed, wk_full))
+    value_rows = lowered(plain_product(normed, wv_full))
+    attended_t, prob = attend(
+        bias_flat.astype(F32), key_rows, queries.T, value_rows.T, feature_k, feature_q, near
+    )
+    attended = attended_t.T
+    residual = embedded + plain_product(attended, wo_full)
+    normed_two = lowered(normalize(residual, gain_two))
+    inner_act = plain_product(normed_two, inner_full)
+    hidden = lowered(jax.nn.gelu(inner_act, approximate=True))
+    block_out = residual + plain_product(hidden, outer_full)
+    slope = jax.vjp(lambda u: jax.nn.gelu(u, approximate=True), inner_act)[1](jnp.ones_like(inner_act))[0]
+    return ForwardOut(
+        full_query=wq_full,
+        full_key=wk_full,
+        full_value=wv_full,
+        full_output=wo_full,
+        full_inner=inner_full,
+        full_outer=outer_full,
+        asked=asked,
+        slots=jnp.broadcast_to(token_slot[None, :], (8, TOK_DEV)),
+        gains=jnp.concatenate([gain_one, gain_two, jnp.zeros((6, D), F32)], axis=0),
+        block_out=lowered(block_out),
+        embedded=embedded,
+        normed=normed,
+        query=queries,
+        value=value_rows,
+        key_t=key_rows.T,
+        attended=attended,
+        attended_t=attended_t,
+        prob=prob,
+        residual=residual,
+        normed_two=normed_two,
+        hidden=hidden,
+        slope=lowered(slope),
+    )
+
+
+def backward_apart(dims, f, cotangent):
+    dp_count = dims[0] * dims[1] * dims[2]
+    cap = 2 * TOK_DEV // dp_count
+    chip_rows = D // dp_count
+    bias_rows = NB * HEADS // dp_count
+    wq_full, wk_full, wv_full, wo_full = (
+        part.reshape(D, D) for part in (f.full_query, f.full_key, f.full_value, f.full_output)
+    )
+    inner_full = f.full_inner.reshape(D, -1)
+    outer_full = f.full_outer.reshape(-1, D)
+    gain_one, gain_two = f.gains[0:1], f.gains[1:2]
+    prob, residual, normed_two, hidden = f.prob, f.residual, f.normed_two, f.hidden
+    embedded, normed, attended, attended_t = f.embedded, f.normed, f.attended, f.attended_t
+    all_slots = jnp.arange(dp_count * cap, dtype=jnp.int32)
+    spread_t = (all_slots[:, None] == f.slots[:1]).astype(BF16)
+    near_hot = (near_places().reshape(-1)[None, :] == jnp.arange(NB, dtype=jnp.int32)[:, None]).astype(BF16)
+
+    grad_out = cotangent.astype(F32)
+    grad_w_outer = lowered(gram_product(hidden, cotangent))
+    grad_hidden = back_product(cotangent, outer_full)
+    grad_inner = lowered(grad_hidden * f.slope.astype(F32))
+    grad_w_inner = lowered(gram_product(normed_two, grad_inner))
+    grad_normed_two = back_product(grad_inner, inner_full)
+    norm_two_pull = jax.vjp(normalize, residual, gain_two)[1]
+    grad_resid_norm, grad_gain_two = norm_two_pull(grad_normed_two)
+    grad_residual = grad_out + grad_resid_norm
+    grad_branch = lowered(grad_residual)
+    grad_w_output = lowered(gram_product(attended, grad_branch))
+    grad_attended = lowered(back_product(grad_branch, wo_full))
+    grad_values, grad_keys, grad_queries_t, bias_sums = attend_back(
+        prob, f.value, grad_attended.T, attended_t, grad_attended, f.query, f.key_t
+    )
+    grad_queries = grad_queries_t.T
+    near_sums = lax.dot_general(
+        bias_sums[:, :3].reshape(HEADS, 6 * TILE),
+        near_hot.astype(F32),
+        (((1,), (1,)), ((), ())),
+        precision=lax.Precision.HIGHEST,
+        preferred_element_type=F32,
+    )
+    far_behind = jnp.sum(bias_sums[:, 3], axis=1)
+    far_ahead = jnp.sum(bias_sums[:, 4], axis=1)
+    grad_bias = near_sums.T.at[15].add(far_behind).at[31].add(far_ahead)
+    grad_w_query = lowered(gram_product(normed, grad_queries))
+    grad_w_key = lowered(gram_product(normed, grad_keys))
+    grad_w_value = lowered(gram_product(normed, grad_values))
+    grad_normed = (
+        back_product(grad_queries, wq_full)
+        + back_product(grad_keys, wk_full)
+        + back_product(grad_values, wv_full)
+    )
+    norm_one_pull = jax.vjp(normalize, embedded, gain_one)[1]
+    grad_embed_norm, grad_gain_one = norm_one_pull(grad_normed)
+    input_grad = grad_residual + grad_embed_norm
+
+    small_grads = jnp.zeros((dp_count, 8, TILE), F32)
+    small_grads = small_grads.at[:, 0, :chip_rows].set(grad_gain_one.reshape(dp_count, chip_rows))
+    small_grads = small_grads.at[:, 1, :chip_rows].set(grad_gain_two.reshape(dp_count, chip_rows))
+    small_grads = small_grads.at[:, 2, : bias_rows].set(
+        grad_bias.reshape(dp_count, bias_rows)
+    )
+    leaving = lowered(plain_product(spread_t, lowered(input_grad))).reshape(dp_count, cap, D)
+    square = (*dims, chip_rows, D)
+    sums = reduce_grads(
+        dims,
+        [g.reshape(square) for g in (grad_w_query, grad_w_key, grad_w_value, grad_w_output)],
+        grad_w_inner.reshape(*dims, chip_rows, -1),
+        grad_w_outer.reshape(*dims, 2, -1, D),
+        small_grads,
+        leaving,
+    )
+    return BackwardOut(*sums, input_grad)
 
 
 def body(
@@ -928,156 +2874,56 @@
     w_outer,
     cotangent,
 ):
-    dp_count = dims[0] * dims[1] * dims[2]
-    cap = 2 * TOK_DEV // dp_count
-    owner_rows = table.shape[0]
-    core = lax.axis_index("fsdp")
-    counts_row = send_counts[0]
-    owner_ids = jnp.arange(dp_count, dtype=jnp.int32)
-    send_ends = jnp.sum(
-        jnp.where(owner_ids[None, :] <= owner_ids[:, None], counts_row[None, :], 0), axis=1
-    )
-    send_starts = send_ends - counts_row
-    places = jnp.arange(TOK_DEV, dtype=jnp.int32)
-    lanes = jnp.arange(TILE, dtype=jnp.int32)
-    wanted = send_starts[:, None] + lanes[None, :]
-    asks = jnp.sum(
-        jnp.where(wanted[:, :, None] == places[None, None, :], row_in_owner[None, None, :], 0), axis=2
-    )
-    asks = jnp.where((lanes[None, :] < counts_row[:, None]) & (lanes[None, :] < cap), asks, -1)
-    asks = jnp.broadcast_to(asks[:, None, :], (dp_count, 8, TILE))
-    past = (places[:, None] >= send_ends[None, :]).astype(jnp.int32)
-    owners = jnp.sum(past, axis=1, dtype=jnp.int32)
-    owner_start = jnp.sum(past * counts_row[None, :], axis=1, dtype=jnp.int32)
-    slots = owners * cap + places - owner_start
-    token_slot = jnp.sum(jnp.where(row_order[0][None, :] == places[:, None], slots[None, :], 0), axis=1)
-    all_slots = jnp.arange(dp_count * cap, dtype=jnp.int32)
-    spread = (token_slot[:, None] == all_slots[None, :]).astype(BF16)
-    spread_t = (all_slots[:, None] == token_slot[None, :]).astype(BF16)
-
     shard = norm1_gain.shape[0]
     bias_shard = position_bias.shape[0]
-    small = jnp.zeros((16, TILE), BF16)
-    small = small.at[0, :shard].set(norm1_gain).at[1, :shard].set(norm2_gain)
-    small = small.at[2, :bias_shard].set(position_bias)
-    rows, asked, *gathered = fetch(
-        dims, asks, table, (w_query, w_key, w_value, w_output), w_inner, w_outer, small
-    )
-    wq_full, wk_full, wv_full, wo_full = (part.reshape(D, D) for part in gathered[:4])
-    inner_full = gathered[4].reshape(D, -1)
-    outer_full = gathered[5].reshape(-1, D)
-    small_full = gathered[6].reshape(2 * dp_count, 16, TILE)
-    gain_one = small_full[:, 0, :shard].reshape(1, D).astype(F32)
-    gain_two = small_full[:, 1, :shard].reshape(1, D).astype(F32)
-    bias_flat = small_full[:, 2, :bias_shard].reshape(NB * HEADS)
-    bias_table = bias_flat.reshape(NB, HEADS)
-
-    embedded = plain_product(spread, rows.reshape(dp_count * cap, D))
-    normed = lowered(normalize(embedded, gain_one))
-
-    span_shift = 6 + bucket[0]
-    document = places >> span_shift
-    within = places - (document << span_shift)
-    doc_ids = jnp.arange(8, dtype=jnp.int32)
-    doc_length = jnp.sum(jnp.where(document[:, None] == doc_ids[None, :], lengths[None, :], 0), axis=1)
-    usable = (document[:, None] == doc_ids[None, :]) & (within < doc_length)[:, None]
-    feature_k = jnp.pad(jnp.where(usable, 0.0, -BIG).astype(BF16), ((0, 0), (0, TILE - 8)))
-    feature_q = jnp.concatenate(
-        [
-            (doc_ids[:, None] == document[None, :]).astype(BF16),
-            (jnp.arange(8, dtype=jnp.int32)[:, None] == (places // TILE)[None, :]).astype(BF16),
-            jnp.zeros((TILE - 16, TOK_DEV), BF16),
-        ],
-        axis=0,
-    )
-    near_hot = (near_places().reshape(-1)[None, :] == jnp.arange(NB, dtype=jnp.int32)[:, None]).astype(BF16)
-    near = gram_product(bias_table, near_hot).reshape(HEADS, 3, 2 * TILE)
-
-    queries = lowered(plain_product(normed, wq_full))
-    key_rows = lowered(plain_product(normed, wk_full))
-    value_rows = lowered(plain_product(normed, wv_full))
-    attended_t, prob = attend(
-        bias_flat.astype(F32), key_rows, queries.T, value_rows.T, feature_k, feature_q, near
-    )
-    attended = attended_t.T
-    residual = embedded + plain_product(attended, wo_full)
-    normed_two = lowered(normalize(residual, gain_two))
-    inner_act = plain_product(normed_two, inner_full)
-    hidden = lowered(jax.nn.gelu(inner_act, approximate=True))
-    layer_out = residual + plain_product(hidden, outer_full)
-
-    grad_out = cotangent.astype(F32)
-    grad_w_outer = lowered(gram_product(hidden, cotangent))
-    grad_hidden = back_product(cotangent, outer_full)
-    gelu_pull = jax.vjp(lambda pre_act: jax.nn.gelu(pre_act, approximate=True), inner_act)[1]
-    grad_inner = lowered(gelu_pull(grad_hidden)[0])
-    grad_w_inner = lowered(gram_product(normed_two, grad_inner))
-    grad_normed_two = back_product(grad_inner, inner_full)
-    norm_two_pull = jax.vjp(normalize, residual, gain_two)[1]
-    grad_resid_norm, grad_gain_two = norm_two_pull(grad_normed_two)
-    grad_residual = grad_out + grad_resid_norm
-    grad_branch = lowered(grad_residual)
-    grad_w_output = lowered(gram_product(attended, grad_branch))
-    grad_attended = lowered(back_product(grad_branch, wo_full))
-    grad_values, grad_keys, grad_queries_t, bias_sums = attend_back(
-        prob, value_rows, grad_attended.T, attended_t, grad_attended, queries, key_rows.T
-    )
-    grad_queries = grad_queries_t.T
-    near_sums = lax.dot_general(
-        bias_sums[:, :3].reshape(HEADS, 6 * TILE),
-        near_hot.astype(F32),
-        (((1,), (1,)), ((), ())),
-        precision=lax.Precision.HIGHEST,
-        preferred_element_type=F32,
-    )
-    far_behind = jnp.sum(bias_sums[:, 3], axis=1)
-    far_ahead = jnp.sum(bias_sums[:, 4], axis=1)
-    grad_bias = near_sums.T.at[15].add(far_behind).at[31].add(far_ahead)
-    grad_w_query = lowered(gram_product(normed, grad_queries))
-    grad_w_key = lowered(gram_product(normed, grad_keys))
-    grad_w_value = lowered(gram_product(normed, grad_values))
-    grad_normed = (
-        back_product(grad_queries, wq_full)
-        + back_product(grad_keys, wk_full)
-        + back_product(grad_values, wv_full)
-    )
-    norm_one_pull = jax.vjp(normalize, embedded, gain_one)[1]
-    grad_embed_norm, grad_gain_one = norm_one_pull(grad_normed)
-    input_grad = grad_residual + grad_embed_norm
-
-    chip_rows = 2 * shard
-    small_grads = jnp.zeros((dp_count, 8, TILE), F32)
-    small_grads = small_grads.at[:, 0, :chip_rows].set(grad_gain_one.reshape(dp_count, chip_rows))
-    small_grads = small_grads.at[:, 1, :chip_rows].set(grad_gain_two.reshape(dp_count, chip_rows))
-    small_grads = small_grads.at[:, 2, : 2 * bias_shard].set(
-        grad_bias.reshape(dp_count, 2 * bias_shard)
-    )
-    leaving = lowered(plain_product(spread_t, lowered(input_grad))).reshape(dp_count, cap, D)
-    square = (*dims, chip_rows, D)
-    sum_query, sum_key, sum_value, sum_output, sum_inner, sum_outer, sum_small, incoming = reduce_grads(
+    squares = (w_query, w_key, w_value, w_output)
+    small = pack_small(norm1_gain, norm2_gain, position_bias)
+    plan = forward if 2 * shard % 16 == 0 else forward_apart
+    f = plan(
         dims,
-        [g.reshape(square) for g in (grad_w_query, grad_w_key, grad_w_value, grad_w_output)],
-        grad_w_inner.reshape(*dims, chip_rows, -1),
-        grad_w_outer.reshape(*dims, 2, -1, D),
-        small_grads,
-        leaving,
-    )
-    ids = asked[:, :, 0, :cap].reshape(1, 2 * dp_count * cap)
-    table_grad = collect(ids, incoming.reshape(2 * dp_count * cap, D), owner_rows)
-    gain_one_sum = lax.dynamic_slice(sum_small[0], (core * shard,), (shard,))
-    gain_two_sum = lax.dynamic_slice(sum_small[1], (core * shard,), (shard,))
-    bias_sum = lax.dynamic_slice(sum_small[2], (core * bias_shard,), (bias_shard,))
+        send_counts,
+        bucket,
+        lengths,
+        row_in_owner[None, :],
+        row_order,
+        table,
+        squares,
+        w_inner,
+        w_outer,
+        small,
+    )
+    pull = backward if 2 * shard % 16 == 0 else backward_apart
+    b = pull(dims, f, cotangent)
+    ready = (
+        f.block_out,
+        b.input_grad,
+        b.out_query,
+        b.out_key,
+        b.out_value,
+        b.out_output,
+        b.out_inner,
+        b.out_outer,
+    )
+    table_grad, gain_one_sum, gain_two_sum, bias_sum, *placed = collect(
+        f.asked,
+        b.out_small,
+        b.incoming,
+        ready,
+        table.shape[0],
+        (shard, shard, bias_shard),
+    )
+    block_out, input_grad, sum_query, sum_key, sum_value, sum_output, sum_inner, sum_outer = placed
     return (
-        lowered(layer_out),
+        block_out,
         input_grad,
         table_grad,
-        gain_one_sum,
+        gain_one_sum[0],
         sum_query,
         sum_key,
         sum_value,
         sum_output,
-        bias_sum,
-        gain_two_sum,
+        bias_sum[0],
+        gain_two_sum[0],
         sum_inner,
         sum_outer,
     )

time: 347 us -> 252 us (0.73)
  matrix products: 49 us -> 0 us
  local copies, waits for them, and re-layouts: 38.6 us -> 1.34 us
  other arithmetic: 10.8 us -> 0.6 us
  Pallas kernels: 243 us -> 248 us
    dot_general x22 -> x0, matrix products: 49 us -> none  [the longest x8 19.3 us: plain_product(): return jnp.dot(left_side, right_side, preferred_element_type=F32)]
    unnamed x101 -> x0, local copies, waits for them, and re-layouts: 29.1 us -> none
    reduce_sum x6 -> x0, other arithmetic: 5.04 us -> none  [the longest x1 1.59 us: body(): jnp.sum(jnp.where(wanted[:, :, None] == places[None, None, :], row_in_own...]
    pallas_call x5 -> x3, Pallas kernels: 243 us -> 248 us  [the longest x1 123 us: forward(): pl.pallas_call(partial(forward_kernel, dims, cap, forward_plan), out_shap...]
    convert_element_type x8 -> x0, local copies, waits for them, and re-layouts: 3.61 us -> none  [the longest x4 3.24 us: lowered(): return array_in.astype(BF16)]
where the time goes in v3:
time: 252 us
  Pallas kernels  248 us (98%)
    pallas_call x1, Pallas kernels, forward(): pl.pallas_call(partial(forward_kernel, dims, cap, forward_plan), out_shap...  123 us
    pallas_call x1, Pallas kernels, backward(): pl.pallas_call(partial(backward_kernel, dims, cap, backward_plan), out_sh...  113 us
    pallas_call x1, Pallas kernels, collect(): pl.pallas_call(partial(collect_kernel, cap, sizes), grid=(-(-owner_rows /...  13.1 us

profile of v3, /device:TPU:0, one launch (start us, length us, event | category | flops | bytes accessed | tf_op | source)
XLA Modules:
  0.0 251.8 jit_solution(13939946658739307869)
XLA Ops:
  1.3 0.7 pad_bitcast_fusion.2
  1.9 0.7 pad_bitcast_fusion
  2.6 0.6 fusion.4.refs_12_
  3.2 122.6 %forward.1 = (bf16[4,2,2,48,768]{4,3,2,1,0:T(8,128)(2,1)}, bf16[4,2,2,48,768]{4,3,2,1,0:T(8,128)(2,1)}, bf16[4,2,2,48,768]{4,3,2,1,0:T(8,128)(2,1)}, bf16[4,2,2,...) custom-call(s32[1,16]{1,0:T(1,128)} %refs_0_.1, ...), custom_call_target="tpu_custom_call" | custom-call | tf_op jit(solution)/shard_map/forward/pallas_call | solution.py:1844
  125.9 112.6 %backward.1 = (f32[24,768]{1,0:T(8,128)}, f32[24,768]{1,0:T(8,128)}, f32[24,768]{1,0:T(8,128)}, f32[24,768]{1,0:T(8,128)}, f32[24,3072]{1,0:T(8,128)}, /*index=5...) custom-call(bf16[4,2,2,48,768]{4,3,2,1,0:T(8,128)(2,1)} %get-tuple-element.55.refs_0_, ...), custom_call_target="tpu_custom_call" | custom-call | tf_op jit(solution)/shard_map/backward/pallas_call | solution.py:2656
  238.5 13.1 %collect.1 = (f32[2008,768]{1,0:T(8,128)}, f32[1,24]{1,0:T(1,128)}, f32[1,24]{1,0:T(1,128)}, f32[1,12]{1,0:T(1,128)}, bf16[512,768]{1,0:T(8,128)(2,1)}, /*index=...) custom-call(s32[2,16,8,128]{3,2,1,0:T(8,128)} %get-tuple-element.54., ...), custom_call_target="tpu_custom_call" | custom-call | tf_op jit(solution)/shard_map/collect/pallas_call | solution.py:953

commit v4 on v3

--- a/solution.py
+++ b/solution.py
@@ -946,7 +946,7 @@
 
 
 def collect(asked, small, incoming, ready, owner_rows, sizes):
-    high = 256
+    high = 672
     cap = incoming.shape[2]
     slots = incoming.shape[0] * incoming.shape[1] * cap
     lines = [jax.ShapeDtypeStruct((1, size), F32) for size in sizes]
@@ -1033,7 +1033,6 @@
     asked: Any
     slots: Any
     gains: Any
-    block_out: Any
     embedded: Any
     normed: Any
     query: Any
@@ -1075,7 +1074,6 @@
     value_w: Any
     output_w: Any
     inner_w: Any
-    outer_w: Any
     embedded_v: Any
     normed_v: Any
     query_v: Any
@@ -1090,7 +1088,6 @@
     normed_two_v: Any
     hidden_v: Any
     slope_v: Any
-    block_v: Any
     prob_v: Any
     slots_v: Any
     ask_send: Any
@@ -1167,8 +1164,7 @@
     k.load(4)
     k.move(3, 2, 3)
     k.widen()
-    k.load(5)
-    k.narrow()
+    k.outer()
 
 
 def forward_kernel(dims, cap, plan, *refs):
@@ -1581,7 +1577,6 @@
         (r.full_value, r.value_w, 10),
         (r.full_output, r.output_w, 11),
         (r.full_inner, r.inner_w, *INNER),
-        (r.full_outer, r.outer_w, *OUTER),
     )
 
     def load(*numbers):
@@ -1622,30 +1617,27 @@
                 near_tile(near[:, kind * 2 * TILE : (kind + 1) * 2 * TILE]) for kind in range(3)
             ]
             values = r.value_tv[pl.ds(pl.multiple_of(number * HEAD_DIM, HEAD_DIM), HEAD_DIM), :]
-            for strip in range(2):
-                cols = slice(strip * 256, (strip + 1) * 256)
-                right = jnp.concatenate([r.query_tv[span, cols], r.feature_q[:, cols]], axis=0)
-                scores = plain_product(left, right)
-                rows = []
-                for key_block in range(tiles):
-                    parts = []
-                    for inner in range(2):
-                        gap = key_block - (strip * 2 + inner)
-                        part = scores[
-                            key_block * TILE : (key_block + 1) * TILE,
-                            inner * TILE : (inner + 1) * TILE,
-                        ]
-                        parts.append(part + bias_tiles[gap + 1] if abs(gap) <= 1 else part)
-                    rows.append(jnp.concatenate(parts, axis=1))
-                scores = jnp.concatenate(rows, axis=0)
-                peak = jnp.max(scores, axis=0, keepdims=True)
-                powers = jnp.exp(scores - peak)
-                share = 1.0 / jnp.sum(powers, axis=0, keepdims=True)
-                weights = lowered(powers * share)
-                r.prob_v[slot, head, :, cols] = weights
-                r.attended_tv[
-                    pl.ds(pl.multiple_of(number * HEAD_DIM, HEAD_DIM), HEAD_DIM), cols
-                ] = lowered(plain_product(values, weights))
+            right = jnp.concatenate([r.query_tv[span, :], r.feature_q[...]], axis=0)
+            scores = plain_product(left, right)
+            rows = []
+            for key_block in range(tiles):
+                parts = []
+                for query_block in range(tiles):
+                    gap = key_block - query_block
+                    part = scores[
+                        key_block * TILE : (key_block + 1) * TILE,
+                        query_block * TILE : (query_block + 1) * TILE,
+                    ]
+                    parts.append(part + bias_tiles[gap + 1] if abs(gap) <= 1 else part)
+                rows.append(jnp.concatenate(parts, axis=1))
+            scores = jnp.concatenate(rows, axis=0)
+            peak = jnp.max(scores, axis=0, keepdims=True)
+            powers = jnp.exp(scores - peak)
+            share = 1.0 / jnp.sum(powers, axis=0, keepdims=True)
+            weights = lowered(powers * share)
+            r.prob_v[slot, head] = weights
+            own = pl.ds(pl.multiple_of(number * HEAD_DIM, HEAD_DIM), HEAD_DIM)
+            r.attended_tv[own, :] = lowered(plain_product(values, weights))
         r.attended_v[:, span] = jnp.transpose(r.attended_tv[span, :])
         prob_copy(pair).start()
         return carry
@@ -1690,16 +1682,9 @@
         save(r.hidden_v, r.hidden)
         save(r.slope_v, r.slope)
 
-    def narrow(number, carry):
-        span = pl.ds(pl.multiple_of(number * 256, 256), 256)
-        values = r.residual_v[:, span] + plain_product(r.hidden_v[...], r.outer_w[:, span])
-        r.block_v[:, span] = lowered(values)
-        return carry
-
-    def narrow_all():
-        waits[5].wait()
-        lax.fori_loop(0, D // 256, narrow, 0)
-        save(r.block_v, r.block_out)
+    def outer_end():
+        for piece in OUTER:
+            core_copy(piece).wait_recv()
 
     steps = SimpleNamespace(
         begin=begin,
@@ -1719,7 +1704,7 @@
         attend=attend_some,
         branch=branch_out,
         widen=widen_all,
-        narrow=narrow_all,
+        outer=outer_end,
     )
     plan(steps)
 
@@ -1760,7 +1745,6 @@
         asked=((2, count, 8, TILE), jnp.int32),
         slots=((8, TOK_DEV), jnp.int32),
         gains=((8, D), F32),
-        block_out=(tokens, BF16),
         embedded=(tokens, F32),
         normed=(tokens, BF16),
         query=(tokens, BF16),
@@ -1804,7 +1788,6 @@
         value_w=whole,
         output_w=whole,
         inner_w=vmem((D, hidden), BF16),
-        outer_w=vmem((hidden, D), BF16),
         embedded_v=vmem(tokens, F32),
         normed_v=vmem(tokens, BF16),
         query_v=vmem(tokens, BF16),
@@ -1819,7 +1802,6 @@
         normed_two_v=vmem(tokens, BF16),
         hidden_v=vmem((TOK_DEV, hidden), BF16),
         slope_v=vmem((TOK_DEV, hidden), BF16),
-        block_v=vmem(tokens, BF16),
         prob_v=vmem((2, 2, TOK_DEV, TOK_DEV), BF16),
         slots_v=vmem((8, TOK_DEV), jnp.int32),
         ask_send=dma((count - 1,)),
@@ -1907,6 +1889,7 @@
     out_small: Any
     incoming: Any
     input_grad: Any
+    block_out: Any
 
 
 class BackwardScratch(NamedTuple):
@@ -1960,38 +1943,39 @@
 def backward_plan(k):
     k.outer()
     k.back()
-    k.move(0, 0, 1, 2, 3)
+    k.move(0, *OUTER)
     k.inner()
     k.two()
-    k.move(0, 4, 5, 6, 7)
+    k.move(0, *INNER)
     k.branch()
+    k.attend(0, 6)
+    k.move(1, *OUTER)
     k.square(11)
-    k.attend(0, 2)
-    k.move(1, 0, 1, 2, 3)
-    k.attend(2, 6)
-    k.move(2, 0, 1, 2, 3)
+    k.move(2, *OUTER)
     k.one()
-    k.move(1, 4, 5, 6, 7)
-    k.sink(1, 0, 1, 2, 3)
+    k.sink(1, *OUTER)
     k.leave(0, 4)
-    k.own()
-    k.sink(2, 0, 1, 2, 3)
     k.square(8)
     k.square(9)
     k.square(10)
-    k.move(2, 4, 5, 6, 7)
-    k.move(0, 8, 9, 10, 11)
-    k.finish(0, 1, 2, 3)
-    k.sink(1, 4, 5, 6, 7)
+    k.own()
+    k.sink(2, *OUTER)
+    k.move(1, *INNER)
+    k.reload()
+    k.move(0, *SQUARE)
+    k.layer()
+    k.move(2, *INNER)
+    k.move(1, *SQUARE)
+    k.finish(*OUTER)
+    k.sink(1, *INNER)
     k.small()
-    k.move(1, 8, 9, 10, 11)
-    k.sink(2, 4, 5, 6, 7)
-    k.move(2, 8, 9, 10, 11)
-    k.finish(4, 5, 6, 7)
-    k.sink(1, 8, 9, 10, 11)
+    k.move(2, *SQUARE)
+    k.sink(2, *INNER)
+    k.sink(1, *SQUARE)
+    k.finish(*INNER)
     k.over(0, 4)
-    k.sink(2, 8, 9, 10, 11)
-    k.finish(8, 9, 10, 11)
+    k.sink(2, *SQUARE)
+    k.finish(*SQUARE)
     k.end()
 
 
@@ -2359,27 +2343,22 @@
                 axis=0,
                 keepdims=True,
             )
-            strips = []
             near_sums = [jnp.zeros((TILE, TILE), F32) for _ in range(3)]
             far_sums = [jnp.zeros((TILE, TILE), F32) for _ in range(2)]
-            for strip in range(2):
-                lanes = slice(strip * 256, (strip + 1) * 256)
-                grad_prob = plain_product(masked[0], r.branch_tv[span, lanes])
-                scores = lowered(prob[:, lanes].astype(F32) * (grad_prob - inner[:, lanes]))
-                strips.append(scores)
-                values = scores.astype(F32)
-                for key_block in range(tiles):
-                    for part in range(2):
-                        gap = key_block - (strip * 2 + part)
-                        tile = values[
-                            key_block * TILE : (key_block + 1) * TILE,
-                            part * TILE : (part + 1) * TILE,
-                        ]
-                        if abs(gap) <= 1:
-                            near_sums[gap + 1] = near_sums[gap + 1] + tile
-                        else:
-                            far_sums[gap > 0] = far_sums[gap > 0] + tile
-            scores = jnp.concatenate(strips, axis=1)
+            grad_prob = plain_product(masked[0], r.branch_tv[span, :])
+            scores = lowered(prob.astype(F32) * (grad_prob - inner))
+            wide = scores.astype(F32)
+            for key_block in range(tiles):
+                for query_block in range(tiles):
+                    gap = key_block - query_block
+                    tile = wide[
+                        key_block * TILE : (key_block + 1) * TILE,
+                        query_block * TILE : (query_block + 1) * TILE,
+                    ]
+                    if abs(gap) <= 1:
+                        near_sums[gap + 1] = near_sums[gap + 1] + tile
+                    else:
+                        far_sums[gap > 0] = far_sums[gap > 0] + tile
             value_sum = value_sum + plain_product(prob, masked[1])
             key_sum = key_sum + plain_product(scores, masked[2])
             turned.append(plain_product(r.key_tv[own, :], scores))
@@ -2533,7 +2512,34 @@
         r.small_sum[...] = r.small_sum[...] + r.small_pair[...]
         small_save.start()
 
+    block_save = pltpu.make_async_copy(r.cot_v, r.block_out, r.local_sem.at[15])
+
+    def reload():
+        for piece in INNER:
+            pair_copy(piece).wait_send()
+        late.extend(
+            (
+                load(r.hidden, r.hidden_v),
+                load(r.full_outer.reshape(outer_rows, D), r.outer_w),
+                load(r.residual, r.residual_v),
+            )
+        )
+
+    def narrow(number, carry):
+        span = pl.ds(pl.multiple_of(number * 256, 256), 256)
+        values = r.residual_v[:, span] + plain_product(r.hidden_v[...], r.outer_w[:, span])
+        r.cot_v[:, span] = lowered(values)
+        return carry
+
+    def layer_out():
+        for copy in late[-3:]:
+            copy.wait()
+        lax.fori_loop(0, D // 256, narrow, 0)
+        block_save.start()
+
     steps = SimpleNamespace(
+        reload=reload,
+        layer=layer_out,
         outer=outer_grad,
         back=inner_back,
         inner=inner_grad,
@@ -2559,7 +2565,8 @@
 
     lax.fori_loop(0, count, wait_over, 0)
     for piece in range(len(spans)):
-        pair_copy(piece).wait_send()
+        if piece not in INNER:
+            pair_copy(piece).wait_send()
         for phase in range(2):
             for copy in axis_copies(piece, phase):
                 copy.wait_send()
@@ -2569,6 +2576,7 @@
             copy.wait()
     grad_save.wait()
     small_save.wait()
+    block_save.wait()
 
 
 def backward(dims, f, cotangent):
@@ -2621,7 +2629,7 @@
         near_sums=vmem((16, 1, 6 * TILE), F32),
         far_sums=vmem((16, 1, 2 * TILE), F32),
         gain_sums=vmem((8, D), F32),
-        load_sem=dma((19,)),
+        load_sem=dma((22,)),
         prob_sem=dma((2, 2)),
         row_send=dma((count,)),
         row_recv=dma((count,)),
@@ -2631,7 +2639,7 @@
         small_recv=dma((count - 1,)),
         pair_send=dma((13,)),
         pair_recv=dma((13,)),
-        local_sem=dma((15,)),
+        local_sem=dma((16,)),
         chain_send=dma((12, 2, dims[0] - 1)),
         chain_recv=dma((12, 2, dims[0] - 1)),
         axis_send=dma((12, 2, steps)),
@@ -2650,6 +2658,7 @@
         out_small=((8, TILE), F32),
         incoming=((2, count, cap, D), BF16),
         input_grad=(tokens, F32),
+        block_out=(tokens, BF16),
     )
     used = {name: part for name, part in f._asdict().items() if name in BackwardIn._fields}
     given = BackwardIn(**used, cotangent=cotangent)
@@ -2753,7 +2762,6 @@
     normed_two = lowered(normalize(residual, gain_two))
     inner_act = plain_product(normed_two, inner_full)
     hidden = lowered(jax.nn.gelu(inner_act, approximate=True))
-    block_out = residual + plain_product(hidden, outer_full)
     slope = jax.vjp(lambda u: jax.nn.gelu(u, approximate=True), inner_act)[1](jnp.ones_like(inner_act))[0]
     return ForwardOut(
         full_query=wq_full,
@@ -2765,7 +2773,6 @@
         asked=asked,
         slots=jnp.broadcast_to(token_slot[None, :], (8, TOK_DEV)),
         gains=jnp.concatenate([gain_one, gain_two, jnp.zeros((6, D), F32)], axis=0),
-        block_out=lowered(block_out),
         embedded=embedded,
         normed=normed,
         query=queries,
@@ -2852,7 +2859,8 @@
         small_grads,
         leaving,
     )
-    return BackwardOut(*sums, input_grad)
+    block_out = lowered(residual + plain_product(hidden, outer_full))
+    return BackwardOut(*sums, input_grad, block_out)
 
 
 def body(
@@ -2895,7 +2903,7 @@
     pull = backward if 2 * shard % 16 == 0 else backward_apart
     b = pull(dims, f, cotangent)
     ready = (
-        f.block_out,
+        b.block_out,
         b.input_grad,
         b.out_query,
         b.out_key,

time: 252 us -> 240 us (0.952)
  Pallas kernels: 248 us -> 235 us
    pallas_call x1, Pallas kernels: 123 us -> 114 us  [forward(): pl.pallas_call(partial(forward_kernel, dims, cap, forward_plan), out_shap...]
    pallas_call x1, Pallas kernels: 113 us -> 110 us  [backward(): pl.pallas_call(partial(backward_kernel, dims, cap, backward_plan), out_sh...]
where the time goes in v4:
time: 240 us; the launch traced here: 239 us
  Pallas kernels  235 us (98%)
    pallas_call x1, Pallas kernels, forward(): pl.pallas_call(partial(forward_kernel, dims, cap, forward_plan), out_shap...  114 us
    pallas_call x1, Pallas kernels, backward(): pl.pallas_call(partial(backward_kernel, dims, cap, backward_plan), out_sh...  110 us
    pallas_call x1, Pallas kernels, collect(): pl.pallas_call(partial(collect_kernel, cap, sizes), grid=(-(-owner_rows /...  12.3 us

profile of v4, /device:TPU:0, one launch (start us, length us, event | category | flops | bytes accessed | tf_op | source)
XLA Modules:
  0.0 238.8 jit_solution(6365051753019156445)
XLA Ops:
  1.3 0.7 pad_bitcast_fusion.2
  1.9 0.7 pad_bitcast_fusion
  2.6 0.6 fusion.4.refs_12_
  3.2 113.5 %forward.1 = (bf16[4,2,2,48,768]{4,3,2,1,0:T(8,128)(2,1)}, bf16[4,2,2,48,768]{4,3,2,1,0:T(8,128)(2,1)}, bf16[4,2,2,48,768]{4,3,2,1,0:T(8,128)(2,1)}, bf16[4,2,2,...) custom-call(s32[1,16]{1,0:T(1,128)} %refs_0_.1, ...), custom_call_target="tpu_custom_call" | custom-call | tf_op jit(solution)/shard_map/forward/pallas_call | solution.py:1826
  116.8 109.6 %backward.1 = (f32[24,768]{1,0:T(8,128)}, f32[24,768]{1,0:T(8,128)}, f32[24,768]{1,0:T(8,128)}, f32[24,768]{1,0:T(8,128)}, f32[24,3072]{1,0:T(8,128)}, /*index=5...) custom-call(bf16[4,2,2,48,768]{4,3,2,1,0:T(8,128)(2,1)} %get-tuple-e, ...), custom_call_target="tpu_custom_call" | custom-call | tf_op jit(solution)/shard_map/backward/pallas_call | solution.py:2665
  226.4 12.3 %collect.1 = (f32[2008,768]{1,0:T(8,128)}, f32[1,24]{1,0:T(1,128)}, f32[1,24]{1,0:T(1,128)}, f32[1,12]{1,0:T(1,128)}, bf16[512,768]{1,0:T(8,128)(2,1)}, /*index=...) custom-call(s32[2,16,8,128]{3,2,1,0:T(8,128)} %get-tuple-element.54., ...), custom_call_target="tpu_custom_call" | custom-call | tf_op jit(solution)/shard_map/collect/pallas_call | solution.py:953

commit v5 on v4

--- a/solution.py
+++ b/solution.py
@@ -1538,7 +1538,7 @@
         return carry
 
     def embed(part, carry):
-        rows = pl.ds(part * 256, 256)
+        rows = pl.ds(part * 512, 512)
         values = plain_product(r.spread[rows, :], landed[0])
         r.embedded_v[rows, :] = values
         scale = lax.rsqrt(jnp.mean(values * values, axis=1, keepdims=True) + EPSILON)
@@ -1549,7 +1549,7 @@
         lax.fori_loop(0, count, wait_row, 0)
         own_rows.wait()
         landed.append(r.landed[...].reshape(count * cap, D))
-        lax.fori_loop(0, TOK_DEV // 256, embed, 0)
+        lax.fori_loop(0, TOK_DEV // 512, embed, 0)
         save(r.embedded_v, r.embedded)
         save(r.normed_v, r.normed)
 
@@ -1648,7 +1648,7 @@
         lax.fori_loop(first, last, attend_pair, 0)
 
     def add_branch(part, carry):
-        rows = pl.ds(part * 256, 256)
+        rows = pl.ds(part * 512, 512)
         values = r.embedded_v[rows, :] + plain_product(r.attended_v[rows, :], r.output_w[...])
         r.residual_v[rows, :] = values
         scale = lax.rsqrt(jnp.mean(values * values, axis=1, keepdims=True) + EPSILON)
@@ -1659,7 +1659,7 @@
         save(r.attended_tv, r.attended_t)
         save(r.attended_v, r.attended)
         waits[3].wait()
-        lax.fori_loop(0, TOK_DEV // 256, add_branch, 0)
+        lax.fori_loop(0, TOK_DEV // 512, add_branch, 0)
         save(r.residual_v, r.residual)
         save(r.normed_two_v, r.normed_two)
 
@@ -2286,7 +2286,7 @@
         return scale * scaled - values * (scale * scale * scale * inner)
 
     def two_back(part, carry):
-        rows = pl.ds(part * 256, 256)
+        rows = pl.ds(part * 512, 512)
         spread = back_product(r.slope_v[rows, :], r.inner_w[...])
         values = r.cot_v[rows, :].astype(F32) + norm_back(1, r.residual_v[rows, :], spread)
         r.grad_v[rows, :] = values
@@ -2298,7 +2298,7 @@
         residual_load.wait()
         gains_load.wait()
         r.gain_sums[...] = jnp.zeros(r.gain_sums.shape, F32)
-        lax.fori_loop(0, TOK_DEV // 256, two_back, 0)
+        lax.fori_loop(0, TOK_DEV // 512, two_back, 0)
         for number, full in enumerate((r.full_query, r.full_key, r.full_value)):
             late.append(load(full.reshape(D, D), r.inner_w.at[:, pl.ds(number * D, D)]))
         late.append(load(r.embedded, r.residual_v))
@@ -2384,7 +2384,7 @@
         lax.fori_loop(first, last, attend_pair, 0)
 
     def one_back(part, carry):
-        rows = pl.ds(part * 256, 256)
+        rows = pl.ds(part * 512, 512)
         spread = back_product(r.merged_v[rows, :], r.inner_w[:, 0 : 3 * D])
         values = r.grad_v[rows, :] + norm_back(0, r.residual_v[rows, :], spread)
         r.grad_v[rows, :] = values
@@ -2396,7 +2396,7 @@
     def one_grad():
         for copy in (*late, slots_load):
             copy.wait()
-        lax.fori_loop(0, TOK_DEV // 256, one_back, 0)
+        lax.fori_loop(0, TOK_DEV // 512, one_back, 0)
         grad_save.start()
 
     def row_copy(owner):

time: 240 us -> 239 us (level)
  no operation moved by 1% of the time
where the time goes in v5:
time: 239 us; the launch traced here: 238 us
  Pallas kernels  235 us (98%)
    pallas_call x1, Pallas kernels, forward(): pl.pallas_call(partial(forward_kernel, dims, cap, forward_plan), out_shap...  113 us
    pallas_call x1, Pallas kernels, backward(): pl.pallas_call(partial(backward_kernel, dims, cap, backward_plan), out_sh...  109 us
    pallas_call x1, Pallas kernels, collect(): pl.pallas_call(partial(collect_kernel, cap, sizes), grid=(-(-owner_rows /...  12.3 us

profile of v5, /device:TPU:0, one launch (start us, length us, event | category | flops | bytes accessed | tf_op | source)
XLA Modules:
  0.0 238.1 jit_solution(8004028767428432135)
XLA Ops:
  1.3 0.7 pad_bitcast_fusion.2
  1.9 0.7 pad_bitcast_fusion
  2.6 0.6 fusion.4.refs_12_
  3.2 113.3 %forward.1 = (bf16[4,2,2,48,768]{4,3,2,1,0:T(8,128)(2,1)}, bf16[4,2,2,48,768]{4,3,2,1,0:T(8,128)(2,1)}, bf16[4,2,2,48,768]{4,3,2,1,0:T(8,128)(2,1)}, bf16[4,2,2,...) custom-call(s32[1,16]{1,0:T(1,128)} %refs_0_.1, ...), custom_call_target="tpu_custom_call" | custom-call | tf_op jit(solution)/shard_map/forward/pallas_call | solution.py:1826
  116.5 109.1 %backward.1 = (f32[24,768]{1,0:T(8,128)}, f32[24,768]{1,0:T(8,128)}, f32[24,768]{1,0:T(8,128)}, f32[24,768]{1,0:T(8,128)}, f32[24,3072]{1,0:T(8,128)}, /*index=5...) custom-call(bf16[4,2,2,48,768]{4,3,2,1,0:T(8,128)(2,1)} %get-tuple-e, ...), custom_call_target="tpu_custom_call" | custom-call | tf_op jit(solution)/shard_map/backward/pallas_call | solution.py:2665
  225.6 12.3 %collect.1 = (f32[2008,768]{1,0:T(8,128)}, f32[1,24]{1,0:T(1,128)}, f32[1,24]{1,0:T(1,128)}, f32[1,12]{1,0:T(1,128)}, bf16[512,768]{1,0:T(8,128)(2,1)}, /*index=...) custom-call(s32[2,16,8,128]{3,2,1,0:T(8,128)} %get-tuple-element.54., ...), custom_call_target="tpu_custom_call" | custom-call | tf_op jit(solution)/shard_map/collect/pallas_call | solution.py:953
